TPU v7x, 256 devices: a whole 4x4x8 slice. The times are simulated.
256 devices in a mesh: gx: 32 (over z_hi, x, y), gy: 8 (over z_lo, core).
Axes of the slice: x: 4, y: 4, z: 8 (z_hi: 2, z_lo: 4; z = z_hi * 4 + z_lo), core: 2. Of those that a mesh axis runs over, the one named last changes fastest.
Arguments:
- populations: float32 [27, 24, 256, 1024], P(None, None, 'gx', 'gy'), may hold values from 0 to 1, as said below
- solid_mask: int32 [24, 256, 1024], P(None, 'gx', 'gy'), may hold values from 0 to 1, as said below
- link_cell: int32 [1048576], P(('gx', 'gy')), may hold values from 0 to 24575, as said below
- link_dir: int32 [1048576], P(('gx', 'gy')), may hold values from 0 to 26, as said below
- link_second: int32 [1048576], P(('gx', 'gy')), may hold values from 0 to 31199, as said below
- link_q: float32 [1048576], P(('gx', 'gy')), may hold values from 0.05 to 0.95
- link_panel: int32 [1048576], P(('gx', 'gy')), may hold values from -1 to 32767, as said below
Outputs:
- populations_next: float32 [27, 24, 256, 1024], P(None, None, 'gx', 'gy')
- panel_force: float32 [3, 32768], P(None, ('gx', 'gy'))
Inputs may be any that keep to these rules, and one draw needn't show every extreme that they name: `solid_mask`: every value is 0 or 1; building cells stand in columns of 2 x 2 cells rising from the ground. `populations`: positive; the cell's populations are near a discrete equilibrium with density near 1 and speed under 0.25. `link_cell`: within one tile the live slots come first and name distinct cells. `link_dir`: never 13 (the rest direction); the second node lies inside 0..23 vertically. `link_second`: it is the link's cell minus c_d, widened coordinates. `link_panel`: panel p is owned by tile p // 128, tiles numbered streamwise index times 8 plus spanwise index; a live link's panel is owned by its own tile or by the tile one step streamwise before or after it (periodic) with the same spanwise index. In every draw one tile has all 4096 slots live and another has 512.
All inputs are finite; a program needn't handle non-finite values.
Results may differ from a plain program's by a relative error of at most 0.0003.
Values sent between devices are 32-bit elements; how exact they have to be, the bound alone decides.
No kernel may reach another device: no remote copies, remote signals or barrier semaphores. Data moves between devices by JAX's collectives and lax.ppermute only.
A program may use at most 128 MiB of HBM per device.

v0:
```python
import jax
import jax.numpy as jnp
from jax import lax
from jax.sharding import PartitionSpec as P

PAN_DEV = 128


RELAXATION = 1.7


def with_halo(cells, sides, width):
    for axis, dim in sides:
        count = lax.axis_size(axis)
        head = lax.slice_in_dim(cells, 0, width, axis=dim)
        tail = lax.slice_in_dim(cells, cells.shape[dim] - width, cells.shape[dim], axis=dim)
        cells = jnp.concatenate(
            [
                lax.ppermute(tail, axis, [(i, (i + 1) % count) for i in range(count)]),
                cells,
                lax.ppermute(head, axis, [((i + 1) % count, i) for i in range(count)]),
            ],
            axis=dim,
        )
    return cells


def from_behind(value, axis, steps):
    count = lax.axis_size(axis)
    pairs = [(source, (source + steps) % count) for source in range(count)]
    return lax.ppermute(value, axis, pairs)


def mixed_sum(plane_sum):
    return plane_sum[2, 2] + plane_sum[0, 0] - plane_sum[2, 0] - plane_sum[0, 2]


def raw_moments(populations):
    lattice = populations.reshape((3, 3, 3) + populations.shape[1:])
    along_x = lattice.sum((1, 2))
    along_y = lattice.sum((0, 2))
    along_z = lattice.sum((0, 1))
    density = along_x.sum(0)
    return jnp.stack(
        [
            density,
            along_x[2] - along_x[0],
            along_y[2] - along_y[0],
            along_z[2] - along_z[0],
            along_x[2] + along_x[0],
            along_y[2] + along_y[0],
            along_z[2] + along_z[0],
            mixed_sum(lattice.sum(2)),
            mixed_sum(lattice.sum(1)),
            mixed_sum(lattice.sum(0)),
        ]
    )


def inverse_basis(velocity):
    square = velocity * velocity
    return [
        [(square - velocity) / 2.0, (2.0 * velocity - 1.0) / 2.0, 0.5],
        [1.0 - square, -2.0 * velocity, -1.0],
        [(square + velocity) / 2.0, (2.0 * velocity + 1.0) / 2.0, 0.5],
    ]


def place_key(first, second_index, inserted, axis):
    if axis == 0:
        return (inserted, first, second_index)
    if axis == 1:
        return (first, inserted, second_index)
    return (first, second_index, inserted)


def apply_axis(entries, velocity, axis):
    weights = inverse_basis(velocity)
    result = {}
    for first in range(3):
        for second_index in range(3):
            for target in range(3):
                summed = None
                for power in range(3):
                    source = place_key(first, second_index, power, axis)
                    if source in entries:
                        term = weights[target][power] * entries[source]
                        summed = term if summed is None else summed + term
                result[place_key(first, second_index, target, axis)] = summed
    return result


def relax(moments):
    density = moments[0]
    velocity = [moments[1] / density, moments[2] / density, moments[3] / density]

    def spread_of(row, first, second_index, diagonal):
        central = moments[row] / density - velocity[first] * velocity[second_index]
        return (1.0 - RELAXATION) * central + RELAXATION / 3.0 * diagonal

    var_xx = spread_of(4, 0, 0, 1.0)
    var_yy = spread_of(5, 1, 1, 1.0)
    var_zz = spread_of(6, 2, 2, 1.0)
    var_xy = spread_of(7, 0, 1, 0.0)
    var_xz = spread_of(8, 0, 2, 0.0)
    var_yz = spread_of(9, 1, 2, 0.0)
    entries = {
        (0, 0, 0): jnp.ones_like(density),
        (2, 0, 0): var_xx,
        (0, 2, 0): var_yy,
        (0, 0, 2): var_zz,
        (1, 1, 0): var_xy,
        (1, 0, 1): var_xz,
        (0, 1, 1): var_yz,
        (2, 2, 0): var_xx * var_yy + 2.0 * var_xy * var_xy,
        (2, 0, 2): var_xx * var_zz + 2.0 * var_xz * var_xz,
        (0, 2, 2): var_yy * var_zz + 2.0 * var_yz * var_yz,
        (2, 1, 1): var_xx * var_yz + 2.0 * var_xy * var_xz,
        (1, 2, 1): var_yy * var_xz + 2.0 * var_xy * var_yz,
        (1, 1, 2): var_zz * var_xy + 2.0 * var_xz * var_yz,
        (2, 2, 2): var_xx * var_yy * var_zz
        + 2.0 * (var_xx * var_yz * var_yz + var_yy * var_xz * var_xz + var_zz * var_xy * var_xy)
        + 8.0 * var_xy * var_yz * var_xz,
    }
    sectioned = apply_axis(entries, velocity[2], 2)
    sectioned = apply_axis(sectioned, velocity[1], 1)
    sectioned = apply_axis(sectioned, velocity[0], 0)
    return jnp.stack(
        [density * sectioned[a, b, c] for a in range(3) for b in range(3) for c in range(3)]
    )


def wall_shift(shifted, reverse, lift):
    if lift == 1:
        return jnp.concatenate([reverse[:1], shifted[:-1]], 0)
    if lift == -1:
        return jnp.concatenate([shifted[1:], reverse[-1:]], 0)
    return shifted


def interpolate(fraction, toward, second, reverse):
    near = 2.0 * fraction * toward + (1.0 - 2.0 * fraction) * second
    far = toward / (2.0 * fraction) + (2.0 * fraction - 1.0) / (2.0 * fraction) * reverse
    return jnp.where(fraction < 0.5, near, far)


def per_device(populations, solid_mask, link_cell, link_dir, link_second, link_q, link_panel):
    column_depth, tile_rows, tile_cols = populations.shape[1:]
    moments_here = raw_moments(populations)
    collided = relax(moments_here)
    padded = with_halo(collided, (("gx", 2), ("gy", 3)), 1)
    fields = []
    for direction in range(27):
        step_x = direction // 9 - 1
        step_y = direction // 3 % 3 - 1
        step_z = direction % 3 - 1
        shifted = padded[
            direction, :, 1 - step_x : 1 - step_x + tile_rows, 1 - step_y : 1 - step_y + tile_cols
        ]
        fields.append(wall_shift(shifted, collided[26 - direction], step_z))
    cell_count = column_depth * tile_rows * tile_cols
    wide_count = column_depth * (tile_rows + 2) * (tile_cols + 2)
    flat_new = jnp.stack(fields).reshape(27 * cell_count)
    flat_post = collided.reshape(27 * cell_count)
    flat_wide = padded.reshape(27 * wide_count)
    active = link_panel >= 0
    toward = flat_post[link_dir * cell_count + link_cell]
    second = flat_wide[link_dir * wide_count + link_second]
    reverse = flat_post[(26 - link_dir) * cell_count + link_cell]
    bounce = interpolate(link_q, toward, second, reverse)
    target = (26 - link_dir) * cell_count + link_cell
    flat_new = flat_new.at[target].set(jnp.where(active, bounce, flat_new[target]))
    fluid = (1 - solid_mask).astype(jnp.float32)
    populations_next = flat_new.reshape(27, column_depth, tile_rows, tile_cols) * fluid[None]
    momentum = jnp.where(active, toward + bounce, 0.0)
    velocity = jnp.stack([link_dir // 9 - 1, link_dir // 3 % 3 - 1, link_dir % 3 - 1]).astype(
        jnp.float32
    )
    pushes = velocity * momentum[None]
    streamwise = lax.axis_size("gx")
    spanwise = lax.axis_size("gy")
    owner_tile = link_panel // PAN_DEV
    offset = (owner_tile // spanwise - lax.axis_index("gx") + 1) % streamwise
    slot_index = jnp.where(active, offset * PAN_DEV + link_panel % PAN_DEV, 3 * PAN_DEV)
    partial_near = (
        jnp.zeros((3, 3 * PAN_DEV), jnp.float32).at[:, slot_index].add(pushes, mode="drop")
    )
    from_left = from_behind(partial_near[:, 2 * PAN_DEV :], "gx", 1)
    from_right = from_behind(partial_near[:, :PAN_DEV], "gx", -1)
    own_forces = partial_near[:, PAN_DEV : 2 * PAN_DEV] + from_left + from_right
    return (populations_next, own_forces)


def solution(mesh):
    return jax.shard_map(
        per_device,
        mesh=mesh,
        in_specs=(
            P(None, None, "gx", "gy"),
            P(None, "gx", "gy"),
            P(("gx", "gy")),
            P(("gx", "gy")),
            P(("gx", "gy")),
            P(("gx", "gy")),
            P(("gx", "gy")),
        ),
        out_specs=(P(None, None, "gx", "gy"), P(None, ("gx", "gy"))),
        check_vma=False,
    )
```

profile of v0, /device:TPU:0, one launch (start us, length us, event | category | flops | bytes accessed | tf_op | source)
XLA Modules:
  0.0 353.2 jit_solution(7118407350517446592)
XLA Ops:
  0.6 2.0 reduce_sum.65
  3.8 0.7 fusion.15
  4.5 1.3 add_multiply_fusion.2
  7.9 0.7 constant_dynamic-update-slice_fusion.13
  9.2 1.2 fusion.90
  10.5 10.1 %collective-permute-start.1 = (f32[27,24,1,128]{3,2,1,0:T(1,128)}, f32[27,24,1,128]{3,2,1,0:T(1,128)S(1)}, u32[]{:S(2)}, u32[]{:S(2)}) collective-permute-start(f32[27,24,1,128]{3,2,1,0:T(1,128)} %get-tuple-element.144), channel_id=1, source_target_pairs={{8,0},{16,8},{24,16},{32,24},{40,32},{48,40},{56,48},{64,56},{72,6... | collective-permute-start | bytes 995336 | tf_op jit(solution)/shard_map/ppermute | solution.py:21
  20.6 1.2 add_multiply_fusion
  21.9 0.6 broadcast_multiply_fusion.5
  22.5 1.3 add_multiply_fusion.21
  23.9 1.7 add_add_fusion.2
  25.6 1.3 add_multiply_fusion.20
  26.9 1.4 fusion.57
  28.3 1.3 add_multiply_fusion.23
  29.7 1.4 add_multiply_fusion.22
  31.0 1.3 add_multiply_fusion.19
  32.3 1.3 add_multiply_fusion.18
  33.7 0.6 compare_select_fusion
  35.6 0.6 slice.480
  36.8 40.5 %gather_fusion = f32[4096]{0:T(1024)} fusion(f32[663552]{0:T(1024)S(1)} %bitcast.272, s32[4096]{0:T(1024)S(1)} %get-tuple-element.211), kind=kCustom, calls=%fused_computation | custom fusion | bytes 49152 | tf_op jit(solution)/shard_map/gather | solution.py:167
  77.3 40.5 %gather_fusion.2 = f32[4096]{0:T(1024)} fusion(f32[663552]{0:T(1024)S(1)} %bitcast.273, s32[4096]{0:T(1024)S(1)} %get-tuple-element.212), kind=kCustom, calls=%fused_computation.2 | custom fusion | bytes 49152 | tf_op jit(solution)/shard_map/gather | solution.py:169
  117.8 1.0 pad_maximum_fusion.1
  118.8 6.2 %fusion.89 = (f32[27,24,10,1]{3,2,1,0:T(8,128)}, f32[27,24,10,1]{3,2,1,0:T(8,128)}) fusion(f32[27,24,10,128]{3,2,1,0:T(8,128)S(1)} %pad_maximum_fusion.1), kind=kLoop, calls=%fused_computation.425 | loop fusion | bytes 103680 | tf_op jit(solution)/shard_map/slice | solution.py:16
  125.0 5.4 %copy.30 = f32[27,24,10,1]{0,1,3,2:T(8,128)} copy(f32[27,24,10,1]{3,2,1,0:T(8,128)} %get-tuple-element.136) | data formatting | bytes 51840 | tf_op jit(solution)/shard_map/slice | solution.py:16
  130.4 5.4 %copy.28 = f32[27,24,10,1]{0,1,3,2:T(8,128)} copy(f32[27,24,10,1]{3,2,1,0:T(8,128)} %get-tuple-element.137) | data formatting | bytes 51840 | tf_op jit(solution)/shard_map/slice | solution.py:15
  135.8 3.5 %collective-permute-start.2 = (f32[27,24,10,1]{0,1,3,2:T(8,128)}, f32[27,24,10,1]{0,1,3,2:T(8,128)}, u32[]{:S(2)}, u32[]{:S(2)}) collective-permute-start(f32[27,24,10,1]{0,1,3,2:T(8,128)} %copy.28), channel_id=1, source_target_pairs={{1,0},{2,1},{3,2},{4,3},{5,4},{6,5},{7,6},{0,7},{9,8},{10,9},{11,1... | collective-permute-start | bytes 77768 | tf_op jit(solution)/shard_map/ppermute | solution.py:21
  139.4 6.7 %copy.31 = f32[27,24,10,1]{3,2,1,0:T(8,128)} copy(f32[27,24,10,1]{0,1,3,2:T(8,128)} %collective-permute-done.3) | data formatting | bytes 51840 | tf_op jit(solution)/shard_map/ppermute | solution.py:19
  146.2 6.7 %copy.29 = f32[27,24,10,1]{3,2,1,0:T(8,128)} copy(f32[27,24,10,1]{0,1,3,2:T(8,128)} %collective-permute-done.2) | data formatting | bytes 51840 | tf_op jit(solution)/shard_map/ppermute | solution.py:21
  152.9 12.8 %pad_maximum_fusion = f32[27,24,10,130]{3,2,1,0:T(8,128)} fusion(f32[27,24,10,1]{3,2,1,0:T(8,128)} %copy.29, f32[27,24,1,128]{3,2,1,0:T(1,128)S(1)} %collective-permute-done.1, f32[27,24,8,128]{3,2,1,0:T(8,128)S(1)} %constant_dynamic-update-slice_fusion, f32[27,24,1,128]{3,2,1,0:T(1,128)S(1)} %collective-permute-done, f32[27,24,10,1]{3,2,1,0:T(8,128)} %copy.31), kind=kLoop, calls=%fused_computation.6 | loop fusion | flops 3369600 | bytes 6739200 | tf_op jit(solution)/shard_map/concatenate | solution.py:17
  165.7 7.4 %reshape.532 = f32[842400]{0:T(1024)} reshape(f32[27,24,10,130]{3,2,1,0:T(8,128)} %pad_maximum_fusion) | data formatting | bytes 6739200 | tf_op jit(solution)/shard_map/reshape | solution.py:165
  173.1 1.6 maximum_bitcast_fusion.25
  174.7 0.6 constant_dynamic-update-slice_fusion.53
  175.4 2.1 constant_dynamic-update-slice_fusion.52
  177.5 0.6 constant_dynamic-update-slice_fusion.51
  178.1 0.6 constant_dynamic-update-slice_fusion.50
  178.8 0.7 constant_dynamic-update-slice_fusion.49
  179.4 0.6 constant_dynamic-update-slice_fusion.48
  180.1 0.6 constant_dynamic-update-slice_fusion.47
  180.8 0.8 constant_dynamic-update-slice_fusion.46
  181.6 0.6 constant_dynamic-update-slice_fusion.45
  182.9 0.6 constant_dynamic-update-slice_fusion.44
  183.6 0.8 constant_dynamic-update-slice_fusion.43
  184.4 0.6 constant_dynamic-update-slice_fusion.42
  185.0 0.6 constant_dynamic-update-slice_fusion.41
  185.7 0.6 constant_dynamic-update-slice_fusion.40
  186.3 0.6 constant_dynamic-update-slice_fusion.39
  187.7 0.6 constant_dynamic-update-slice_fusion.38
  188.3 0.8 constant_dynamic-update-slice_fusion.37
  189.1 0.6 constant_dynamic-update-slice_fusion.36
  189.7 0.6 constant_dynamic-update-slice_fusion.35
  190.4 0.8 constant_dynamic-update-slice_fusion.34
  191.2 0.6 constant_dynamic-update-slice_fusion.33
  191.8 0.6 constant_dynamic-update-slice_fusion.32
  192.5 0.7 constant_dynamic-update-slice_fusion.31
  193.1 0.6 constant_dynamic-update-slice_fusion.30
  193.8 0.6 constant_dynamic-update-slice_fusion.29
  194.4 0.8 constant_dynamic-update-slice_fusion.28
  195.2 0.6 constant_dynamic-update-slice_fusion.27
  195.8 52.1 %gather_fusion.3 = f32[4096]{0:T(1024)S(1)} fusion(f32[663552]{0:T(1024)} %bitcast.48, s32[4096]{0:T(1024)S(1)} %get-tuple-element.212), kind=kCustom, calls=%fused_computation.3 | custom fusion | bytes 49152 | tf_op jit(solution)/shard_map/gather | solution.py:172
  248.0 48.7 %gather_fusion.1 = f32[4096]{0:T(1024)S(1)} fusion(f32[842400]{0:T(1024)} %reshape.532, s32[4096]{0:T(1024)S(1)} %copy-done.18), kind=kCustom, calls=%fused_computation.1 | custom fusion | bytes 49152 | tf_op jit(solution)/shard_map/gather | solution.py:168
  297.5 22.5 %scatter_custom_fusion.1 = f32[3,384]{0,1:T(8,128)S(1)} fusion(s32[4096]{0:T(1024)} %compare_select_fusion, f32[4096,3]{1,0:T(8,128)S(1)} %copy.34, f32[]{:T(128)} %constant.110.clone.1), kind=kCustom, calls=%fused_computation.188 | custom fusion | flops 12288 | bytes 5120 | tf_op jit(solution)/shard_map/scatter-add | solution.py:186
  320.0 10.2 %collective-permute-start.5 = (f32[3,128]{0,1:T(8,128)S(1)}, f32[3,128]{0,1:T(8,128)S(1)}, u32[]{:S(2)}, u32[]{:S(2)}) collective-permute-start(f32[3,128]{0,1:T(8,128)S(1)} %get-tuple-element.182), channel_id=1, source_target_pairs={{0,248},{8,0},{16,8},{24,16},{32,24},{40,32},{48,40},{56,48},{64,5... | collective-permute-start | bytes 4616 | tf_op jit(solution)/shard_map/ppermute | solution.py:31
  330.3 18.7 %scatter_fusion = f32[663552]{0:T(1024)} fusion(f32[663552]{0:T(1024)} %bitcast.48, s32[4096]{0:T(1024)S(1)} %copy-done.14, f32[4096]{0:T(1024)S(1)} %fusion.74), kind=kCustom, calls=%fused_computation.4 | custom fusion | bytes 65536 | tf_op jit(solution)/shard_map/scatter | solution.py:172
  349.0 3.5 broadcast_multiply_fusion
  352.6 0.7 copy.35
  (135 shorter events, 7.8 us)
Async XLA Ops:
  0.6 2.5 copy-start
  5.8 14.8 %copy-start.1 = (f32[24,8,128]{2,1,0:T(8,128)}, f32[24,8,128]{2,1,0:T(8,128)S(1)}, u32[]{:S(2)}) copy-start(f32[24,8,128]{2,1,0:T(8,128)S(1)} %get-tuple-element.31) | copy-start | bytes 294916
  5.8 14.8 %copy-start.2 = (f32[24,8,128]{2,1,0:T(8,128)}, f32[24,8,128]{2,1,0:T(8,128)S(1)}, u32[]{:S(2)}) copy-start(f32[24,8,128]{2,1,0:T(8,128)S(1)} %get-tuple-element.33) | copy-start | bytes 294916
  5.8 14.8 %copy-start.3 = (f32[24,8,128]{2,1,0:T(8,128)}, f32[24,8,128]{2,1,0:T(8,128)S(1)}, u32[]{:S(2)}) copy-start(f32[24,8,128]{2,1,0:T(8,128)S(1)} %get-tuple-element.37) | copy-start | bytes 294916
  5.8 14.8 %copy-start.4 = (f32[24,8,128]{2,1,0:T(8,128)}, f32[24,8,128]{2,1,0:T(8,128)S(1)}, u32[]{:S(2)}) copy-start(f32[24,8,128]{2,1,0:T(8,128)S(1)} %get-tuple-element.39) | copy-start | bytes 294916
  5.8 14.8 %copy-start.5 = (f32[24,8,128]{2,1,0:T(8,128)}, f32[24,8,128]{2,1,0:T(8,128)S(1)}, u32[]{:S(2)}) copy-start(f32[24,8,128]{2,1,0:T(8,128)S(1)} %get-tuple-element.40) | copy-start | bytes 294916
  5.8 14.8 %copy-start.6 = (f32[24,8,128]{2,1,0:T(8,128)}, f32[24,8,128]{2,1,0:T(8,128)S(1)}, u32[]{:S(2)}) copy-start(f32[24,8,128]{2,1,0:T(8,128)S(1)} %get-tuple-element.41) | copy-start | bytes 294916
  10.5 107.3 %collective-permute-start.1 = (f32[27,24,1,128]{3,2,1,0:T(1,128)}, f32[27,24,1,128]{3,2,1,0:T(1,128)S(1)}, u32[]{:S(2)}, u32[]{:S(2)}) collective-permute-start(f32[27,24,1,128]{3,2,1,0:T(1,128)} %get-tuple-element.144), channel_id=1, source_target_pairs={{8,0},{16,8},{24,16},{32,24},{40,32},{48,40},{56,48},{64,56},{72,6... | collective-permute-start | bytes 995336 | tf_op jit(solution)/shard_map/ppermute | solution.py:21
  20.6 97.2 %collective-permute-start = (f32[27,24,1,128]{3,2,1,0:T(1,128)}, f32[27,24,1,128]{3,2,1,0:T(1,128)S(1)}, u32[]{:S(2)}, u32[]{:S(2)}) collective-permute-start(f32[27,24,1,128]{3,2,1,0:T(1,128)} %get-tuple-element.143), channel_id=1, source_target_pairs={{0,8},{8,16},{16,24},{24,32},{32,40},{40,48},{48,56},{56,64},{64,7... | collective-permute-start | bytes 995336 | tf_op jit(solution)/shard_map/ppermute | solution.py:19
  20.6 13.0 %copy-start.12 = (s32[4096]{0:T(1024)S(1)}, s32[4096]{0:T(1024)}, u32[]{:S(2)}) copy-start(s32[4096]{0:T(1024)} %param.13) | copy-start | bytes 49156
  22.5 11.8 %copy-start.7 = (f32[24,8,128]{2,1,0:T(8,128)S(1)}, f32[24,8,128]{2,1,0:T(8,128)}, u32[]{:S(2)}) copy-start(f32[24,8,128]{2,1,0:T(8,128)} %get-tuple-element.197) | copy-start | bytes 294916
  22.5 13.0 %copy-start.9 = (f32[24,8,128]{2,1,0:T(8,128)S(1)}, f32[24,8,128]{2,1,0:T(8,128)}, u32[]{:S(2)}) copy-start(f32[24,8,128]{2,1,0:T(8,128)} %get-tuple-element.22) | copy-start | bytes 294916
  77.3 40.5 %copy-start.13 = (s32[24,8,128]{2,1,0:T(8,128)S(1)}, s32[24,8,128]{2,1,0:T(8,128)}, u32[]{:S(2)}) copy-start(s32[24,8,128]{2,1,0:T(8,128)} %param.8) | copy-start | bytes 294916
  130.4 9.0 %collective-permute-start.3 = (f32[27,24,10,1]{0,1,3,2:T(8,128)}, f32[27,24,10,1]{0,1,3,2:T(8,128)}, u32[]{:S(2)}, u32[]{:S(2)}) collective-permute-start(f32[27,24,10,1]{0,1,3,2:T(8,128)} %copy.30), channel_id=1, source_target_pairs={{0,1},{1,2},{2,3},{3,4},{4,5},{5,6},{6,7},{7,0},{8,9},{9,10},{10,1... | collective-permute-start | bytes 77768 | tf_op jit(solution)/shard_map/ppermute | solution.py:19
  135.8 10.3 %collective-permute-start.2 = (f32[27,24,10,1]{0,1,3,2:T(8,128)}, f32[27,24,10,1]{0,1,3,2:T(8,128)}, u32[]{:S(2)}, u32[]{:S(2)}) collective-permute-start(f32[27,24,10,1]{0,1,3,2:T(8,128)} %copy.28), channel_id=1, source_target_pairs={{1,0},{2,1},{3,2},{4,3},{5,4},{6,5},{7,6},{0,7},{9,8},{10,9},{11,1... | collective-permute-start | bytes 77768 | tf_op jit(solution)/shard_map/ppermute | solution.py:21
  173.1 1.6 copy-start.29
  174.7 6.0 %slice-start = ((s8[5308416]{0:T(1024)(128)(4,1)}), s8[4194304]{0:T(1024)(128)(4,1)S(1)}, s32[]{:S(2)}) async-start(s8[5308416]{0:T(1024)(128)(4,1)} %bitcast.274), calls=%async_computation | async-start | bytes 8388608
  175.4 2.1 copy-start.30
  175.4 2.8 copy-start.34
  175.4 5.4 %slice-start.1 = ((s8[5308416]{0:T(1024)(128)(4,1)}), s8[1114112]{0:T(1024)(128)(4,1)S(1)}, s32[]{:S(2)}) async-start(s8[5308416]{0:T(1024)(128)(4,1)} %bitcast.274), calls=%async_computation.1 | async-start | bytes 2228224
  177.5 2.0 copy-start.35
  177.5 2.6 copy-start.27
  178.8 3.4 slice-start.2
  180.7 0.8 copy-start.28
  180.8 1.5 slice-start.3
  182.2 0.7 copy-start.25
  183.5 0.8 copy-start.26
  183.5 1.5 copy-start.11
  183.5 1.5 copy-start.37
  183.5 2.1 copy-start.8
  183.6 2.8 copy-start.10
  183.6 2.8 copy-start.36
  187.0 0.7 copy-start.23
  188.3 0.8 copy-start.24
  188.3 1.4 copy-start.21
  190.4 0.8 copy-start.22
  190.4 1.4 copy-start.32
  191.2 2.0 copy-start.33
  195.8 52.1 %copy-start.18 = (s32[4096]{0:T(1024)S(1)}, s32[4096]{0:T(1024)}, u32[]{:S(2)}) copy-start(s32[4096]{0:T(1024)} %get-tuple-element.210) | copy-start | bytes 49156
  247.9 48.8 %copy-start.19 = (f32[4096]{0:T(1024)S(1)}, f32[4096]{0:T(1024)}, u32[]{:S(2)}) copy-start(f32[4096]{0:T(1024)} %gather_fusion) | copy-start | bytes 49156
  247.9 48.8 %copy-start.20 = (f32[4096]{0:T(1024)S(1)}, f32[4096]{0:T(1024)}, u32[]{:S(2)}) copy-start(f32[4096]{0:T(1024)} %gather_fusion.2) | copy-start | bytes 49156
  248.0 48.8 %copy-start.31 = (f32[4096]{0:T(1024)S(1)}, f32[4096]{0:T(1024)}, u32[]{:S(2)}) copy-start(f32[4096]{0:T(1024)} %param.12) | copy-start | bytes 49156
  248.0 48.8 %copy-start.15 = (s32[4096]{0:T(1024)S(1)}, s32[4096]{0:T(1024)}, u32[]{:S(2)}) copy-start(s32[4096]{0:T(1024)} %get-tuple-element.209) | copy-start | bytes 49156
  248.0 48.8 %copy-start.16 = (s32[4096]{0:T(1024)S(1)}, s32[4096]{0:T(1024)}, u32[]{:S(2)}) copy-start(s32[4096]{0:T(1024)} %get-tuple-element.214) | copy-start | bytes 49156
  248.0 48.8 %copy-start.17 = (s32[4096]{0:T(1024)S(1)}, s32[4096]{0:T(1024)}, u32[]{:S(2)}) copy-start(s32[4096]{0:T(1024)} %get-tuple-element.215) | copy-start | bytes 49156
  296.7 33.6 %copy-start.14 = (s32[4096]{0:T(1024)S(1)}, s32[4096]{0:T(1024)}, u32[]{:S(2)}) copy-start(s32[4096]{0:T(1024)} %get-tuple-element.213) | copy-start | bytes 49156
  320.0 32.5 %collective-permute-start.5 = (f32[3,128]{0,1:T(8,128)S(1)}, f32[3,128]{0,1:T(8,128)S(1)}, u32[]{:S(2)}, u32[]{:S(2)}) collective-permute-start(f32[3,128]{0,1:T(8,128)S(1)} %get-tuple-element.182), channel_id=1, source_target_pairs={{0,248},{8,0},{16,8},{24,16},{32,24},{40,32},{48,40},{56,48},{64,5... | collective-permute-start | bytes 4616 | tf_op jit(solution)/shard_map/ppermute | solution.py:31
  330.3 22.3 %collective-permute-start.4 = (f32[3,128]{0,1:T(8,128)S(1)}, f32[3,128]{0,1:T(8,128)S(1)}, u32[]{:S(2)}, u32[]{:S(2)}) collective-permute-start(f32[3,128]{0,1:T(8,128)S(1)} %get-tuple-element.181), channel_id=1, source_target_pairs={{0,8},{8,16},{16,24},{24,32},{32,40},{40,48},{48,56},{56,64},{64,7... | collective-permute-start | bytes 4616 | tf_op jit(solution)/shard_map/ppermute | solution.py:31
where the time goes:
time: 357 us; the launch traced here: 353 us
  local copies, waits for them, and re-layouts  245 us (69%)
  other arithmetic  82.8 us (23%)
  starting transfers between devices  23.9 us (7%)
    gather x1, local copies, waits for them, and re-layouts, per_device(): flat_new[target]  52.1 us
    gather x1, local copies, waits for them, and re-layouts, per_device(): second = flat_wide[link_dir * wide_count + link_second]  48.7 us
    gather x1, local copies, waits for them, and re-layouts, per_device(): toward = flat_post[link_dir * cell_count + link_cell]  40.5 us
    gather x1, local copies, waits for them, and re-layouts, per_device(): reverse = flat_post[(26 - link_dir) * cell_count + link_cell]  40.5 us
    scatter-add x1, other arithmetic, per_device(): jnp.zeros((3, 3 * PAN_DEV), jnp.float32).at[:, slot_index]  22.5 us
    unnamed x53, other arithmetic  21.6 us
    scatter x1, local copies, waits for them, and re-layouts, per_device(): flat_new.at[target].set(jnp.where(active, bounce, flat_new[target]))  18.7 us
    concatenate x2, other arithmetic, with_halo(): jnp.concatenate([lax.ppermute(tail, axis, [(i, (i + 1) % count) for i in...  13.8 us
  transfers between devices with their start and end apart: 6, of which 0 were waited for; matrix products, arithmetic and copies ran while one was open for 37% of the time, Pallas kernels for 0%

commit v1 on v0

v1 whole, which is shorter than its diff:
```python
import functools

import jax
import jax.numpy as jnp
from jax import lax
from jax.experimental import pallas as pl
from jax.experimental.pallas import tpu as pltpu
from jax.sharding import PartitionSpec as P

PAN_DEV = 128
RELAXATION = 1.7
DEPTH, ROWS, COLS = 24, 8, 128
PLANES = DEPTH * ROWS
LINKS = 4096
HALF = DEPTH // 2
CHUNKS = 8
F32 = jnp.float32
BF16 = jnp.bfloat16
VMEM = pltpu.VMEM
WHOLE = pl.BlockSpec(memory_space=pltpu.VMEM)
SOMEWHERE = pl.BlockSpec(memory_space=pl.ANY)


def params(mib):
    return pltpu.CompilerParams(vmem_limit_bytes=mib * 2**20)


def plane_rows(index, z):
    return pl.ds(pl.multiple_of((index * DEPTH + z) * ROWS, ROWS), ROWS)


def inverse_map(m0, m1, m2, u):
    if m0 is None and m1 is None and m2 is None:
        return None, None, None
    w = None if m0 is None else u * m0
    if m1 is not None:
        w = m1 if w is None else w + m1
    t = None
    if w is not None:
        t = u * (w if m1 is None else w + m1)
    if m2 is not None:
        t = m2 if t is None else t + m2
    if w is None:
        return t, -t, t
    return t - w, (-t if m0 is None else m0 - t), t + w


def collide(f):
    def at(a, b, c):
        return f[a * 9 + b * 3 + c]

    ends = [[at(a, b, 2) + at(a, b, 0) for b in range(3)] for a in range(3)]
    dz = [[at(a, b, 2) - at(a, b, 0) for b in range(3)] for a in range(3)]
    s = [[ends[a][b] + at(a, b, 1) for b in range(3)] for a in range(3)]
    row = [s[a][0] + s[a][1] + s[a][2] for a in range(3)]
    density = row[0] + row[1] + row[2]
    q0 = s[0][0] + s[1][0] + s[2][0]
    q2 = s[0][2] + s[1][2] + s[2][2]
    dzx = [dz[a][0] + dz[a][1] + dz[a][2] for a in range(3)]
    dzy0 = dz[0][0] + dz[1][0] + dz[2][0]
    dzy2 = dz[0][2] + dz[1][2] + dz[2][2]
    pzz = sum(ends[a][b] for a in range(3) for b in range(3))
    inv = 1.0 / density
    ux = (row[2] - row[0]) * inv
    uy = (q2 - q0) * inv
    uz = (dzx[0] + dzx[1] + dzx[2]) * inv
    keep = 1.0 - RELAXATION
    third = RELAXATION / 3.0

    def spread(p, first, second):
        return keep * (p * inv - first * second)

    xx = spread(row[2] + row[0], ux, ux) + third
    yy = spread(q2 + q0, uy, uy) + third
    zz = spread(pzz, uz, uz) + third
    xy = spread((s[2][2] - s[2][0]) + (s[0][0] - s[0][2]), ux, uy)
    xz = spread(dzx[2] - dzx[0], ux, uz)
    yz = spread(dzy2 - dzy0, uy, uz)
    xy2, xz2, yz2 = 2.0 * xy, 2.0 * xz, 2.0 * yz
    e220 = xx * yy + xy2 * xy
    e202 = xx * zz + xz2 * xz
    eyz = yy * zz + yz2 * yz
    e211 = xx * yz + xy2 * xz
    e121 = yy * xz + xy2 * yz
    e112 = zz * xy + xz2 * yz
    e222 = xx * eyz + xz2 * e121 + xy2 * e112
    k = {
        (0, 0, 0): jnp.ones_like(density),
        (2, 0, 0): xx,
        (0, 2, 0): yy,
        (0, 0, 2): zz,
        (1, 1, 0): xy,
        (1, 0, 1): xz,
        (0, 1, 1): yz,
        (2, 2, 0): e220,
        (2, 0, 2): e202,
        (0, 2, 2): eyz,
        (2, 1, 1): e211,
        (1, 2, 1): e121,
        (1, 1, 2): e112,
        (2, 2, 2): e222,
    }
    along_z, along_y, result = {}, {}, [None] * 27
    for a in range(3):
        for b in range(3):
            out = inverse_map(k.get((a, b, 0)), k.get((a, b, 1)), k.get((a, b, 2)), uz)
            for c in range(3):
                along_z[a, b, c] = out[c]
    for a in range(3):
        for c in range(3):
            out = inverse_map(along_z[a, 0, c], along_z[a, 1, c], along_z[a, 2, c], uy)
            for b in range(3):
                along_y[a, b, c] = out[b]
    scale = [density, 0.5 * density, 0.25 * density, 0.125 * density]
    for b in range(3):
        for c in range(3):
            out = inverse_map(along_y[0, b, c], along_y[1, b, c], along_y[2, b, c], ux)
            for a in range(3):
                moving = abs(a - 1) + abs(b - 1) + abs(c - 1)
                result[a * 9 + b * 3 + c] = scale[moving] * out[a]
    return result


def collide_kernel(pop_ref, col_ref, near_ref, far_ref, buf, sem):
    even = lax.rem(lax.axis_index("gy"), 2) == 0
    step = DEPTH // CHUNKS
    copies = [
        pltpu.make_async_copy(
            pop_ref.at[:, pl.ds(i * step, step)], buf.at[:, pl.ds(i * step, step)], sem.at[i]
        )
        for i in range(CHUNKS)
    ]
    for copy in copies:
        copy.start()
    lane = lax.broadcasted_iota(jnp.int32, (ROWS, COLS), 1)

    def body(z, carry):
        low, high = carry
        f = collide([buf[d, z] for d in range(27)])
        first = lax.rem(z, HALF) * 9
        for d in range(27):
            col_ref[plane_rows(d, z), :] = f[d]
        for a in range(3):
            for c in range(3):
                spot = first + a * 3 + c
                here = lane == spot
                low = jnp.where(here, pltpu.roll(f[a * 9 + c], spot, 1), low)
                high = jnp.where(here, pltpu.roll(f[a * 9 + 6 + c], spot + 1, 1), high)
        return low, high

    zero = jnp.zeros((ROWS, COLS), F32)
    for half in range(2):
        carry = (zero, zero)
        for i in range(half * CHUNKS // 2, (half + 1) * CHUNKS // 2):
            copies[i].wait()
            carry = lax.fori_loop(i * step, (i + 1) * step, body, carry)
        low, high = carry
        near_ref[half] = jnp.where(even, high, low)
        far_ref[half] = jnp.where(even, low, high)


def side_kernel(col_ref, near_ref, far_ref, side_ref, pair_ref, other_ref, edges):
    even = lax.rem(lax.axis_index("gy"), 2) == 0
    even_x = lax.rem(lax.axis_index("gx"), 2) == 0
    lane = lax.broadcasted_iota(jnp.int32, (ROWS, COLS), 1)
    for half in range(2):
        edges[0, half] = jnp.where(even, far_ref[half], near_ref[half])
        edges[1, half] = jnp.where(even, near_ref[half], far_ref[half])

    def body(z, half):
        first = (z - half * HALF) * 9
        low, high = edges[0, half], edges[1, half]
        for a in range(3):
            for c in range(3):
                spot = first + a * 3 + c
                up = pltpu.roll(col_ref[plane_rows(a * 9 + 6 + c, z), :], 1, 1)
                up = jnp.where(lane == 0, pltpu.roll(low, COLS - spot, 1), up)
                side_ref[plane_rows(a * 6 + 3 + c, z), :] = up
                down = pltpu.roll(col_ref[plane_rows(a * 9 + c, z), :], COLS - 1, 1)
                down = jnp.where(
                    lane == COLS - 1, pltpu.roll(high, COLS - 1 - spot, 1), down
                )
                side_ref[plane_rows(a * 6 + c, z), :] = down
        return half

    for half in range(2):
        lax.fori_loop(half * HALF, (half + 1) * HALF, body, half)
    for ref, forward in ((pair_ref, even_x), (other_ref, jnp.logical_not(even_x))):
        a = jnp.where(forward, 2, 0)
        x = jnp.where(forward, ROWS - 1, 0)
        for b in range(3):
            for c in range(3):
                if b == 1:
                    source, start = col_ref, (a * 9 + 3 + c) * PLANES + x
                else:
                    source, start = side_ref, (a * 6 + (b // 2) * 3 + c) * PLANES + x
                ref[b * 3 + c] = source[pl.ds(start, DEPTH, stride=ROWS), :]


def table_kernel(cell_ref, dir_ref, q_ref, panel_ref, dense_ref, row_ref, lane_ref, pan_ref, push_ref):
    gx = lax.axis_index("gx")
    count = lax.axis_size("gx")
    per_row = PAN_DEV * lax.axis_size("gy")
    width = 256
    row_iota = lax.broadcasted_iota(jnp.int32, (PLANES, width), 0)
    lane_iota = lax.broadcasted_iota(jnp.int32, (COLS, width), 0)
    push_iota = lax.broadcasted_iota(jnp.int32, (24, width), 0)
    dense_ref[...] = jnp.zeros_like(dense_ref)

    def load(ref, i):
        return jnp.concatenate([ref[pl.ds(2 * i, 1), :], ref[pl.ds(2 * i + 1, 1), :]], axis=1)

    def body(i, carry):
        at = pl.ds(pl.multiple_of(i * width, width), width)
        cell, direction = load(cell_ref, i), load(dir_ref, i)
        q, panel = load(q_ref, i), load(panel_ref, i)
        active = panel >= 0
        near = q < 0.5
        twice = 2.0 * q
        weight = jnp.where(near, twice, 1.0 / twice)
        weight_hi = weight.astype(BF16).astype(F32)
        weight_lo = weight - weight_hi
        code = (direction + 1 + jnp.where(near, 27, 0)).astype(F32)
        row = jnp.where(active, cell // COLS, -1)
        rows = jnp.where(row_iota == row, 1.0, 0.0).astype(BF16)
        row_ref[:, at] = rows
        here = lane_iota == cell % COLS
        lane_ref[:, at] = jnp.where(here, 1.0, 0.0).astype(BF16)
        values = jnp.concatenate(
            [jnp.where(here, v, 0.0).astype(BF16) for v in (weight_hi, weight_lo, code)], axis=0
        )
        dense_ref[...] += lax.dot_general(
            rows, values, (((1,), (1,)), ((), ())), preferred_element_type=F32
        )
        pan_ref[:, at] = jnp.where(lane_iota == panel % PAN_DEV, 1.0, 0.0).astype(BF16)
        offset = panel // per_row - gx + 1
        offset = jnp.where(offset < 0, offset + count, offset)
        offset = jnp.where(offset >= count, offset - count, offset)
        part = push_iota % 8
        step = jnp.where(
            part == 0,
            direction // 9 - 1,
            jnp.where(part == 1, direction // 3 % 3 - 1, direction % 3 - 1),
        )
        chosen = active & (push_iota // 8 == offset) & (part < 3)
        push_ref[:, at] = jnp.where(chosen, step, 0).astype(F32)
        return carry

    lax.fori_loop(0, LINKS // width, body, 0)


def stream_kernel(
    col_ref, side_ref, pair_ref, other_ref, dense_ref, row_ref, lane_ref, pan_ref, push_ref, mask_ref,
    out_ref, own_ref, send_pair_ref, send_other_ref,
    buf, halo, momentum, sem,
):
    even_x = lax.rem(lax.axis_index("gx"), 2) == 0
    halo[0] = jnp.where(even_x, other_ref[...], pair_ref[...])
    halo[1] = jnp.where(even_x, pair_ref[...], other_ref[...])
    sub = lax.broadcasted_iota(jnp.int32, (ROWS, COLS), 0)

    def body(z, bottom, top):
        code = dense_ref[pl.ds(pl.multiple_of(z * ROWS, ROWS), ROWS), 2 * COLS : 3 * COLS]
        weight = (
            dense_ref[pl.ds(pl.multiple_of(z * ROWS, ROWS), ROWS), :COLS]
            + dense_ref[pl.ds(pl.multiple_of(z * ROWS, ROWS), ROWS), COLS : 2 * COLS]
        )
        fluid = (1 - mask_ref[z]).astype(F32)
        near = code > 27.5
        which = jnp.where(near, code - 28.0, code - 1.0)
        toward = jnp.zeros((ROWS, COLS), F32)
        second, reverse = toward, toward
        for d in range(27):
            a, b, c = d // 9, d // 3 % 3, d % 3
            here = col_ref[plane_rows(d, z), :]
            back = col_ref[plane_rows(26 - d, z), :]
            if (c == 2 and bottom) or (c == 0 and top):
                moved = back
            else:
                zs = z - (c - 1)
                if b == 1:
                    moved = col_ref[plane_rows(d, zs), :]
                else:
                    moved = side_ref[plane_rows(a * 6 + (b // 2) * 3 + c, zs), :]
                if a == 2:
                    edge = halo[0, b * 3 + c, pl.ds(zs, 1), :]
                    moved = jnp.where(sub == 0, edge, pltpu.roll(moved, 1, 0))
                elif a == 0:
                    edge = halo[1, b * 3 + c, pl.ds(zs, 1), :]
                    moved = jnp.where(sub == ROWS - 1, edge, pltpu.roll(moved, ROWS - 1, 0))
            buf[d, z] = moved
            if d != 13:
                match = which == float(d)
                toward = jnp.where(match, here, toward)
                second = jnp.where(match, moved, second)
                reverse = jnp.where(match, back, reverse)
        other = jnp.where(near, second, reverse)
        bounce = other + weight * (toward - other)
        momentum[pl.ds(pl.multiple_of(z * ROWS, ROWS), ROWS), :] = jnp.where(
            code > 0.5, toward + bounce, 0.0
        )
        for d in range(27):
            value = buf[d, z]
            if d != 13:
                value = jnp.where(which == float(26 - d), bounce, value)
            buf[d, z] = value * fluid

    body(0, True, False)
    lax.fori_loop(1, DEPTH - 1, lambda z, carry: (body(z, False, False), carry)[1], 0)
    body(DEPTH - 1, False, True)
    copy = pltpu.make_async_copy(buf, out_ref, sem)
    copy.start()

    turned = momentum[...].T
    turned_hi = turned.astype(BF16)
    turned_lo = (turned - turned_hi.astype(F32)).astype(BF16)
    width = 512

    def gather(i, total):
        at = pl.ds(pl.multiple_of(i * width, width), width)
        rows = row_ref[:, at]
        picked = jnp.dot(turned_hi, rows, preferred_element_type=F32) + jnp.dot(
            turned_lo, rows, preferred_element_type=F32
        )
        value = jnp.sum(picked * lane_ref[:, at].astype(F32), axis=0, keepdims=True)
        push = push_ref[:, at] * value
        push_hi = push.astype(BF16).astype(F32)
        push = jnp.concatenate([push_hi, push - push_hi], axis=0).astype(BF16)
        return total + lax.dot_general(
            push, pan_ref[:, at], (((1,), (1,)), ((), ())), preferred_element_type=F32
        )

    total = lax.fori_loop(0, LINKS // width, gather, jnp.zeros((48, PAN_DEV), F32))
    force = total[:24] + total[24:]
    own_ref[...] = force[8:16]
    send_pair_ref[...] = jnp.where(even_x, force[16:24], force[0:8])
    send_other_ref[...] = jnp.where(even_x, force[0:8], force[16:24])
    copy.wait()


def pair_swap(count):
    return [(i, i ^ 1) for i in range(count)]


def other_swap(count):
    return [(i, (i + 1) % count if i % 2 else (i - 1) % count) for i in range(count)]


def per_device(populations, solid_mask, link_cell, link_dir, link_second, link_q, link_panel):
    nx, ny = lax.axis_size("gx"), lax.axis_size("gy")
    small = jax.ShapeDtypeStruct((ROWS, PAN_DEV), F32)
    column = jax.ShapeDtypeStruct((2, ROWS, COLS), F32)
    edge = jax.ShapeDtypeStruct((9, DEPTH, COLS), F32)
    collided, y_pair, y_other = pl.pallas_call(
        collide_kernel,
        out_shape=(VMEM((27 * PLANES, COLS), F32), column, column),
        in_specs=[SOMEWHERE],
        scratch_shapes=[VMEM((27, DEPTH, ROWS, COLS), F32), pltpu.SemaphoreType.DMA((CHUNKS,))],
        compiler_params=params(16),
        name="collide",
    )(populations)
    y_other = lax.ppermute(y_other, "gy", other_swap(ny))
    y_pair = lax.ppermute(y_pair, "gy", pair_swap(ny))
    tables = [t.reshape(LINKS // COLS, COLS) for t in (link_cell, link_dir, link_q, link_panel)]
    dense = pl.pallas_call(
        table_kernel,
        out_shape=(
            VMEM((PLANES, 3 * COLS), F32),
            VMEM((PLANES, LINKS), BF16),
            VMEM((COLS, LINKS), BF16),
            VMEM((PAN_DEV, LINKS), BF16),
            VMEM((24, LINKS), F32),
        ),
        in_specs=[WHOLE] * 4,
        compiler_params=params(16),
        cost_estimate=pl.CostEstimate(flops=6 * 10**9, bytes_accessed=70000, transcendentals=0),
        name="tables",
    )(*tables)
    side, x_pair, x_other = pl.pallas_call(
        side_kernel,
        out_shape=(VMEM((18 * PLANES, COLS), F32), edge, edge),
        in_specs=[WHOLE] * 3,
        scratch_shapes=[VMEM((2, 2, ROWS, COLS), F32)],
        compiler_params=params(16),
        name="sides",
    )(collided, y_pair, y_other)
    x_other = lax.ppermute(x_other, "gx", other_swap(nx))
    x_pair = lax.ppermute(x_pair, "gx", pair_swap(nx))
    populations_next, own, to_pair, to_other = pl.pallas_call(
        stream_kernel,
        out_shape=(jax.ShapeDtypeStruct(populations.shape, F32), small, small, small),
        in_specs=[WHOLE] * 10,
        out_specs=(SOMEWHERE, WHOLE, WHOLE, WHOLE),
        scratch_shapes=[
            VMEM((27, DEPTH, ROWS, COLS), F32),
            VMEM((2, 9, DEPTH, COLS), F32),
            VMEM((PLANES, COLS), F32),
            pltpu.SemaphoreType.DMA,
        ],
        compiler_params=params(24),
        name="stream",
    )(collided, side, x_pair, x_other, *dense, solid_mask)
    from_other = lax.ppermute(to_other, "gx", other_swap(nx))
    from_pair = lax.ppermute(to_pair, "gx", pair_swap(nx))
    return populations_next, (own + from_pair + from_other)[:3]


def solution(mesh):
    return jax.shard_map(
        per_device,
        mesh=mesh,
        in_specs=(
            P(None, None, "gx", "gy"),
            P(None, "gx", "gy"),
            P(("gx", "gy")),
            P(("gx", "gy")),
            P(("gx", "gy")),
            P(("gx", "gy")),
            P(("gx", "gy")),
        ),
        out_specs=(P(None, None, "gx", "gy"), P(None, ("gx", "gy"))),
        check_vma=False,
    )
```

time: 357 us -> 46.9 us (0.13); the launches traced: 353 us -> 46.8 us
  local copies, waits for them, and re-layouts: 245 us -> 2.35 us
  other arithmetic: 82.8 us -> 0.01 us
  Pallas kernels: 0 us -> 15.8 us
  waiting for transfers between devices: 0.02 us -> 5.77 us
    gather x4 -> x0, local copies, waits for them, and re-layouts: 182 us -> none  [the longest x1 52.1 us: per_device(): flat_new[target]]
    scatter-add x1 -> x0, other arithmetic: 22.5 us -> none  [per_device(): jnp.zeros((3, 3 * PAN_DEV), jnp.float32).at[:, slot_index]]
    unnamed x53 -> x0, other arithmetic: 21.6 us -> none
    slice x9 -> x1, local copies, waits for them, and re-layouts: 20.7 us -> 0.58 us  [per_device(): return (populations_next, (own + from_pair + from_other)[:3])]
    scatter x1 -> x0, local copies, waits for them, and re-layouts: 18.7 us -> none  [per_device(): flat_new.at[target].set(jnp.where(active, bounce, flat_new[target]))]
    pallas_call x0 -> x4, Pallas kernels: none -> 15.8 us  [the longest x1 5.14 us: per_device(): pl.pallas_call(table_kernel, out_shape=(VMEM((PLANES, 3 * COLS), F32), VM...]
    concatenate x2 -> x0, other arithmetic: 13.8 us -> none  [with_halo(): jnp.concatenate([lax.ppermute(tail, axis, [(i, (i + 1) % count) for i in...]
    mul x10 -> x0, other arithmetic: 13.5 us -> none  [the longest x7 9.32 us: relax(): density * sectioned[a, b, c]]
  transfers between devices with their start and end apart: 6 -> 6, of which waited for: 0 -> 2; matrix products, arithmetic and copies ran while one was open for 37% -> 0% of each run, Pallas kernels for 0% -> 11%
where the time goes in v1:
time: 46.9 us; the launch traced here: 46.8 us
  starting transfers between devices  22.1 us (47%)
  Pallas kernels  15.8 us (34%)
  waiting for transfers between devices  5.77 us (12%)
  local copies, waits for them, and re-layouts  2.35 us (5%)
  between operations  0.73 us (2%)
    ppermute x1, starting transfers between devices, per_device(): x_other = lax.ppermute(x_other, 'gx', other_swap(nx))  9.87 us
    ppermute x1, starting transfers between devices, per_device(): from_other = lax.ppermute(to_other, 'gx', other_swap(nx))  8.04 us
    pallas_call x1, Pallas kernels, per_device(): pl.pallas_call(table_kernel, out_shape=(VMEM((PLANES, 3 * COLS), F32), VM...  5.14 us
    pallas_call x1, Pallas kernels, per_device(): pl.pallas_call(stream_kernel, out_shape=(jax.ShapeDtypeStruct(populations...  4.21 us
    pallas_call x1, Pallas kernels, per_device(): pl.pallas_call(collide_kernel, out_shape=(VMEM((27 * PLANES, COLS), F32),...  3.82 us
    ppermute x1, waiting for transfers between devices, per_device(): from_other = lax.ppermute(to_other, 'gx', other_swap(nx))  3.79 us
    ppermute x1, starting transfers between devices, per_device(): y_other = lax.ppermute(y_other, 'gy', other_swap(ny))  2.99 us
    pallas_call x1, Pallas kernels, per_device(): pl.pallas_call(side_kernel, out_shape=(VMEM((18 * PLANES, COLS), F32), ed...  2.6 us
  transfers between devices with their start and end apart: 6, of which 2 were waited for; matrix products, arithmetic and copies ran while one was open for 0% of the time, Pallas kernels for 11%

profile of v1, /device:TPU:0, one launch (start us, length us, event | category | flops | bytes accessed | tf_op | source)
XLA Modules:
  0.0 46.8 jit_solution(12054121178193920373)
XLA Ops:
  0.6 0.0 copy-start
  0.6 1.7 %copy-done = f32[27,24,8,128]{3,2,1,0:T(8,128)S(1)} copy-done((f32[27,24,8,128]{3,2,1,0:T(8,128)S(1)}, f32[27,24,8,128]{3,2,1,0:T(8,128)}, u32[]{:S(2)}) %copy-start) | copy-done | bytes 2654232
  2.4 0.0 copy-start.2
  2.4 0.0 copy-start.3
  2.4 0.0 copy-start.4
  2.4 0.0 copy-start.5
  2.4 3.8 %collide.1 = (f32[5184,128]{1,0:T(8,128)S(1)}, f32[2,8,128]{2,1,0:T(8,128)S(1)}, f32[2,8,128]{2,1,0:T(8,128)S(1)}) custom-call(f32[27,24,8,128]{3,2,1,0:T(8,128)S(1)} %copy-done), custom_call_target="tpu_custom_call" | custom-call | tf_op jit(solution)/shard_map/collide/pallas_call | solution.py:354
  6.2 0.1 collective-permute-start
  6.3 3.0 %collective-permute-start.1 = (f32[2,8,128]{2,1,0:T(8,128)S(1)}, f32[2,8,128]{2,1,0:T(8,128)S(1)}, u32[]{:S(2)}, u32[]{:S(2)}) collective-permute-start(f32[2,8,128]{2,1,0:T(8,128)S(1)} %get-tuple-element.19), channel_id=1, source_target_pairs={{0,7},{1,2},{2,1},{3,4},{4,3},{5,6},{6,5},{7,0},{8,15},{9,10},{10,... | collective-permute-start | bytes 24584 | tf_op jit(solution)/shard_map/ppermute | solution.py:362
  9.3 0.0 collective-permute-done.near_ref
  9.3 2.0 %collective-permute-done.1.far_ref = f32[2,8,128]{2,1,0:T(8,128)S(1)} collective-permute-done((f32[2,8,128]{2,1,0:T(8,128)S(1)}, f32[2,8,128]{2,1,0:T(8,128)S(1)}, u32[]{:S(2)}, u32[]{:S(2)}) %collective-permute-start.1) | collective-permute-done | bytes 8224 | tf_op jit(solution)/shard_map/ppermute | solution.py:362
  11.3 2.6 %sides.1 = (f32[3456,128]{1,0:T(8,128)S(1)}, f32[9,24,128]{2,1,0:T(8,128)S(1)}, f32[9,24,128]{2,1,0:T(8,128)S(1)}) custom-call(f32[5184,128]{1,0:T(8,128)S(1)} %get-tuple-element.17.col_ref, f32[2,8,128]{2,1,0:T(8,128)S(1)} %collective-permute-done.near_ref, f32[2,8,128]{2,1,0:T(8,128)S(1)} %collective-permute-done.1.far_ref), custom_call_target="tpu_custom_call" | custom-call | tf_op jit(solution)/shard_map/sides/pallas_call | solution.py:379
  13.9 1.1 %collective-permute-start.2 = (f32[9,24,128]{2,1,0:T(8,128)S(1)}, f32[9,24,128]{2,1,0:T(8,128)S(1)}, u32[]{:S(2)}, u32[]{:S(2)}) collective-permute-start(f32[9,24,128]{2,1,0:T(8,128)S(1)} %get-tuple-element.21), channel_id=1, source_target_pairs={{0,8},{8,0},{16,24},{24,16},{32,40},{40,32},{48,56},{56,48},{64,72... | collective-permute-start | bytes 331784 | tf_op jit(solution)/shard_map/ppermute | solution.py:388
  14.9 9.9 %collective-permute-start.3 = (f32[9,24,128]{2,1,0:T(8,128)S(1)}, f32[9,24,128]{2,1,0:T(8,128)S(1)}, u32[]{:S(2)}, u32[]{:S(2)}) collective-permute-start(f32[9,24,128]{2,1,0:T(8,128)S(1)} %get-tuple-element.22), channel_id=1, source_target_pairs={{0,248},{8,16},{16,8},{24,32},{32,24},{40,48},{48,40},{56,64},{64,... | collective-permute-start | bytes 331784 | tf_op jit(solution)/shard_map/ppermute | solution.py:387
  24.8 0.0 copy-done.2
  24.8 0.0 copy-done.3
  24.8 0.0 copy-done.4
  24.8 0.0 copy-done.5
  24.8 0.0 copy-start.1
  24.8 5.1 %tables.1 = (f32[192,384]{1,0:T(8,128)S(1)}, bf16[192,4096]{1,0:T(8,128)(2,1)S(1)}, bf16[128,4096]{1,0:T(8,128)(2,1)S(1)}, bf16[128,4096]{1,0:T(8,128)(2,1)S(1)}, f32[24,4096]{1,0:T(8,128)S(1)}) custom-call(s32[32,128]{1,0:T(8,128)S(1)} %bitcast.4, s32[32,128]{1,0:T(8,128)S(1)} %bitcast.5, f32[32,128]{1,0:T(8,128)S(1)} %bitcast.6, s32[32,128]{1,0:T(8,128)S(1)} %bitcast.7), custom_call_target="tpu_custom_call" | custom-call | flops 6000000000 | bytes 70000 | tf_op jit(solution)/shard_map/tables/pallas_call | solution.py:365
  30.0 0.0 collective-permute-done.2.pair_ref
  30.0 0.0 collective-permute-done.3.other_ref
  30.0 0.0 copy-done.1
  30.0 4.2 %stream.1 = (f32[27,24,8,128]{3,2,1,0:T(8,128)}, f32[8,128]{1,0:T(8,128)S(1)}, f32[8,128]{1,0:T(8,128)S(1)}, f32[8,128]{1,0:T(8,128)S(1)}) custom-call(f32[5184,128]{1,0:T(8,128)S(1)} %get-tuple-element.17.col_ref, f32[3456,128]{1,0:T(8,128)S(1)} %get-tuple-element.20.side_ref, f32[9,24,128]{2,1,0:T(8,128)S(1)} %collective-permute-done.2.pair_ref, ...), custom_call_target="tpu_custom_call" | custom-call | tf_op jit(solution)/shard_map/stream/pallas_call | solution.py:389
  34.2 0.1 collective-permute-start.4
  34.3 8.0 %collective-permute-start.5 = (f32[8,128]{1,0:T(8,128)S(1)}, f32[8,128]{1,0:T(8,128)S(1)}, u32[]{:S(2)}, u32[]{:S(2)}) collective-permute-start(f32[8,128]{1,0:T(8,128)S(1)} %get-tuple-element.31), channel_id=1, source_target_pairs={{0,248},{8,16},{16,8},{24,32},{32,24},{40,48},{48,40},{56,64},{64,... | collective-permute-start | bytes 12296 | tf_op jit(solution)/shard_map/ppermute | solution.py:403
  42.4 0.0 collective-permute-done.4
  42.4 3.8 %collective-permute-done.5 = f32[8,128]{1,0:T(8,128)S(1)} collective-permute-done((f32[8,128]{1,0:T(8,128)S(1)}, f32[8,128]{1,0:T(8,128)S(1)}, u32[]{:S(2)}, u32[]{:S(2)}) %collective-permute-start.5) | collective-permute-done | bytes 4128 | tf_op jit(solution)/shard_map/ppermute | solution.py:403
  46.2 0.6 %slice.3 = f32[3,128]{1,0:T(4,128)} slice(f32[8,128]{1,0:T(8,128)S(1)} %add_add_fusion), slice={[0:3], [0:128]} | slice | bytes 3072 | tf_op jit(solution)/shard_map/slice | solution.py:405
  (1 shorter events, 0.0 us)
Async XLA Ops:
  0.6 1.8 %copy-start = (f32[27,24,8,128]{3,2,1,0:T(8,128)S(1)}, f32[27,24,8,128]{3,2,1,0:T(8,128)}, u32[]{:S(2)}) copy-start(f32[27,24,8,128]{3,2,1,0:T(8,128)} %pop_ref.1) | copy-start | bytes 7962628
  2.4 22.4 %copy-start.2 = (s32[4096]{0:T(1024)S(1)}, s32[4096]{0:T(1024)}, u32[]{:S(2)}) copy-start(s32[4096]{0:T(1024)} %param.9) | copy-start | bytes 49156
  2.4 22.4 %copy-start.3 = (s32[4096]{0:T(1024)S(1)}, s32[4096]{0:T(1024)}, u32[]{:S(2)}) copy-start(s32[4096]{0:T(1024)} %param.10) | copy-start | bytes 49156
  2.4 22.4 %copy-start.4 = (f32[4096]{0:T(1024)S(1)}, f32[4096]{0:T(1024)}, u32[]{:S(2)}) copy-start(f32[4096]{0:T(1024)} %param.11) | copy-start | bytes 49156
  2.4 22.4 %copy-start.5 = (s32[4096]{0:T(1024)S(1)}, s32[4096]{0:T(1024)}, u32[]{:S(2)}) copy-start(s32[4096]{0:T(1024)} %param.12) | copy-start | bytes 49156
  6.2 3.1 %collective-permute-start = (f32[2,8,128]{2,1,0:T(8,128)S(1)}, f32[2,8,128]{2,1,0:T(8,128)S(1)}, u32[]{:S(2)}, u32[]{:S(2)}) collective-permute-start(f32[2,8,128]{2,1,0:T(8,128)S(1)} %get-tuple-element.18), channel_id=1, source_target_pairs={{0,1},{1,0},{2,3},{3,2},{4,5},{5,4},{6,7},{7,6},{8,9},{9,8},{10,11... | collective-permute-start | bytes 24584 | tf_op jit(solution)/shard_map/ppermute | solution.py:363
  6.3 5.0 %collective-permute-start.1 = (f32[2,8,128]{2,1,0:T(8,128)S(1)}, f32[2,8,128]{2,1,0:T(8,128)S(1)}, u32[]{:S(2)}, u32[]{:S(2)}) collective-permute-start(f32[2,8,128]{2,1,0:T(8,128)S(1)} %get-tuple-element.19), channel_id=1, source_target_pairs={{0,7},{1,2},{2,1},{3,4},{4,3},{5,6},{6,5},{7,0},{8,15},{9,10},{10,... | collective-permute-start | bytes 24584 | tf_op jit(solution)/shard_map/ppermute | solution.py:362
  13.9 16.1 %collective-permute-start.2 = (f32[9,24,128]{2,1,0:T(8,128)S(1)}, f32[9,24,128]{2,1,0:T(8,128)S(1)}, u32[]{:S(2)}, u32[]{:S(2)}) collective-permute-start(f32[9,24,128]{2,1,0:T(8,128)S(1)} %get-tuple-element.21), channel_id=1, source_target_pairs={{0,8},{8,0},{16,24},{24,16},{32,40},{40,32},{48,56},{56,48},{64,72... | collective-permute-start | bytes 331784 | tf_op jit(solution)/shard_map/ppermute | solution.py:388
  14.9 15.1 %collective-permute-start.3 = (f32[9,24,128]{2,1,0:T(8,128)S(1)}, f32[9,24,128]{2,1,0:T(8,128)S(1)}, u32[]{:S(2)}, u32[]{:S(2)}) collective-permute-start(f32[9,24,128]{2,1,0:T(8,128)S(1)} %get-tuple-element.22), channel_id=1, source_target_pairs={{0,248},{8,16},{16,8},{24,32},{32,24},{40,48},{48,40},{56,64},{64,... | collective-permute-start | bytes 331784 | tf_op jit(solution)/shard_map/ppermute | solution.py:387
  24.8 5.2 %copy-start.1 = (s32[24,8,128]{2,1,0:T(8,128)S(1)}, s32[24,8,128]{2,1,0:T(8,128)}, u32[]{:S(2)}) copy-start(s32[24,8,128]{2,1,0:T(8,128)} %mask_ref.1) | copy-start | bytes 294916
  34.2 8.1 %collective-permute-start.4 = (f32[8,128]{1,0:T(8,128)S(1)}, f32[8,128]{1,0:T(8,128)S(1)}, u32[]{:S(2)}, u32[]{:S(2)}) collective-permute-start(f32[8,128]{1,0:T(8,128)S(1)} %get-tuple-element.30), channel_id=1, source_target_pairs={{0,8},{8,0},{16,24},{24,16},{32,40},{40,32},{48,56},{56,48},{64,72... | collective-permute-start | bytes 12296 | tf_op jit(solution)/shard_map/ppermute | solution.py:404
  34.3 11.8 %collective-permute-start.5 = (f32[8,128]{1,0:T(8,128)S(1)}, f32[8,128]{1,0:T(8,128)S(1)}, u32[]{:S(2)}, u32[]{:S(2)}) collective-permute-start(f32[8,128]{1,0:T(8,128)S(1)} %get-tuple-element.31), channel_id=1, source_target_pairs={{0,248},{8,16},{16,8},{24,32},{32,24},{40,48},{48,40},{56,64},{64,... | collective-permute-start | bytes 12296 | tf_op jit(solution)/shard_map/ppermute | solution.py:403

commit v2 on v1

--- a/solution.py
+++ b/solution.py
@@ -13,12 +13,19 @@
 PLANES = DEPTH * ROWS
 LINKS = 4096
 HALF = DEPTH // 2
-CHUNKS = 8
+CHUNKS = 4
+UNROLL_A = 6
+UNROLL_T = 8
+UNROLL_S = 11
+UNROLL_G = 4
+TABLE_WIDTH = 512
+GATHER_WIDTH = 1024
 F32 = jnp.float32
 BF16 = jnp.bfloat16
 VMEM = pltpu.VMEM
 WHOLE = pl.BlockSpec(memory_space=pltpu.VMEM)
 SOMEWHERE = pl.BlockSpec(memory_space=pl.ANY)
+HBM = pl.BlockSpec(memory_space=pltpu.HBM)
 
 
 def params(mib):
@@ -153,62 +160,72 @@
         carry = (zero, zero)
         for i in range(half * CHUNKS // 2, (half + 1) * CHUNKS // 2):
             copies[i].wait()
-            carry = lax.fori_loop(i * step, (i + 1) * step, body, carry)
+            carry = lax.fori_loop(i * step, (i + 1) * step, body, carry, unroll=UNROLL_A)
         low, high = carry
-        near_ref[half] = jnp.where(even, high, low)
-        far_ref[half] = jnp.where(even, low, high)
-
-
-def side_kernel(col_ref, near_ref, far_ref, side_ref, pair_ref, other_ref, edges):
+        near_ref[pl.ds(half * ROWS, ROWS), :] = jnp.where(even, high, low)
+        far_ref[pl.ds(half * ROWS, ROWS), :] = jnp.where(even, low, high)
+    wide = lax.broadcasted_iota(jnp.int32, (DEPTH, COLS), 1)
+    low = jnp.zeros((DEPTH, COLS), F32)
+    high = low
+    for end in range(2):
+        for c in range(3):
+            spot = end * 3 + c
+            start = (end * 18 + c) * PLANES + end * (ROWS - 1)
+            column = col_ref[pl.ds(start, DEPTH, stride=ROWS), :]
+            low = jnp.where(wide == spot, pltpu.roll(column, spot, 1), low)
+            column = col_ref[pl.ds(start + 6 * PLANES, DEPTH, stride=ROWS), :]
+            high = jnp.where(wide == spot, pltpu.roll(column, spot + 1, 1), high)
+    near_ref[2 * ROWS :, :] = jnp.where(even, high, low)
+    far_ref[2 * ROWS :, :] = jnp.where(even, low, high)
+
+
+def edge_kernel(col_ref, near_ref, far_ref, pair_ref, other_ref):
     even = lax.rem(lax.axis_index("gy"), 2) == 0
     even_x = lax.rem(lax.axis_index("gx"), 2) == 0
-    lane = lax.broadcasted_iota(jnp.int32, (ROWS, COLS), 1)
-    for half in range(2):
-        edges[0, half] = jnp.where(even, far_ref[half], near_ref[half])
-        edges[1, half] = jnp.where(even, near_ref[half], far_ref[half])
-
-    def body(z, half):
-        first = (z - half * HALF) * 9
-        low, high = edges[0, half], edges[1, half]
-        for a in range(3):
-            for c in range(3):
-                spot = first + a * 3 + c
-                up = pltpu.roll(col_ref[plane_rows(a * 9 + 6 + c, z), :], 1, 1)
-                up = jnp.where(lane == 0, pltpu.roll(low, COLS - spot, 1), up)
-                side_ref[plane_rows(a * 6 + 3 + c, z), :] = up
-                down = pltpu.roll(col_ref[plane_rows(a * 9 + c, z), :], COLS - 1, 1)
-                down = jnp.where(
-                    lane == COLS - 1, pltpu.roll(high, COLS - 1 - spot, 1), down
-                )
-                side_ref[plane_rows(a * 6 + c, z), :] = down
-        return half
-
-    for half in range(2):
-        lax.fori_loop(half * HALF, (half + 1) * HALF, body, half)
-    for ref, forward in ((pair_ref, even_x), (other_ref, jnp.logical_not(even_x))):
-        a = jnp.where(forward, 2, 0)
-        x = jnp.where(forward, ROWS - 1, 0)
+    lane = lax.broadcasted_iota(jnp.int32, (DEPTH, COLS), 1)
+    low = jnp.where(even, far_ref[2 * ROWS :, :], near_ref[2 * ROWS :, :])
+    high = jnp.where(even, near_ref[2 * ROWS :, :], far_ref[2 * ROWS :, :])
+    for end in range(2):
+        rows = []
         for b in range(3):
             for c in range(3):
-                if b == 1:
-                    source, start = col_ref, (a * 9 + 3 + c) * PLANES + x
-                else:
-                    source, start = side_ref, (a * 6 + (b // 2) * 3 + c) * PLANES + x
-                ref[b * 3 + c] = source[pl.ds(start, DEPTH, stride=ROWS), :]
-
-
-def table_kernel(cell_ref, dir_ref, q_ref, panel_ref, dense_ref, row_ref, lane_ref, pan_ref, push_ref):
+                start = (end * 18 + b * 3 + c) * PLANES + end * (ROWS - 1)
+                row = col_ref[pl.ds(start, DEPTH, stride=ROWS), :]
+                spot = end * 3 + c
+                if b == 2:
+                    halo = pltpu.roll(low, (COLS - spot) % COLS, 1)
+                    row = jnp.where(lane == 0, halo, pltpu.roll(row, 1, 1))
+                elif b == 0:
+                    halo = pltpu.roll(high, COLS - 1 - spot, 1)
+                    row = jnp.where(lane == COLS - 1, halo, pltpu.roll(row, COLS - 1, 1))
+                rows.append(row)
+
+        @pl.when(even_x == (end == 1))
+        def _():
+            for k in range(9):
+                pair_ref[k] = rows[k]
+
+        @pl.when(even_x != (end == 1))
+        def _():
+            for k in range(9):
+                other_ref[k] = rows[k]
+
+
+def table_kernel(
+    cell_ref, dir_ref, q_ref, panel_ref, dense_ref, row_ref, lane_ref, pan_ref, push_ref, gathered
+):
     gx = lax.axis_index("gx")
     count = lax.axis_size("gx")
     per_row = PAN_DEV * lax.axis_size("gy")
-    width = 256
+    width = TABLE_WIDTH
     row_iota = lax.broadcasted_iota(jnp.int32, (PLANES, width), 0)
     lane_iota = lax.broadcasted_iota(jnp.int32, (COLS, width), 0)
     push_iota = lax.broadcasted_iota(jnp.int32, (24, width), 0)
-    dense_ref[...] = jnp.zeros_like(dense_ref)
+    gathered[...] = jnp.zeros_like(gathered)
 
     def load(ref, i):
-        return jnp.concatenate([ref[pl.ds(2 * i, 1), :], ref[pl.ds(2 * i + 1, 1), :]], axis=1)
+        n = width // COLS
+        return jnp.concatenate([ref[pl.ds(n * i + j, 1), :] for j in range(n)], axis=1)
 
     def body(i, carry):
         at = pl.ds(pl.multiple_of(i * width, width), width)
@@ -220,22 +237,27 @@
         weight = jnp.where(near, twice, 1.0 / twice)
         weight_hi = weight.astype(BF16).astype(F32)
         weight_lo = weight - weight_hi
-        code = (direction + 1 + jnp.where(near, 27, 0)).astype(F32)
+        offset = panel // per_row - gx + 1
+        offset = jnp.where(offset < 0, offset + count, offset)
+        offset = jnp.where(offset >= count, offset - count, offset)
+        code = (direction + 1 + jnp.where(near, 27, 0) + 54 * offset).astype(F32)
+        spot = panel % PAN_DEV
         row = jnp.where(active, cell // COLS, -1)
         rows = jnp.where(row_iota == row, 1.0, 0.0).astype(BF16)
         row_ref[:, at] = rows
         here = lane_iota == cell % COLS
         lane_ref[:, at] = jnp.where(here, 1.0, 0.0).astype(BF16)
         values = jnp.concatenate(
-            [jnp.where(here, v, 0.0).astype(BF16) for v in (weight_hi, weight_lo, code)], axis=0
+            [
+                jnp.where(here, v, 0.0).astype(BF16)
+                for v in (weight_hi, weight_lo, code, spot.astype(F32))
+            ],
+            axis=0,
         )
-        dense_ref[...] += lax.dot_general(
+        gathered[...] += lax.dot_general(
             rows, values, (((1,), (1,)), ((), ())), preferred_element_type=F32
         )
-        pan_ref[:, at] = jnp.where(lane_iota == panel % PAN_DEV, 1.0, 0.0).astype(BF16)
-        offset = panel // per_row - gx + 1
-        offset = jnp.where(offset < 0, offset + count, offset)
-        offset = jnp.where(offset >= count, offset - count, offset)
+        pan_ref[:, at] = jnp.where(lane_iota == spot, 1.0, 0.0).astype(BF16)
         part = push_iota % 8
         step = jnp.where(
             part == 0,
@@ -246,28 +268,47 @@
         push_ref[:, at] = jnp.where(chosen, step, 0).astype(F32)
         return carry
 
-    lax.fori_loop(0, LINKS // width, body, 0)
+    lax.fori_loop(0, LINKS // width, body, 0, unroll=UNROLL_T)
+    dense_ref[:PLANES, :] = gathered[:, :COLS] + gathered[:, COLS : 2 * COLS]
+    dense_ref[PLANES : 2 * PLANES, :] = gathered[:, 2 * COLS : 3 * COLS]
+    dense_ref[2 * PLANES :, :] = gathered[:, 3 * COLS :]
+
+
+def split_code(code):
+    offset = jnp.where(code > 108.5, 2.0, jnp.where(code > 54.5, 1.0, 0.0))
+    code = code - 54.0 * offset
+    near = code > 27.5
+    return offset, near, jnp.where(near, code - 28.0, code - 1.0)
+
+
+def by_panel(push, pan):
+    push_hi = push.astype(BF16).astype(F32)
+    push = jnp.concatenate([push_hi, push - push_hi], axis=0).astype(BF16)
+    return lax.dot_general(push, pan, (((1,), (1,)), ((), ())), preferred_element_type=F32)
 
 
 def stream_kernel(
-    col_ref, side_ref, pair_ref, other_ref, dense_ref, row_ref, lane_ref, pan_ref, push_ref, mask_ref,
-    out_ref, own_ref, send_pair_ref, send_other_ref,
-    buf, halo, momentum, sem,
+    col_ref, near_ref, far_ref, pair_ref, dense_ref, row_ref, lane_ref, pan_ref, push_ref, mask_ref,
+    new_ref, force_ref, late_push_ref, late_pan_ref,
+    edges, halo, momentum,
 ):
+    even = lax.rem(lax.axis_index("gy"), 2) == 0
     even_x = lax.rem(lax.axis_index("gx"), 2) == 0
-    halo[0] = jnp.where(even_x, other_ref[...], pair_ref[...])
-    halo[1] = jnp.where(even_x, pair_ref[...], other_ref[...])
+    halo[0] = jnp.where(even_x, 0.0, pair_ref[...])
+    halo[1] = jnp.where(even_x, pair_ref[...], 0.0)
+    for half in range(2):
+        at = pl.ds(half * ROWS, ROWS)
+        edges[0, half] = jnp.where(even, far_ref[at, :], near_ref[at, :])
+        edges[1, half] = jnp.where(even, near_ref[at, :], far_ref[at, :])
     sub = lax.broadcasted_iota(jnp.int32, (ROWS, COLS), 0)
+    lane = lax.broadcasted_iota(jnp.int32, (ROWS, COLS), 1)
 
     def body(z, bottom, top):
-        code = dense_ref[pl.ds(pl.multiple_of(z * ROWS, ROWS), ROWS), 2 * COLS : 3 * COLS]
-        weight = (
-            dense_ref[pl.ds(pl.multiple_of(z * ROWS, ROWS), ROWS), :COLS]
-            + dense_ref[pl.ds(pl.multiple_of(z * ROWS, ROWS), ROWS), COLS : 2 * COLS]
-        )
+        here_rows = pl.ds(pl.multiple_of(z * ROWS, ROWS), ROWS)
+        code = dense_ref[pl.ds(pl.multiple_of(PLANES + z * ROWS, ROWS), ROWS), :]
+        weight = dense_ref[here_rows, :]
         fluid = (1 - mask_ref[z]).astype(F32)
-        near = code > 27.5
-        which = jnp.where(near, code - 28.0, code - 1.0)
+        offset, near, which = split_code(code)
         toward = jnp.zeros((ROWS, COLS), F32)
         second, reverse = toward, toward
         for d in range(27):
@@ -278,17 +319,22 @@
                 moved = back
             else:
                 zs = z - (c - 1)
-                if b == 1:
-                    moved = col_ref[plane_rows(d, zs), :]
-                else:
-                    moved = side_ref[plane_rows(a * 6 + (b // 2) * 3 + c, zs), :]
+                moved = col_ref[plane_rows(d, zs), :]
+                half = jnp.where(zs < HALF, 0, 1)
+                spot = (zs - half * HALF) * 9 + a * 3 + c
+                if b == 2:
+                    side = pltpu.roll(edges[0, half], COLS - spot, 1)
+                    moved = jnp.where(lane == 0, side, pltpu.roll(moved, 1, 1))
+                elif b == 0:
+                    side = pltpu.roll(edges[1, half], COLS - 1 - spot, 1)
+                    moved = jnp.where(lane == COLS - 1, side, pltpu.roll(moved, COLS - 1, 1))
                 if a == 2:
                     edge = halo[0, b * 3 + c, pl.ds(zs, 1), :]
                     moved = jnp.where(sub == 0, edge, pltpu.roll(moved, 1, 0))
                 elif a == 0:
                     edge = halo[1, b * 3 + c, pl.ds(zs, 1), :]
                     moved = jnp.where(sub == ROWS - 1, edge, pltpu.roll(moved, ROWS - 1, 0))
-            buf[d, z] = moved
+            new_ref[plane_rows(d, z), :] = moved
             if d != 13:
                 match = which == float(d)
                 toward = jnp.where(match, here, toward)
@@ -296,25 +342,23 @@
                 reverse = jnp.where(match, back, reverse)
         other = jnp.where(near, second, reverse)
         bounce = other + weight * (toward - other)
-        momentum[pl.ds(pl.multiple_of(z * ROWS, ROWS), ROWS), :] = jnp.where(
-            code > 0.5, toward + bounce, 0.0
-        )
+        momentum[here_rows, :] = jnp.where(code > 0.5, toward + bounce, 0.0)
         for d in range(27):
-            value = buf[d, z]
+            value = new_ref[plane_rows(d, z), :]
             if d != 13:
                 value = jnp.where(which == float(26 - d), bounce, value)
-            buf[d, z] = value * fluid
+            new_ref[plane_rows(d, z), :] = value * fluid
 
     body(0, True, False)
-    lax.fori_loop(1, DEPTH - 1, lambda z, carry: (body(z, False, False), carry)[1], 0)
+    lax.fori_loop(
+        1, DEPTH - 1, lambda z, carry: (body(z, False, False), carry)[1], 0, unroll=UNROLL_S
+    )
     body(DEPTH - 1, False, True)
-    copy = pltpu.make_async_copy(buf, out_ref, sem)
-    copy.start()
 
     turned = momentum[...].T
     turned_hi = turned.astype(BF16)
     turned_lo = (turned - turned_hi.astype(F32)).astype(BF16)
-    width = 512
+    width = GATHER_WIDTH
 
     def gather(i, total):
         at = pl.ds(pl.multiple_of(i * width, width), width)
@@ -323,18 +367,94 @@
             turned_lo, rows, preferred_element_type=F32
         )
         value = jnp.sum(picked * lane_ref[:, at].astype(F32), axis=0, keepdims=True)
-        push = push_ref[:, at] * value
-        push_hi = push.astype(BF16).astype(F32)
-        push = jnp.concatenate([push_hi, push - push_hi], axis=0).astype(BF16)
-        return total + lax.dot_general(
-            push, pan_ref[:, at], (((1,), (1,)), ((), ())), preferred_element_type=F32
+        return total + by_panel(push_ref[:, at] * value, pan_ref[:, at])
+
+    total = lax.fori_loop(
+        0, LINKS // width, gather, jnp.zeros((48, PAN_DEV), F32), unroll=UNROLL_G
+    )
+    force_ref[...] = total[:24] + total[24:]
+
+    last = jnp.where(even_x, 0, ROWS - 1)
+    picked = [dense_ref[pl.ds(i * PLANES + last, DEPTH, stride=ROWS), :] for i in range(3)]
+    offset, near, which = split_code(picked[1])
+    lead = jnp.where(even_x, 18.0, 0.0)
+    across = near & (which >= lead) & (which < lead + 9.0)
+    share = jnp.where(across, 1.0 - picked[0], 0.0)
+    k = jnp.where(across, which - lead, 0.0)
+    step_y = jnp.where(k > 5.5, 1.0, jnp.where(k > 2.5, 0.0, -1.0))
+    step_z = k - 3.0 * step_y - 4.0
+    step_x = jnp.where(even_x, share, -share)
+    step_y, step_z = step_y * share, step_z * share
+    push_iota = lax.broadcasted_iota(jnp.int32, (24, COLS), 0)
+    part, owner = push_iota % 8, (push_iota // 8).astype(F32)
+    pan_iota = lax.broadcasted_iota(jnp.int32, (PAN_DEV, COLS), 0).astype(F32)
+    for z in range(DEPTH):
+        row = slice(z, z + 1)
+        steps = jnp.where(
+            part == 0,
+            step_x[row],
+            jnp.where(part == 1, step_y[row], jnp.where(part == 2, step_z[row], 0.0)),
         )
-
-    total = lax.fori_loop(0, LINKS // width, gather, jnp.zeros((48, PAN_DEV), F32))
-    force = total[:24] + total[24:]
+        at = slice(z * COLS, (z + 1) * COLS)
+        late_push_ref[:, at] = jnp.where(owner == offset[row], steps, 0.0)
+        late_pan_ref[:, at] = jnp.where(pan_iota == picked[2][row], 1.0, 0.0).astype(BF16)
+
+
+def late_row(dense_ref, even_x):
+    last = jnp.where(even_x, 0, ROWS - 1)
+    weight = dense_ref[pl.ds(last, DEPTH, stride=ROWS), :]
+    _, near, which = split_code(dense_ref[pl.ds(PLANES + last, DEPTH, stride=ROWS), :])
+    return near, which, weight
+
+
+def late_kernel(other_ref, dense_ref, force_ref, late_push_ref, late_pan_ref, own_ref, send_pair_ref, send_other_ref):
+    even_x = lax.rem(lax.axis_index("gx"), 2) == 0
+    near, which, weight = late_row(dense_ref, even_x)
+    lead = jnp.where(even_x, 18.0, 0.0)
+    second = jnp.zeros((DEPTH, COLS), F32)
+    for k in range(9):
+        row = other_ref[k]
+        if k % 3 == 2:
+            row = pltpu.roll(row, 1, 0)
+        elif k % 3 == 0:
+            row = pltpu.roll(row, DEPTH - 1, 0)
+        second = jnp.where(which == lead + float(k), row, second)
+    second = jnp.concatenate([second[z : z + 1] for z in range(DEPTH)], axis=1)
+    late = by_panel(late_push_ref[...] * second, late_pan_ref[...])
+    force = force_ref[...] + late[:24] + late[24:]
     own_ref[...] = force[8:16]
     send_pair_ref[...] = jnp.where(even_x, force[16:24], force[0:8])
     send_other_ref[...] = jnp.where(even_x, force[0:8], force[16:24])
+
+
+def finish_kernel(new_in_ref, other_ref, dense_ref, mask_ref, out_ref, new_ref, sem):
+    del new_in_ref
+    even_x = lax.rem(lax.axis_index("gx"), 2) == 0
+    near, which, weight = late_row(dense_ref, even_x)
+    last = jnp.where(even_x, 0, ROWS - 1)
+    lead_index = jnp.where(even_x, 18, 0)
+    lead = lead_index.astype(F32)
+    fluid = (1 - mask_ref[pl.ds(last, DEPTH, stride=ROWS), :]).astype(F32)
+    level = lax.broadcasted_iota(jnp.int32, (DEPTH, COLS), 0)
+    for k in range(9):
+        row = other_ref[k]
+        inside = level >= 0
+        if k % 3 == 2:
+            row = pltpu.roll(row, 1, 0)
+            inside = level > 0
+        elif k % 3 == 0:
+            row = pltpu.roll(row, DEPTH - 1, 0)
+            inside = level < DEPTH - 1
+        row = row * fluid
+        index = lead_index + k
+        at = pl.ds(index * PLANES + last, DEPTH, stride=ROWS)
+        free = inside & (which != 26.0 - lead - float(k))
+        new_ref[at, :] = jnp.where(free, row, new_ref[at, :])
+        at = pl.ds((26 - index) * PLANES + last, DEPTH, stride=ROWS)
+        hit = near & (which == lead + float(k))
+        new_ref[at, :] = new_ref[at, :] + jnp.where(hit, (1.0 - weight) * row, 0.0)
+    copy = pltpu.make_async_copy(new_ref, out_ref, sem)
+    copy.start()
     copy.wait()
 
 
@@ -349,60 +469,84 @@
 def per_device(populations, solid_mask, link_cell, link_dir, link_second, link_q, link_panel):
     nx, ny = lax.axis_size("gx"), lax.axis_size("gy")
     small = jax.ShapeDtypeStruct((ROWS, PAN_DEV), F32)
-    column = jax.ShapeDtypeStruct((2, ROWS, COLS), F32)
+    column = jax.ShapeDtypeStruct((2 * ROWS + DEPTH, COLS), F32)
     edge = jax.ShapeDtypeStruct((9, DEPTH, COLS), F32)
     collided, y_pair, y_other = pl.pallas_call(
         collide_kernel,
         out_shape=(VMEM((27 * PLANES, COLS), F32), column, column),
-        in_specs=[SOMEWHERE],
+        in_specs=[HBM],
         scratch_shapes=[VMEM((27, DEPTH, ROWS, COLS), F32), pltpu.SemaphoreType.DMA((CHUNKS,))],
         compiler_params=params(16),
         name="collide",
-    )(populations)
+    )(pltpu.with_memory_space_constraint(populations, pltpu.HBM))
     y_other = lax.ppermute(y_other, "gy", other_swap(ny))
     y_pair = lax.ppermute(y_pair, "gy", pair_swap(ny))
+    x_pair, x_other = pl.pallas_call(
+        edge_kernel,
+        out_shape=(edge, edge),
+        in_specs=[WHOLE] * 3,
+        compiler_params=params(16),
+        name="edges",
+    )(collided, y_pair, y_other)
+    x_other = lax.ppermute(x_other, "gx", other_swap(nx))
+    x_pair = lax.ppermute(x_pair, "gx", pair_swap(nx))
     tables = [t.reshape(LINKS // COLS, COLS) for t in (link_cell, link_dir, link_q, link_panel)]
-    dense = pl.pallas_call(
+    tables = pl.pallas_call(
         table_kernel,
         out_shape=(
-            VMEM((PLANES, 3 * COLS), F32),
+            VMEM((3 * PLANES, COLS), F32),
             VMEM((PLANES, LINKS), BF16),
             VMEM((COLS, LINKS), BF16),
             VMEM((PAN_DEV, LINKS), BF16),
             VMEM((24, LINKS), F32),
         ),
         in_specs=[WHOLE] * 4,
+        scratch_shapes=[VMEM((PLANES, 4 * COLS), F32)],
         compiler_params=params(16),
         cost_estimate=pl.CostEstimate(flops=6 * 10**9, bytes_accessed=70000, transcendentals=0),
         name="tables",
     )(*tables)
-    side, x_pair, x_other = pl.pallas_call(
-        side_kernel,
-        out_shape=(VMEM((18 * PLANES, COLS), F32), edge, edge),
-        in_specs=[WHOLE] * 3,
-        scratch_shapes=[VMEM((2, 2, ROWS, COLS), F32)],
-        compiler_params=params(16),
-        name="sides",
-    )(collided, y_pair, y_other)
-    x_other = lax.ppermute(x_other, "gx", other_swap(nx))
-    x_pair = lax.ppermute(x_pair, "gx", pair_swap(nx))
-    populations_next, own, to_pair, to_other = pl.pallas_call(
+    dense = tables[0]
+    moved, force, late_push, late_pan = pl.pallas_call(
         stream_kernel,
-        out_shape=(jax.ShapeDtypeStruct(populations.shape, F32), small, small, small),
+        out_shape=(
+            VMEM((27 * PLANES, COLS), F32),
+            VMEM((24, PAN_DEV), F32),
+            VMEM((24, DEPTH * COLS), F32),
+            VMEM((PAN_DEV, DEPTH * COLS), BF16),
+        ),
         in_specs=[WHOLE] * 10,
-        out_specs=(SOMEWHERE, WHOLE, WHOLE, WHOLE),
         scratch_shapes=[
-            VMEM((27, DEPTH, ROWS, COLS), F32),
+            VMEM((2, 2, ROWS, COLS), F32),
             VMEM((2, 9, DEPTH, COLS), F32),
             VMEM((PLANES, COLS), F32),
-            pltpu.SemaphoreType.DMA,
         ],
         compiler_params=params(24),
         name="stream",
-    )(collided, side, x_pair, x_other, *dense, solid_mask)
+    )(collided, y_pair, y_other, x_pair, *tables, solid_mask)
+    own, to_pair, to_other = pl.pallas_call(
+        late_kernel,
+        out_shape=(small, small, small),
+        in_specs=[WHOLE] * 5,
+        compiler_params=params(16),
+        name="late",
+    )(x_other, dense, force, late_push, late_pan)
     from_other = lax.ppermute(to_other, "gx", other_swap(nx))
     from_pair = lax.ppermute(to_pair, "gx", pair_swap(nx))
-    return populations_next, (own + from_pair + from_other)[:3]
+    populations_next, _ = pl.pallas_call(
+        finish_kernel,
+        out_shape=(
+            jax.ShapeDtypeStruct((27 * PLANES, COLS), F32),
+            VMEM((27 * PLANES, COLS), F32),
+        ),
+        in_specs=[WHOLE] * 4,
+        out_specs=(SOMEWHERE, WHOLE),
+        input_output_aliases={0: 1},
+        scratch_shapes=[pltpu.SemaphoreType.DMA],
+        compiler_params=params(16),
+        name="finish",
+    )(moved, x_other, dense, solid_mask.reshape(PLANES, COLS))
+    return populations_next.reshape(populations.shape), (own + from_pair + from_other)[:3]
 
 
 def solution(mesh):

time: 46.9 us -> 38.1 us (0.81)
  Pallas kernels: 15.8 us -> 10.3 us
  local copies, waits for them, and re-layouts: 2.35 us -> 0.61 us
  waiting for transfers between devices: 5.77 us -> 4.31 us
    pallas_call x3 -> x5, Pallas kernels: 11.9 us -> 7.44 us  [the longest x1 2.95 us: per_device(): pl.pallas_call(stream_kernel, out_shape=(VMEM((27 * PLANES, COLS), F32),...]
    unnamed x12 -> x10, local copies, waits for them, and re-layouts: 1.76 us -> 0.02 us
    ppermute x1, waiting for transfers between devices: 3.79 us -> 2.2 us  [per_device(): from_other = lax.ppermute(to_other, 'gx', other_swap(nx))]
    pallas_call x1, Pallas kernels: 3.82 us -> 2.83 us  [per_device(): pl.pallas_call(collide_kernel, out_shape=(VMEM((27 * PLANES, COLS), F32),...]
  transfers between devices with their start and end apart: 6 -> 6, of which waited for: 2 -> 2; matrix products, arithmetic and copies ran while one was open for 0% -> 0% of each run, Pallas kernels for 11% -> 18%
where the time goes in v2:
time: 38.1 us; the launch traced here: 38 us
  starting transfers between devices  22.1 us (58%)
  Pallas kernels  10.3 us (27%)
  waiting for transfers between devices  4.31 us (11%)
  between operations  0.77 us (2%)
  local copies, waits for them, and re-layouts  0.61 us (2%)
    ppermute x1, starting transfers between devices, per_device(): x_other = lax.ppermute(x_other, 'gx', other_swap(nx))  9.89 us
    ppermute x1, starting transfers between devices, per_device(): from_other = lax.ppermute(to_other, 'gx', other_swap(nx))  7.97 us
    ppermute x1, starting transfers between devices, per_device(): y_other = lax.ppermute(y_other, 'gy', other_swap(ny))  2.99 us
    pallas_call x1, Pallas kernels, per_device(): pl.pallas_call(stream_kernel, out_shape=(VMEM((27 * PLANES, COLS), F32),...  2.95 us
    pallas_call x1, Pallas kernels, per_device(): pl.pallas_call(collide_kernel, out_shape=(VMEM((27 * PLANES, COLS), F32),...  2.83 us
    pallas_call x1, Pallas kernels, per_device(): pl.pallas_call(table_kernel, out_shape=(VMEM((3 * PLANES, COLS), F32), VM...  2.26 us
    ppermute x1, waiting for transfers between devices, per_device(): from_other = lax.ppermute(to_other, 'gx', other_swap(nx))  2.2 us
    ppermute x1, waiting for transfers between devices, per_device(): y_other = lax.ppermute(y_other, 'gy', other_swap(ny))  2.1 us
  transfers between devices with their start and end apart: 6, of which 2 were waited for; matrix products, arithmetic and copies ran while one was open for 0% of the time, Pallas kernels for 18%

profile of v2, /device:TPU:0, one launch (start us, length us, event | category | flops | bytes accessed | tf_op | source)
XLA Modules:
  0.0 38.0 jit_solution(8432391446425165959)
XLA Ops:
  0.6 0.0 copy-start.4
  0.6 0.0 copy-start.3
  0.7 0.0 copy-start.2
  0.7 0.0 copy-start.1
  0.7 2.8 %collide.1 = (f32[5184,128]{1,0:T(8,128)S(1)}, f32[40,128]{1,0:T(8,128)S(1)}, f32[40,128]{1,0:T(8,128)S(1)}) custom-call(f32[27,24,8,128]{3,2,1,0:T(8,128)} %pop_ref.1), custom_call_target="tpu_custom_call" | custom-call | tf_op jit(solution)/shard_map/collide/pallas_call | solution.py:474
  3.5 0.1 collective-permute-start
  3.6 3.0 %collective-permute-start.1 = (f32[40,128]{1,0:T(8,128)S(1)}, f32[40,128]{1,0:T(8,128)S(1)}, u32[]{:S(2)}, u32[]{:S(2)}) collective-permute-start(f32[40,128]{1,0:T(8,128)S(1)} %get-tuple-element.22), channel_id=1, source_target_pairs={{0,7},{1,2},{2,1},{3,4},{4,3},{5,6},{6,5},{7,0},{8,15},{9,10},{10,... | collective-permute-start | bytes 61448 | tf_op jit(solution)/shard_map/ppermute | solution.py:482
  6.6 0.0 collective-permute-done.near_ref
  6.6 2.1 %collective-permute-done.1.far_ref = f32[40,128]{1,0:T(8,128)S(1)} collective-permute-done((f32[40,128]{1,0:T(8,128)S(1)}, f32[40,128]{1,0:T(8,128)S(1)}, u32[]{:S(2)}, u32[]{:S(2)}) %collective-permute-start.1) | collective-permute-done | bytes 20512 | tf_op jit(solution)/shard_map/ppermute | solution.py:482
  8.7 0.2 edges.1
  8.9 1.0 %collective-permute-start.2 = (f32[9,24,128]{2,1,0:T(8,128)S(1)}, f32[9,24,128]{2,1,0:T(8,128)S(1)}, u32[]{:S(2)}, u32[]{:S(2)}) collective-permute-start(f32[9,24,128]{2,1,0:T(8,128)S(1)} %get-tuple-element.23), channel_id=1, source_target_pairs={{0,8},{8,0},{16,24},{24,16},{32,40},{40,32},{48,56},{56,48},{64,72... | collective-permute-start | bytes 331784 | tf_op jit(solution)/shard_map/ppermute | solution.py:492
  10.0 9.9 %collective-permute-start.3 = (f32[9,24,128]{2,1,0:T(8,128)S(1)}, f32[9,24,128]{2,1,0:T(8,128)S(1)}, u32[]{:S(2)}, u32[]{:S(2)}) collective-permute-start(f32[9,24,128]{2,1,0:T(8,128)S(1)} %get-tuple-element.30), channel_id=1, source_target_pairs={{0,248},{8,16},{16,8},{24,32},{32,24},{40,48},{48,40},{56,64},{64,... | collective-permute-start | bytes 331784 | tf_op jit(solution)/shard_map/ppermute | solution.py:491
  19.9 0.0 copy-done.4
  19.9 0.0 copy-done.3
  19.9 0.0 copy-done.2
  19.9 0.0 copy-done.1
  19.9 0.0 copy-start
  19.9 2.3 %tables.1 = (f32[576,128]{1,0:T(8,128)S(1)}, bf16[192,4096]{1,0:T(8,128)(2,1)S(1)}, bf16[128,4096]{1,0:T(8,128)(2,1)S(1)}, bf16[128,4096]{1,0:T(8,128)(2,1)S(1)}, f32[24,4096]{1,0:T(8,128)S(1)}) custom-call(s32[32,128]{1,0:T(8,128)S(1)} %bitcast.7, s32[32,128]{1,0:T(8,128)S(1)} %bitcast.8, f32[32,128]{1,0:T(8,128)S(1)} %bitcast.9, s32[32,128]{1,0:T(8,128)S(1)} %bitcast.10), custom_call_target="tpu_custom_call" | custom-call | flops 6000000000 | bytes 70000 | tf_op jit(solution)/shard_map/tables/pallas_call | solution.py:494
  22.1 0.0 collective-permute-done.2.pair_ref
  22.1 0.0 copy-done
  22.2 2.9 %stream.1 = (f32[5184,128]{1,0:T(8,128)S(1)}, f32[24,128]{1,0:T(8,128)S(1)}, f32[24,3072]{1,0:T(8,128)S(1)}, bf16[128,3072]{1,0:T(8,128)(2,1)S(1)}) custom-call(f32[5184,128]{1,0:T(8,128)S(1)} %get-tuple-element.20.col_ref, f32[40,128]{1,0:T(8,128)S(1)} %collective-permute-done.near_ref, f32[40,128]{1,0:T(8,128)S(1)} %collective-permute-done.1.far_ref, ...), custom_call_target="tpu_custom_call" | custom-call | tf_op jit(solution)/shard_map/stream/pallas_call | solution.py:510
  25.1 0.0 collective-permute-done.3.other_ref
  25.1 0.4 %late.1 = (f32[8,128]{1,0:T(8,128)S(1)}, f32[8,128]{1,0:T(8,128)S(1)}, f32[8,128]{1,0:T(8,128)S(1)}) custom-call(f32[9,24,128]{2,1,0:T(8,128)S(1)} %collective-permute-done.3.other_ref, f32[576,128]{1,0:T(8,128)S(1)} %get-tuple-element.24.dense_ref, f32[24,128]{1,0:T(8,128)S(1)} %get-tuple-element.32.force_ref, ...), custom_call_target="tpu_custom_call" | custom-call | tf_op jit(solution)/shard_map/late/pallas_call | solution.py:527
  25.5 0.1 collective-permute-start.4
  25.6 8.0 %collective-permute-start.5 = (f32[8,128]{1,0:T(8,128)S(1)}, f32[8,128]{1,0:T(8,128)S(1)}, u32[]{:S(2)}, u32[]{:S(2)}) collective-permute-start(f32[8,128]{1,0:T(8,128)S(1)} %get-tuple-element.37), channel_id=1, source_target_pairs={{0,248},{8,16},{16,8},{24,32},{32,24},{40,48},{48,40},{56,64},{64,... | collective-permute-start | bytes 12296 | tf_op jit(solution)/shard_map/ppermute | solution.py:534
  33.6 1.6 %finish.1 = (f32[5184,128]{1,0:T(8,128)}, f32[5184,128]{1,0:T(8,128)S(1)}) custom-call(f32[5184,128]{1,0:T(8,128)S(1)} %get-tuple-element.29.new_in_ref, f32[9,24,128]{2,1,0:T(8,128)S(1)} %collective-permute-done.3.other_ref, f32[576,128]{1,0:T(8,128)S(1)} %get-tuple-element.24.dense_ref, s32[192,128]{1,0:T(8,128)S(1)} %bitcast.6), custom_call_target="tpu_custom_call", output_to_operand_aliasing={{1}: (0, {})} | custom-call | tf_op jit(solution)/shard_map/finish/pallas_call | solution.py:536
  35.2 0.0 collective-permute-done.4
  35.2 2.2 %collective-permute-done.5 = f32[8,128]{1,0:T(8,128)S(1)} collective-permute-done((f32[8,128]{1,0:T(8,128)S(1)}, f32[8,128]{1,0:T(8,128)S(1)}, u32[]{:S(2)}, u32[]{:S(2)}) %collective-permute-start.5) | collective-permute-done | bytes 4128 | tf_op jit(solution)/shard_map/ppermute | solution.py:534
  37.4 0.6 %slice.3 = f32[3,128]{1,0:T(4,128)} slice(f32[8,128]{1,0:T(8,128)S(1)} %add_add_fusion), slice={[0:3], [0:128]} | slice | bytes 3072 | tf_op jit(solution)/shard_map/slice | solution.py:549
  (1 shorter events, 0.0 us)
Async XLA Ops:
  0.6 19.2 %copy-start.4 = (s32[4096]{0:T(1024)S(1)}, s32[4096]{0:T(1024)}, u32[]{:S(2)}) copy-start(s32[4096]{0:T(1024)} %param.12) | copy-start | bytes 49156
  0.6 19.2 %copy-start.3 = (f32[4096]{0:T(1024)S(1)}, f32[4096]{0:T(1024)}, u32[]{:S(2)}) copy-start(f32[4096]{0:T(1024)} %param.11) | copy-start | bytes 49156
  0.7 19.2 %copy-start.2 = (s32[4096]{0:T(1024)S(1)}, s32[4096]{0:T(1024)}, u32[]{:S(2)}) copy-start(s32[4096]{0:T(1024)} %param.10) | copy-start | bytes 49156
  0.7 19.2 %copy-start.1 = (s32[4096]{0:T(1024)S(1)}, s32[4096]{0:T(1024)}, u32[]{:S(2)}) copy-start(s32[4096]{0:T(1024)} %param.9) | copy-start | bytes 49156
  3.5 3.1 %collective-permute-start = (f32[40,128]{1,0:T(8,128)S(1)}, f32[40,128]{1,0:T(8,128)S(1)}, u32[]{:S(2)}, u32[]{:S(2)}) collective-permute-start(f32[40,128]{1,0:T(8,128)S(1)} %get-tuple-element.21), channel_id=1, source_target_pairs={{0,1},{1,0},{2,3},{3,2},{4,5},{5,4},{6,7},{7,6},{8,9},{9,8},{10,11... | collective-permute-start | bytes 61448 | tf_op jit(solution)/shard_map/ppermute | solution.py:483
  3.6 5.1 %collective-permute-start.1 = (f32[40,128]{1,0:T(8,128)S(1)}, f32[40,128]{1,0:T(8,128)S(1)}, u32[]{:S(2)}, u32[]{:S(2)}) collective-permute-start(f32[40,128]{1,0:T(8,128)S(1)} %get-tuple-element.22), channel_id=1, source_target_pairs={{0,7},{1,2},{2,1},{3,4},{4,3},{5,6},{6,5},{7,0},{8,15},{9,10},{10,... | collective-permute-start | bytes 61448 | tf_op jit(solution)/shard_map/ppermute | solution.py:482
  8.9 13.2 %collective-permute-start.2 = (f32[9,24,128]{2,1,0:T(8,128)S(1)}, f32[9,24,128]{2,1,0:T(8,128)S(1)}, u32[]{:S(2)}, u32[]{:S(2)}) collective-permute-start(f32[9,24,128]{2,1,0:T(8,128)S(1)} %get-tuple-element.23), channel_id=1, source_target_pairs={{0,8},{8,0},{16,24},{24,16},{32,40},{40,32},{48,56},{56,48},{64,72... | collective-permute-start | bytes 331784 | tf_op jit(solution)/shard_map/ppermute | solution.py:492
  10.0 15.1 %collective-permute-start.3 = (f32[9,24,128]{2,1,0:T(8,128)S(1)}, f32[9,24,128]{2,1,0:T(8,128)S(1)}, u32[]{:S(2)}, u32[]{:S(2)}) collective-permute-start(f32[9,24,128]{2,1,0:T(8,128)S(1)} %get-tuple-element.30), channel_id=1, source_target_pairs={{0,248},{8,16},{16,8},{24,32},{32,24},{40,48},{48,40},{56,64},{64,... | collective-permute-start | bytes 331784 | tf_op jit(solution)/shard_map/ppermute | solution.py:491
  19.9 2.3 %copy-start = (s32[24,8,128]{2,1,0:T(8,128)S(1)}, s32[24,8,128]{2,1,0:T(8,128)}, u32[]{:S(2)}) copy-start(s32[24,8,128]{2,1,0:T(8,128)} %mask_ref.1) | copy-start | bytes 294916
  25.5 9.7 %collective-permute-start.4 = (f32[8,128]{1,0:T(8,128)S(1)}, f32[8,128]{1,0:T(8,128)S(1)}, u32[]{:S(2)}, u32[]{:S(2)}) collective-permute-start(f32[8,128]{1,0:T(8,128)S(1)} %get-tuple-element.36), channel_id=1, source_target_pairs={{0,8},{8,0},{16,24},{24,16},{32,40},{40,32},{48,56},{56,48},{64,72... | collective-permute-start | bytes 12296 | tf_op jit(solution)/shard_map/ppermute | solution.py:535
  25.6 11.8 %collective-permute-start.5 = (f32[8,128]{1,0:T(8,128)S(1)}, f32[8,128]{1,0:T(8,128)S(1)}, u32[]{:S(2)}, u32[]{:S(2)}) collective-permute-start(f32[8,128]{1,0:T(8,128)S(1)} %get-tuple-element.37), channel_id=1, source_target_pairs={{0,248},{8,16},{16,8},{24,32},{32,24},{40,48},{48,40},{56,64},{64,... | collective-permute-start | bytes 12296 | tf_op jit(solution)/shard_map/ppermute | solution.py:534

commit v3 on v2

--- a/solution.py
+++ b/solution.py
@@ -14,7 +14,7 @@
 LINKS = 4096
 HALF = DEPTH // 2
 CHUNKS = 4
-UNROLL_A = 6
+UNROLL_A = 3
 UNROLL_T = 8
 UNROLL_S = 11
 UNROLL_G = 4
@@ -128,63 +128,82 @@
     return result
 
 
-def collide_kernel(pop_ref, col_ref, near_ref, far_ref, buf, sem):
+def rim_kernel(pop_ref, buf_ref, near_ref, far_ref, stacked, turned, sem):
     even = lax.rem(lax.axis_index("gy"), 2) == 0
     step = DEPTH // CHUNKS
     copies = [
         pltpu.make_async_copy(
-            pop_ref.at[:, pl.ds(i * step, step)], buf.at[:, pl.ds(i * step, step)], sem.at[i]
+            pop_ref.at[:, pl.ds(i * step, step)], buf_ref.at[:, pl.ds(i * step, step)], sem.at[i]
         )
         for i in range(CHUNKS)
     ]
     for copy in copies:
         copy.start()
+    stacked[...] = jnp.zeros_like(stacked)
     lane = lax.broadcasted_iota(jnp.int32, (ROWS, COLS), 1)
-
+    packed = [None] * 27
+    for z in range(DEPTH):
+        if z % step == 0:
+            copies[z // step].wait()
+        here = lane // 2 == z
+        for d in range(27):
+            plane = pltpu.roll(buf_ref[d, z], 2 * z + 1, 1)
+            packed[d] = plane if z == 0 else jnp.where(here, plane, packed[d])
+    f = collide(packed)
+    odd = lane % 2 == 1
+    group = lane // 48
+    for side in range(2):
+        rim = []
+        for v in range(3):
+            value = jnp.zeros((ROWS, COLS), F32)
+            for k in range(4 * v, min(4 * v + 4, 9)):
+                d = k // 3 * 9 + k % 3 + (6 if side == 1 else 0)
+                place = k % 4
+                shift = (place // 2) * 48 + place % 2 - (0 if side == 1 else 1)
+                moved = f[d] if shift == 0 else pltpu.roll(f[d], shift % COLS, 1)
+                mine = (group == place // 2) & (odd == (place % 2 == 1))
+                value = jnp.where(mine, moved, value)
+            rim.append(value)
+        for v in range(3):
+            at = slice(v * ROWS, (v + 1) * ROWS)
+
+            @pl.when(even == (side == 1))
+            def _():
+                near_ref[at, :] = rim[v]
+
+            @pl.when(even != (side == 1))
+            def _():
+                far_ref[at, :] = rim[v]
+
+        for end in range(2):
+            for c in range(3):
+                d = end * 18 + c + (6 if side == 1 else 0)
+                x = end * (ROWS - 1)
+                place = end * 3 + c + side * 8
+                stacked[place : place + 1, :] = f[d][x : x + 1, :]
+    turned[...] = stacked[...].T
+    low = turned[pl.ds(1, DEPTH, stride=2), :]
+    high = turned[pl.ds(0, DEPTH, stride=2), :]
+    near_ref[DEPTH:, :] = jnp.where(even, high, low)
+    far_ref[DEPTH:, :] = jnp.where(even, low, high)
+
+
+def collide_kernel(buf_ref, col_ref):
     def body(z, carry):
-        low, high = carry
-        f = collide([buf[d, z] for d in range(27)])
-        first = lax.rem(z, HALF) * 9
+        f = collide([buf_ref[d, z] for d in range(27)])
         for d in range(27):
             col_ref[plane_rows(d, z), :] = f[d]
-        for a in range(3):
-            for c in range(3):
-                spot = first + a * 3 + c
-                here = lane == spot
-                low = jnp.where(here, pltpu.roll(f[a * 9 + c], spot, 1), low)
-                high = jnp.where(here, pltpu.roll(f[a * 9 + 6 + c], spot + 1, 1), high)
-        return low, high
-
-    zero = jnp.zeros((ROWS, COLS), F32)
-    for half in range(2):
-        carry = (zero, zero)
-        for i in range(half * CHUNKS // 2, (half + 1) * CHUNKS // 2):
-            copies[i].wait()
-            carry = lax.fori_loop(i * step, (i + 1) * step, body, carry, unroll=UNROLL_A)
-        low, high = carry
-        near_ref[pl.ds(half * ROWS, ROWS), :] = jnp.where(even, high, low)
-        far_ref[pl.ds(half * ROWS, ROWS), :] = jnp.where(even, low, high)
-    wide = lax.broadcasted_iota(jnp.int32, (DEPTH, COLS), 1)
-    low = jnp.zeros((DEPTH, COLS), F32)
-    high = low
-    for end in range(2):
-        for c in range(3):
-            spot = end * 3 + c
-            start = (end * 18 + c) * PLANES + end * (ROWS - 1)
-            column = col_ref[pl.ds(start, DEPTH, stride=ROWS), :]
-            low = jnp.where(wide == spot, pltpu.roll(column, spot, 1), low)
-            column = col_ref[pl.ds(start + 6 * PLANES, DEPTH, stride=ROWS), :]
-            high = jnp.where(wide == spot, pltpu.roll(column, spot + 1, 1), high)
-    near_ref[2 * ROWS :, :] = jnp.where(even, high, low)
-    far_ref[2 * ROWS :, :] = jnp.where(even, low, high)
+        return carry
+
+    lax.fori_loop(0, DEPTH, body, 0, unroll=UNROLL_A)
 
 
 def edge_kernel(col_ref, near_ref, far_ref, pair_ref, other_ref):
     even = lax.rem(lax.axis_index("gy"), 2) == 0
     even_x = lax.rem(lax.axis_index("gx"), 2) == 0
     lane = lax.broadcasted_iota(jnp.int32, (DEPTH, COLS), 1)
-    low = jnp.where(even, far_ref[2 * ROWS :, :], near_ref[2 * ROWS :, :])
-    high = jnp.where(even, near_ref[2 * ROWS :, :], far_ref[2 * ROWS :, :])
+    low = jnp.where(even, far_ref[DEPTH:, :], near_ref[DEPTH:, :])
+    high = jnp.where(even, near_ref[DEPTH:, :], far_ref[DEPTH:, :])
     for end in range(2):
         rows = []
         for b in range(3):
@@ -193,7 +212,7 @@
                 row = col_ref[pl.ds(start, DEPTH, stride=ROWS), :]
                 spot = end * 3 + c
                 if b == 2:
-                    halo = pltpu.roll(low, (COLS - spot) % COLS, 1)
+                    halo = pltpu.roll(low, COLS - spot - 8, 1)
                     row = jnp.where(lane == 0, halo, pltpu.roll(row, 1, 1))
                 elif b == 0:
                     halo = pltpu.roll(high, COLS - 1 - spot, 1)
@@ -211,21 +230,35 @@
                 other_ref[k] = rows[k]
 
 
+def split_code(code):
+    offset = jnp.where(code > 108.5, 2.0, jnp.where(code > 54.5, 1.0, 0.0))
+    code = code - 54.0 * offset
+    near = code > 27.5
+    return offset, near, jnp.where(near, code - 28.0, code - 1.0)
+
+
 def table_kernel(
-    cell_ref, dir_ref, q_ref, panel_ref, dense_ref, row_ref, lane_ref, pan_ref, push_ref, gathered
+    cell_ref, dir_ref, q_ref, panel_ref,
+    dense_ref, row_ref, lane_ref, pan_ref, push_ref, late_push_ref, late_pan_ref,
+    gathered,
 ):
     gx = lax.axis_index("gx")
     count = lax.axis_size("gx")
     per_row = PAN_DEV * lax.axis_size("gy")
     width = TABLE_WIDTH
-    row_iota = lax.broadcasted_iota(jnp.int32, (PLANES, width), 0)
-    lane_iota = lax.broadcasted_iota(jnp.int32, (COLS, width), 0)
+    row_iota = lax.broadcasted_iota(jnp.int32, (PLANES, width), 0).astype(F32).astype(BF16)
+    lane_iota = lax.broadcasted_iota(jnp.int32, (COLS, width), 0).astype(F32).astype(BF16)
+    one, zero = jnp.ones((), BF16), jnp.zeros((), BF16)
     push_iota = lax.broadcasted_iota(jnp.int32, (24, width), 0)
     gathered[...] = jnp.zeros_like(gathered)
 
     def load(ref, i):
         n = width // COLS
         return jnp.concatenate([ref[pl.ds(n * i + j, 1), :] for j in range(n)], axis=1)
+
+    def spread(value, count):
+        tile = jnp.broadcast_to(value.astype(F32), (16, width)).astype(BF16)
+        return jnp.concatenate([tile] * (count // 16), axis=0)
 
     def body(i, carry):
         at = pl.ds(pl.multiple_of(i * width, width), width)
@@ -243,21 +276,21 @@
         code = (direction + 1 + jnp.where(near, 27, 0) + 54 * offset).astype(F32)
         spot = panel % PAN_DEV
         row = jnp.where(active, cell // COLS, -1)
-        rows = jnp.where(row_iota == row, 1.0, 0.0).astype(BF16)
+        rows = jnp.where(row_iota == spread(row, PLANES), one, zero)
         row_ref[:, at] = rows
-        here = lane_iota == cell % COLS
-        lane_ref[:, at] = jnp.where(here, 1.0, 0.0).astype(BF16)
+        here = lane_iota == spread(cell % COLS, COLS)
+        lane_ref[:, at] = jnp.where(here, one, zero)
         values = jnp.concatenate(
             [
-                jnp.where(here, v, 0.0).astype(BF16)
-                for v in (weight_hi, weight_lo, code, spot.astype(F32))
+                jnp.where(here, spread(v, COLS), zero)
+                for v in (weight_hi, weight_lo, code, spot)
             ],
             axis=0,
         )
         gathered[...] += lax.dot_general(
             rows, values, (((1,), (1,)), ((), ())), preferred_element_type=F32
         )
-        pan_ref[:, at] = jnp.where(lane_iota == spot, 1.0, 0.0).astype(BF16)
+        pan_ref[:, at] = jnp.where(lane_iota == spread(spot, PAN_DEV), one, zero)
         part = push_iota % 8
         step = jnp.where(
             part == 0,
@@ -273,107 +306,7 @@
     dense_ref[PLANES : 2 * PLANES, :] = gathered[:, 2 * COLS : 3 * COLS]
     dense_ref[2 * PLANES :, :] = gathered[:, 3 * COLS :]
 
-
-def split_code(code):
-    offset = jnp.where(code > 108.5, 2.0, jnp.where(code > 54.5, 1.0, 0.0))
-    code = code - 54.0 * offset
-    near = code > 27.5
-    return offset, near, jnp.where(near, code - 28.0, code - 1.0)
-
-
-def by_panel(push, pan):
-    push_hi = push.astype(BF16).astype(F32)
-    push = jnp.concatenate([push_hi, push - push_hi], axis=0).astype(BF16)
-    return lax.dot_general(push, pan, (((1,), (1,)), ((), ())), preferred_element_type=F32)
-
-
-def stream_kernel(
-    col_ref, near_ref, far_ref, pair_ref, dense_ref, row_ref, lane_ref, pan_ref, push_ref, mask_ref,
-    new_ref, force_ref, late_push_ref, late_pan_ref,
-    edges, halo, momentum,
-):
-    even = lax.rem(lax.axis_index("gy"), 2) == 0
-    even_x = lax.rem(lax.axis_index("gx"), 2) == 0
-    halo[0] = jnp.where(even_x, 0.0, pair_ref[...])
-    halo[1] = jnp.where(even_x, pair_ref[...], 0.0)
-    for half in range(2):
-        at = pl.ds(half * ROWS, ROWS)
-        edges[0, half] = jnp.where(even, far_ref[at, :], near_ref[at, :])
-        edges[1, half] = jnp.where(even, near_ref[at, :], far_ref[at, :])
-    sub = lax.broadcasted_iota(jnp.int32, (ROWS, COLS), 0)
-    lane = lax.broadcasted_iota(jnp.int32, (ROWS, COLS), 1)
-
-    def body(z, bottom, top):
-        here_rows = pl.ds(pl.multiple_of(z * ROWS, ROWS), ROWS)
-        code = dense_ref[pl.ds(pl.multiple_of(PLANES + z * ROWS, ROWS), ROWS), :]
-        weight = dense_ref[here_rows, :]
-        fluid = (1 - mask_ref[z]).astype(F32)
-        offset, near, which = split_code(code)
-        toward = jnp.zeros((ROWS, COLS), F32)
-        second, reverse = toward, toward
-        for d in range(27):
-            a, b, c = d // 9, d // 3 % 3, d % 3
-            here = col_ref[plane_rows(d, z), :]
-            back = col_ref[plane_rows(26 - d, z), :]
-            if (c == 2 and bottom) or (c == 0 and top):
-                moved = back
-            else:
-                zs = z - (c - 1)
-                moved = col_ref[plane_rows(d, zs), :]
-                half = jnp.where(zs < HALF, 0, 1)
-                spot = (zs - half * HALF) * 9 + a * 3 + c
-                if b == 2:
-                    side = pltpu.roll(edges[0, half], COLS - spot, 1)
-                    moved = jnp.where(lane == 0, side, pltpu.roll(moved, 1, 1))
-                elif b == 0:
-                    side = pltpu.roll(edges[1, half], COLS - 1 - spot, 1)
-                    moved = jnp.where(lane == COLS - 1, side, pltpu.roll(moved, COLS - 1, 1))
-                if a == 2:
-                    edge = halo[0, b * 3 + c, pl.ds(zs, 1), :]
-                    moved = jnp.where(sub == 0, edge, pltpu.roll(moved, 1, 0))
-                elif a == 0:
-                    edge = halo[1, b * 3 + c, pl.ds(zs, 1), :]
-                    moved = jnp.where(sub == ROWS - 1, edge, pltpu.roll(moved, ROWS - 1, 0))
-            new_ref[plane_rows(d, z), :] = moved
-            if d != 13:
-                match = which == float(d)
-                toward = jnp.where(match, here, toward)
-                second = jnp.where(match, moved, second)
-                reverse = jnp.where(match, back, reverse)
-        other = jnp.where(near, second, reverse)
-        bounce = other + weight * (toward - other)
-        momentum[here_rows, :] = jnp.where(code > 0.5, toward + bounce, 0.0)
-        for d in range(27):
-            value = new_ref[plane_rows(d, z), :]
-            if d != 13:
-                value = jnp.where(which == float(26 - d), bounce, value)
-            new_ref[plane_rows(d, z), :] = value * fluid
-
-    body(0, True, False)
-    lax.fori_loop(
-        1, DEPTH - 1, lambda z, carry: (body(z, False, False), carry)[1], 0, unroll=UNROLL_S
-    )
-    body(DEPTH - 1, False, True)
-
-    turned = momentum[...].T
-    turned_hi = turned.astype(BF16)
-    turned_lo = (turned - turned_hi.astype(F32)).astype(BF16)
-    width = GATHER_WIDTH
-
-    def gather(i, total):
-        at = pl.ds(pl.multiple_of(i * width, width), width)
-        rows = row_ref[:, at]
-        picked = jnp.dot(turned_hi, rows, preferred_element_type=F32) + jnp.dot(
-            turned_lo, rows, preferred_element_type=F32
-        )
-        value = jnp.sum(picked * lane_ref[:, at].astype(F32), axis=0, keepdims=True)
-        return total + by_panel(push_ref[:, at] * value, pan_ref[:, at])
-
-    total = lax.fori_loop(
-        0, LINKS // width, gather, jnp.zeros((48, PAN_DEV), F32), unroll=UNROLL_G
-    )
-    force_ref[...] = total[:24] + total[24:]
-
+    even_x = lax.rem(gx, 2) == 0
     last = jnp.where(even_x, 0, ROWS - 1)
     picked = [dense_ref[pl.ds(i * PLANES + last, DEPTH, stride=ROWS), :] for i in range(3)]
     offset, near, which = split_code(picked[1])
@@ -398,6 +331,99 @@
         at = slice(z * COLS, (z + 1) * COLS)
         late_push_ref[:, at] = jnp.where(owner == offset[row], steps, 0.0)
         late_pan_ref[:, at] = jnp.where(pan_iota == picked[2][row], 1.0, 0.0).astype(BF16)
+
+
+def by_panel(push, pan):
+    push_hi = push.astype(BF16).astype(F32)
+    push = jnp.concatenate([push_hi, push - push_hi], axis=0).astype(BF16)
+    return lax.dot_general(push, pan, (((1,), (1,)), ((), ())), preferred_element_type=F32)
+
+
+def stream_kernel(
+    col_ref, near_ref, far_ref, pair_ref, dense_ref, row_ref, lane_ref, pan_ref, push_ref, mask_ref,
+    new_ref, force_ref,
+    edges, halo, momentum,
+):
+    even = lax.rem(lax.axis_index("gy"), 2) == 0
+    even_x = lax.rem(lax.axis_index("gx"), 2) == 0
+    halo[0] = jnp.where(even_x, 0.0, pair_ref[...])
+    halo[1] = jnp.where(even_x, pair_ref[...], 0.0)
+    edges[0] = jnp.where(even, far_ref[:DEPTH, :], near_ref[:DEPTH, :])
+    edges[1] = jnp.where(even, near_ref[:DEPTH, :], far_ref[:DEPTH, :])
+    sub = lax.broadcasted_iota(jnp.int32, (ROWS, COLS), 0)
+    lane = lax.broadcasted_iota(jnp.int32, (ROWS, COLS), 1)
+
+    def body(z, bottom, top):
+        here_rows = pl.ds(pl.multiple_of(z * ROWS, ROWS), ROWS)
+        code = dense_ref[pl.ds(pl.multiple_of(PLANES + z * ROWS, ROWS), ROWS), :]
+        weight = dense_ref[here_rows, :]
+        fluid = (1 - mask_ref[z]).astype(F32)
+        offset, near, which = split_code(code)
+        toward = jnp.zeros((ROWS, COLS), F32)
+        second, reverse = toward, toward
+        for d in range(27):
+            a, b, c = d // 9, d // 3 % 3, d % 3
+            here = col_ref[plane_rows(d, z), :]
+            back = col_ref[plane_rows(26 - d, z), :]
+            if (c == 2 and bottom) or (c == 0 and top):
+                moved = back
+            else:
+                zs = z - (c - 1)
+                moved = col_ref[plane_rows(d, zs), :]
+                k = a * 3 + c
+                spot = 2 * zs + k % 4 // 2 * 48 + k % 2
+                at = slice(k // 4 * ROWS, k // 4 * ROWS + ROWS)
+                if b == 2:
+                    side = pltpu.roll(edges[0, at, :], COLS - spot, 1)
+                    moved = jnp.where(lane == 0, side, pltpu.roll(moved, 1, 1))
+                elif b == 0:
+                    side = pltpu.roll(edges[1, at, :], COLS - 1 - spot, 1)
+                    moved = jnp.where(lane == COLS - 1, side, pltpu.roll(moved, COLS - 1, 1))
+                if a == 2:
+                    edge = halo[0, b * 3 + c, pl.ds(zs, 1), :]
+                    moved = jnp.where(sub == 0, edge, pltpu.roll(moved, 1, 0))
+                elif a == 0:
+                    edge = halo[1, b * 3 + c, pl.ds(zs, 1), :]
+                    moved = jnp.where(sub == ROWS - 1, edge, pltpu.roll(moved, ROWS - 1, 0))
+            new_ref[plane_rows(d, z), :] = moved
+            if d != 13:
+                match = which == float(d)
+                toward = jnp.where(match, here, toward)
+                second = jnp.where(match, moved, second)
+                reverse = jnp.where(match, back, reverse)
+        other = jnp.where(near, second, reverse)
+        bounce = other + weight * (toward - other)
+        momentum[here_rows, :] = jnp.where(code > 0.5, toward + bounce, 0.0)
+        for d in range(27):
+            value = new_ref[plane_rows(d, z), :]
+            if d != 13:
+                value = jnp.where(which == float(26 - d), bounce, value)
+            new_ref[plane_rows(d, z), :] = value * fluid
+
+    body(0, True, False)
+    lax.fori_loop(
+        1, DEPTH - 1, lambda z, carry: (body(z, False, False), carry)[1], 0, unroll=UNROLL_S
+    )
+    body(DEPTH - 1, False, True)
+
+    turned = momentum[...].T
+    turned_hi = turned.astype(BF16)
+    turned_lo = (turned - turned_hi.astype(F32)).astype(BF16)
+    width = GATHER_WIDTH
+
+    def gather(i, total):
+        at = pl.ds(pl.multiple_of(i * width, width), width)
+        rows = row_ref[:, at]
+        picked = jnp.dot(turned_hi, rows, preferred_element_type=F32) + jnp.dot(
+            turned_lo, rows, preferred_element_type=F32
+        )
+        value = jnp.sum(picked * lane_ref[:, at].astype(F32), axis=0, keepdims=True)
+        return total + by_panel(push_ref[:, at] * value, pan_ref[:, at])
+
+    total = lax.fori_loop(
+        0, LINKS // width, gather, jnp.zeros((48, PAN_DEV), F32), unroll=UNROLL_G
+    )
+    force_ref[...] = total[:24] + total[24:]
 
 
 def late_row(dense_ref, even_x):
@@ -469,18 +495,30 @@
 def per_device(populations, solid_mask, link_cell, link_dir, link_second, link_q, link_panel):
     nx, ny = lax.axis_size("gx"), lax.axis_size("gy")
     small = jax.ShapeDtypeStruct((ROWS, PAN_DEV), F32)
-    column = jax.ShapeDtypeStruct((2 * ROWS + DEPTH, COLS), F32)
+    column = jax.ShapeDtypeStruct((2 * DEPTH, COLS), F32)
     edge = jax.ShapeDtypeStruct((9, DEPTH, COLS), F32)
-    collided, y_pair, y_other = pl.pallas_call(
-        collide_kernel,
-        out_shape=(VMEM((27 * PLANES, COLS), F32), column, column),
+    arrived, y_pair, y_other = pl.pallas_call(
+        rim_kernel,
+        out_shape=(VMEM(populations.shape, F32), column, column),
         in_specs=[HBM],
-        scratch_shapes=[VMEM((27, DEPTH, ROWS, COLS), F32), pltpu.SemaphoreType.DMA((CHUNKS,))],
+        scratch_shapes=[
+            VMEM((COLS, COLS), F32),
+            VMEM((COLS, COLS), F32),
+            pltpu.SemaphoreType.DMA((CHUNKS,)),
+        ],
         compiler_params=params(16),
-        name="collide",
+        name="rims",
     )(pltpu.with_memory_space_constraint(populations, pltpu.HBM))
     y_other = lax.ppermute(y_other, "gy", other_swap(ny))
     y_pair = lax.ppermute(y_pair, "gy", pair_swap(ny))
+    collided = pl.pallas_call(
+        collide_kernel,
+        out_shape=VMEM((27 * PLANES, COLS), F32),
+        in_specs=[WHOLE],
+        compiler_params=params(16),
+        cost_estimate=pl.CostEstimate(flops=10**9, bytes_accessed=5 * 10**6, transcendentals=0),
+        name="collide",
+    )(arrived)
     x_pair, x_other = pl.pallas_call(
         edge_kernel,
         out_shape=(edge, edge),
@@ -499,6 +537,8 @@
             VMEM((COLS, LINKS), BF16),
             VMEM((PAN_DEV, LINKS), BF16),
             VMEM((24, LINKS), F32),
+            VMEM((24, DEPTH * COLS), F32),
+            VMEM((PAN_DEV, DEPTH * COLS), BF16),
         ),
         in_specs=[WHOLE] * 4,
         scratch_shapes=[VMEM((PLANES, 4 * COLS), F32)],
@@ -506,18 +546,17 @@
         cost_estimate=pl.CostEstimate(flops=6 * 10**9, bytes_accessed=70000, transcendentals=0),
         name="tables",
     )(*tables)
+    *tables, late_push, late_pan = tables
     dense = tables[0]
-    moved, force, late_push, late_pan = pl.pallas_call(
+    moved, force = pl.pallas_call(
         stream_kernel,
         out_shape=(
             VMEM((27 * PLANES, COLS), F32),
             VMEM((24, PAN_DEV), F32),
-            VMEM((24, DEPTH * COLS), F32),
-            VMEM((PAN_DEV, DEPTH * COLS), BF16),
         ),
         in_specs=[WHOLE] * 10,
         scratch_shapes=[
-            VMEM((2, 2, ROWS, COLS), F32),
+            VMEM((2, DEPTH, COLS), F32),
             VMEM((2, 9, DEPTH, COLS), F32),
             VMEM((PLANES, COLS), F32),
         ],

time: 38.1 us -> 37.3 us (0.979)
  waiting for transfers between devices: 4.31 us -> 2.45 us
  Pallas kernels: 10.3 us -> 10.8 us
  starting transfers between devices: 22.1 us -> 22.5 us
    ppermute x1, waiting for transfers between devices: 2.1 us -> 0.66 us  [per_device(): y_other = lax.ppermute(y_other, 'gy', other_swap(ny))]
    pallas_call x1 -> x2, Pallas kernels: 2.83 us -> 3.83 us  [the longest x1 2.38 us: per_device(): pl.pallas_call(rim_kernel, out_shape=(VMEM(populations.shape, F32), colum...]
    ppermute x1, waiting for transfers between devices: 2.2 us -> 1.78 us  [per_device(): from_other = lax.ppermute(to_other, 'gx', other_swap(nx))]
    ppermute x1, starting transfers between devices: 7.97 us -> 8.39 us  [per_device(): from_other = lax.ppermute(to_other, 'gx', other_swap(nx))]
  transfers between devices with their start and end apart: 6 -> 6, of which waited for: 2 -> 2; matrix products, arithmetic and copies ran while one was open for 0% -> 0% of each run, Pallas kernels for 18% -> 21%
where the time goes in v3:
time: 37.3 us; the launch traced here: 37.2 us
  starting transfers between devices  22.5 us (60%)
  Pallas kernels  10.8 us (29%)
  waiting for transfers between devices  2.45 us (7%)
  between operations  0.78 us (2%)
  local copies, waits for them, and re-layouts  0.61 us (2%)
    ppermute x1, starting transfers between devices, per_device(): x_other = lax.ppermute(x_other, 'gx', other_swap(nx))  9.89 us
    ppermute x1, starting transfers between devices, per_device(): from_other = lax.ppermute(to_other, 'gx', other_swap(nx))  8.39 us
    ppermute x1, starting transfers between devices, per_device(): y_other = lax.ppermute(y_other, 'gy', other_swap(ny))  2.99 us
    pallas_call x1, Pallas kernels, per_device(): pl.pallas_call(stream_kernel, out_shape=(VMEM((27 * PLANES, COLS), F32),...  2.61 us
    pallas_call x1, Pallas kernels, per_device(): pl.pallas_call(rim_kernel, out_shape=(VMEM(populations.shape, F32), colum...  2.38 us
    pallas_call x1, Pallas kernels, per_device(): pl.pallas_call(table_kernel, out_shape=(VMEM((3 * PLANES, COLS), F32), VM...  2.16 us
    ppermute x1, waiting for transfers between devices, per_device(): from_other = lax.ppermute(to_other, 'gx', other_swap(nx))  1.78 us
    pallas_call x1, Pallas kernels, per_device(): pl.pallas_call(finish_kernel, out_shape=(jax.ShapeDtypeStruct((27 * PLANE...  1.63 us
  transfers between devices with their start and end apart: 6, of which 2 were waited for; matrix products, arithmetic and copies ran while one was open for 0% of the time, Pallas kernels for 21%

profile of v3, /device:TPU:0, one launch (start us, length us, event | category | flops | bytes accessed | tf_op | source)
XLA Modules:
  0.0 37.2 jit_solution(13417065866302737334)
XLA Ops:
  0.6 2.4 %rims.1 = (f32[27,24,8,128]{3,2,1,0:T(8,128)S(1)}, f32[48,128]{1,0:T(8,128)S(1)}, f32[48,128]{1,0:T(8,128)S(1)}) custom-call(f32[27,24,8,128]{3,2,1,0:T(8,128)} %pop_ref.1), custom_call_target="tpu_custom_call" | custom-call | tf_op jit(solution)/shard_map/rims/pallas_call | solution.py:500
  3.0 0.1 collective-permute-start
  3.1 3.0 %collective-permute-start.1 = (f32[48,128]{1,0:T(8,128)S(1)}, f32[48,128]{1,0:T(8,128)S(1)}, u32[]{:S(2)}, u32[]{:S(2)}) collective-permute-start(f32[48,128]{1,0:T(8,128)S(1)} %get-tuple-element.22), channel_id=1, source_target_pairs={{0,7},{1,2},{2,1},{3,4},{4,3},{5,6},{6,5},{7,0},{8,15},{9,10},{10,... | collective-permute-start | bytes 73736 | tf_op jit(solution)/shard_map/ppermute | solution.py:512
  6.1 1.4 %collide.1.col_ref = f32[5184,128]{1,0:T(8,128)S(1)} custom-call(f32[27,24,8,128]{3,2,1,0:T(8,128)S(1)} %get-tuple-element.20.buf_ref), custom_call_target="tpu_custom_call" | custom-call | flops 1000000000 | bytes 5000000 | tf_op jit(solution)/shard_map/collide/pallas_call | solution.py:514
  7.6 0.0 copy-start.1
  7.6 0.0 copy-start.2
  7.6 0.0 copy-start.3
  7.6 0.0 copy-start.4
  7.6 0.0 collective-permute-done.near_ref
  7.6 0.7 %collective-permute-done.1.far_ref = f32[48,128]{1,0:T(8,128)S(1)} collective-permute-done((f32[48,128]{1,0:T(8,128)S(1)}, f32[48,128]{1,0:T(8,128)S(1)}, u32[]{:S(2)}, u32[]{:S(2)}) %collective-permute-start.1) | collective-permute-done | bytes 24608 | tf_op jit(solution)/shard_map/ppermute | solution.py:512
  8.3 0.2 edges.1
  8.5 1.0 %collective-permute-start.2 = (f32[9,24,128]{2,1,0:T(8,128)S(1)}, f32[9,24,128]{2,1,0:T(8,128)S(1)}, u32[]{:S(2)}, u32[]{:S(2)}) collective-permute-start(f32[9,24,128]{2,1,0:T(8,128)S(1)} %get-tuple-element.23), channel_id=1, source_target_pairs={{0,8},{8,0},{16,24},{24,16},{32,40},{40,32},{48,56},{56,48},{64,72... | collective-permute-start | bytes 331784 | tf_op jit(solution)/shard_map/ppermute | solution.py:530
  9.5 9.9 %collective-permute-start.3 = (f32[9,24,128]{2,1,0:T(8,128)S(1)}, f32[9,24,128]{2,1,0:T(8,128)S(1)}, u32[]{:S(2)}, u32[]{:S(2)}) collective-permute-start(f32[9,24,128]{2,1,0:T(8,128)S(1)} %get-tuple-element.30), channel_id=1, source_target_pairs={{0,248},{8,16},{16,8},{24,32},{32,24},{40,48},{48,40},{56,64},{64,... | collective-permute-start | bytes 331784 | tf_op jit(solution)/shard_map/ppermute | solution.py:529
  19.4 0.0 copy-done.1
  19.4 0.0 copy-done.2
  19.4 0.0 copy-done.3
  19.4 0.0 copy-done.4
  19.4 0.0 copy-start
  19.4 2.2 %tables.1 = (f32[576,128]{1,0:T(8,128)S(1)}, bf16[192,4096]{1,0:T(8,128)(2,1)S(1)}, bf16[128,4096]{1,0:T(8,128)(2,1)S(1)}, bf16[128,4096]{1,0:T(8,128)(2,1)S(1)}...) custom-call(s32[32,128]{1,0:T(8,128)S(1)} %bitcast.7, s32[32,128]{1,0:T(8,128)S(1)} %bitcast.8, ...), custom_call_target="tpu_custom_call" | custom-call | flops 6000000000 | bytes 70000 | tf_op jit(solution)/shard_map/tables/pallas_call | solution.py:532
  21.6 0.0 collective-permute-done.2.pair_ref
  21.6 0.0 copy-done
  21.6 2.6 %stream.1 = (f32[5184,128]{1,0:T(8,128)S(1)}, f32[24,128]{1,0:T(8,128)S(1)}) custom-call(f32[5184,128]{1,0:T(8,128)S(1)} %collide.1.col_ref, f32[48,128]{1,0:T(8,128)S(1)} %collective-permute-done.near_ref, f32[48,128]{1,0:T(8,128)S(1)} %collective-permute-done.1.far_ref, f32[9,24,128]{2,1,0:T(8,128)S(1)} %collective-permute-done.2.pair_ref, ...), custom_call_target="tpu_custom_call" | custom-call | tf_op jit(solution)/shard_map/stream/pallas_call | solution.py:551
  24.2 0.0 collective-permute-done.3.other_ref
  24.3 0.4 %late.1 = (f32[8,128]{1,0:T(8,128)S(1)}, f32[8,128]{1,0:T(8,128)S(1)}, f32[8,128]{1,0:T(8,128)S(1)}) custom-call(f32[9,24,128]{2,1,0:T(8,128)S(1)} %collective-permute-done.3.other_ref, f32[576,128]{1,0:T(8,128)S(1)} %get-tuple-element.24.dense_ref, f32[24,128]{1,0:T(8,128)S(1)} %get-tuple-element.32.force_ref, ...), custom_call_target="tpu_custom_call" | custom-call | tf_op jit(solution)/shard_map/late/pallas_call | solution.py:566
  24.7 0.1 collective-permute-start.4
  24.8 8.4 %collective-permute-start.5 = (f32[8,128]{1,0:T(8,128)S(1)}, f32[8,128]{1,0:T(8,128)S(1)}, u32[]{:S(2)}, u32[]{:S(2)}) collective-permute-start(f32[8,128]{1,0:T(8,128)S(1)} %get-tuple-element.37), channel_id=1, source_target_pairs={{0,248},{8,16},{16,8},{24,32},{32,24},{40,48},{48,40},{56,64},{64,... | collective-permute-start | bytes 12296 | tf_op jit(solution)/shard_map/ppermute | solution.py:573
  33.1 1.6 %finish.1 = (f32[5184,128]{1,0:T(8,128)}, f32[5184,128]{1,0:T(8,128)S(1)}) custom-call(f32[5184,128]{1,0:T(8,128)S(1)} %get-tuple-element.29.new_in_ref, f32[9,24,128]{2,1,0:T(8,128)S(1)} %collective-permute-done.3.other_ref, f32[576,128]{1,0:T(8,128)S(1)} %get-tuple-element.24.dense_ref, s32[192,128]{1,0:T(8,128)S(1)} %bitcast.6), custom_call_target="tpu_custom_call", output_to_operand_aliasing={{1}: (0, {})} | custom-call | tf_op jit(solution)/shard_map/finish/pallas_call | solution.py:575
  34.8 0.0 collective-permute-done.4
  34.8 1.8 %collective-permute-done.5 = f32[8,128]{1,0:T(8,128)S(1)} collective-permute-done((f32[8,128]{1,0:T(8,128)S(1)}, f32[8,128]{1,0:T(8,128)S(1)}, u32[]{:S(2)}, u32[]{:S(2)}) %collective-permute-start.5) | collective-permute-done | bytes 4128 | tf_op jit(solution)/shard_map/ppermute | solution.py:573
  36.6 0.6 %slice.3 = f32[3,128]{1,0:T(4,128)} slice(f32[8,128]{1,0:T(8,128)S(1)} %add_add_fusion), slice={[0:3], [0:128]} | slice | bytes 3072 | tf_op jit(solution)/shard_map/slice | solution.py:588
  (1 shorter events, 0.0 us)
Async XLA Ops:
  3.0 4.6 %collective-permute-start = (f32[48,128]{1,0:T(8,128)S(1)}, f32[48,128]{1,0:T(8,128)S(1)}, u32[]{:S(2)}, u32[]{:S(2)}) collective-permute-start(f32[48,128]{1,0:T(8,128)S(1)} %get-tuple-element.21), channel_id=1, source_target_pairs={{0,1},{1,0},{2,3},{3,2},{4,5},{5,4},{6,7},{7,6},{8,9},{9,8},{10,11... | collective-permute-start | bytes 73736 | tf_op jit(solution)/shard_map/ppermute | solution.py:513
  3.1 5.2 %collective-permute-start.1 = (f32[48,128]{1,0:T(8,128)S(1)}, f32[48,128]{1,0:T(8,128)S(1)}, u32[]{:S(2)}, u32[]{:S(2)}) collective-permute-start(f32[48,128]{1,0:T(8,128)S(1)} %get-tuple-element.22), channel_id=1, source_target_pairs={{0,7},{1,2},{2,1},{3,4},{4,3},{5,6},{6,5},{7,0},{8,15},{9,10},{10,... | collective-permute-start | bytes 73736 | tf_op jit(solution)/shard_map/ppermute | solution.py:512
  7.6 11.8 %copy-start.1 = (s32[4096]{0:T(1024)S(1)}, s32[4096]{0:T(1024)}, u32[]{:S(2)}) copy-start(s32[4096]{0:T(1024)} %param.9) | copy-start | bytes 49156
  7.6 11.8 %copy-start.2 = (s32[4096]{0:T(1024)S(1)}, s32[4096]{0:T(1024)}, u32[]{:S(2)}) copy-start(s32[4096]{0:T(1024)} %param.10) | copy-start | bytes 49156
  7.6 11.8 %copy-start.3 = (f32[4096]{0:T(1024)S(1)}, f32[4096]{0:T(1024)}, u32[]{:S(2)}) copy-start(f32[4096]{0:T(1024)} %param.11) | copy-start | bytes 49156
  7.6 11.8 %copy-start.4 = (s32[4096]{0:T(1024)S(1)}, s32[4096]{0:T(1024)}, u32[]{:S(2)}) copy-start(s32[4096]{0:T(1024)} %param.12) | copy-start | bytes 49156
  8.5 13.1 %collective-permute-start.2 = (f32[9,24,128]{2,1,0:T(8,128)S(1)}, f32[9,24,128]{2,1,0:T(8,128)S(1)}, u32[]{:S(2)}, u32[]{:S(2)}) collective-permute-start(f32[9,24,128]{2,1,0:T(8,128)S(1)} %get-tuple-element.23), channel_id=1, source_target_pairs={{0,8},{8,0},{16,24},{24,16},{32,40},{40,32},{48,56},{56,48},{64,72... | collective-permute-start | bytes 331784 | tf_op jit(solution)/shard_map/ppermute | solution.py:530
  9.5 14.7 %collective-permute-start.3 = (f32[9,24,128]{2,1,0:T(8,128)S(1)}, f32[9,24,128]{2,1,0:T(8,128)S(1)}, u32[]{:S(2)}, u32[]{:S(2)}) collective-permute-start(f32[9,24,128]{2,1,0:T(8,128)S(1)} %get-tuple-element.30), channel_id=1, source_target_pairs={{0,248},{8,16},{16,8},{24,32},{32,24},{40,48},{48,40},{56,64},{64,... | collective-permute-start | bytes 331784 | tf_op jit(solution)/shard_map/ppermute | solution.py:529
  19.4 2.2 %copy-start = (s32[24,8,128]{2,1,0:T(8,128)S(1)}, s32[24,8,128]{2,1,0:T(8,128)}, u32[]{:S(2)}) copy-start(s32[24,8,128]{2,1,0:T(8,128)} %mask_ref.1) | copy-start | bytes 294916
  24.7 10.1 %collective-permute-start.4 = (f32[8,128]{1,0:T(8,128)S(1)}, f32[8,128]{1,0:T(8,128)S(1)}, u32[]{:S(2)}, u32[]{:S(2)}) collective-permute-start(f32[8,128]{1,0:T(8,128)S(1)} %get-tuple-element.36), channel_id=1, source_target_pairs={{0,8},{8,0},{16,24},{24,16},{32,40},{40,32},{48,56},{56,48},{64,72... | collective-permute-start | bytes 12296 | tf_op jit(solution)/shard_map/ppermute | solution.py:574
  24.8 11.8 %collective-permute-start.5 = (f32[8,128]{1,0:T(8,128)S(1)}, f32[8,128]{1,0:T(8,128)S(1)}, u32[]{:S(2)}, u32[]{:S(2)}) collective-permute-start(f32[8,128]{1,0:T(8,128)S(1)} %get-tuple-element.37), channel_id=1, source_target_pairs={{0,248},{8,16},{16,8},{24,32},{32,24},{40,48},{48,40},{56,64},{64,... | collective-permute-start | bytes 12296 | tf_op jit(solution)/shard_map/ppermute | solution.py:573

commit v4 on v3

--- a/solution.py
+++ b/solution.py
@@ -17,9 +17,10 @@
 UNROLL_A = 3
 UNROLL_T = 8
 UNROLL_S = 11
-UNROLL_G = 4
+UNROLL_G = 1
+UNROLL_F = 8
 TABLE_WIDTH = 512
-GATHER_WIDTH = 1024
+GATHER_WIDTH = 4096
 F32 = jnp.float32
 BF16 = jnp.bfloat16
 VMEM = pltpu.VMEM
@@ -340,8 +341,8 @@
 
 
 def stream_kernel(
-    col_ref, near_ref, far_ref, pair_ref, dense_ref, row_ref, lane_ref, pan_ref, push_ref, mask_ref,
-    new_ref, force_ref,
+    col_ref, near_ref, far_ref, pair_ref, dense_ref, row_ref, lane_ref, pan_ref, push_ref,
+    new_ref, bounce_ref, force_ref,
     edges, halo, momentum,
 ):
     even = lax.rem(lax.axis_index("gy"), 2) == 0
@@ -357,8 +358,7 @@
         here_rows = pl.ds(pl.multiple_of(z * ROWS, ROWS), ROWS)
         code = dense_ref[pl.ds(pl.multiple_of(PLANES + z * ROWS, ROWS), ROWS), :]
         weight = dense_ref[here_rows, :]
-        fluid = (1 - mask_ref[z]).astype(F32)
-        offset, near, which = split_code(code)
+        _, near, which = split_code(code)
         toward = jnp.zeros((ROWS, COLS), F32)
         second, reverse = toward, toward
         for d in range(27):
@@ -394,11 +394,7 @@
         other = jnp.where(near, second, reverse)
         bounce = other + weight * (toward - other)
         momentum[here_rows, :] = jnp.where(code > 0.5, toward + bounce, 0.0)
-        for d in range(27):
-            value = new_ref[plane_rows(d, z), :]
-            if d != 13:
-                value = jnp.where(which == float(26 - d), bounce, value)
-            new_ref[plane_rows(d, z), :] = value * fluid
+        bounce_ref[here_rows, :] = bounce
 
     body(0, True, False)
     lax.fori_loop(
@@ -407,16 +403,15 @@
     body(DEPTH - 1, False, True)
 
     turned = momentum[...].T
-    turned_hi = turned.astype(BF16)
-    turned_lo = (turned - turned_hi.astype(F32)).astype(BF16)
+    turned_hi = turned.astype(BF16).astype(F32)
+    turned = jnp.concatenate([turned_hi, turned - turned_hi], axis=0).astype(BF16)
     width = GATHER_WIDTH
 
     def gather(i, total):
         at = pl.ds(pl.multiple_of(i * width, width), width)
         rows = row_ref[:, at]
-        picked = jnp.dot(turned_hi, rows, preferred_element_type=F32) + jnp.dot(
-            turned_lo, rows, preferred_element_type=F32
-        )
+        picked = jnp.dot(turned, rows, preferred_element_type=F32)
+        picked = picked[:COLS] + picked[COLS:]
         value = jnp.sum(picked * lane_ref[:, at].astype(F32), axis=0, keepdims=True)
         return total + by_panel(push_ref[:, at] * value, pan_ref[:, at])
 
@@ -453,32 +448,43 @@
     send_other_ref[...] = jnp.where(even_x, force[0:8], force[16:24])
 
 
-def finish_kernel(new_in_ref, other_ref, dense_ref, mask_ref, out_ref, new_ref, sem):
-    del new_in_ref
+def finish_kernel(
+    new_in_ref, bounce_in_ref, other_ref, dense_ref, mask_ref, out_ref, new_ref, bounce_ref, sem
+):
+    del new_in_ref, bounce_in_ref
     even_x = lax.rem(lax.axis_index("gx"), 2) == 0
     near, which, weight = late_row(dense_ref, even_x)
     last = jnp.where(even_x, 0, ROWS - 1)
     lead_index = jnp.where(even_x, 18, 0)
     lead = lead_index.astype(F32)
-    fluid = (1 - mask_ref[pl.ds(last, DEPTH, stride=ROWS), :]).astype(F32)
     level = lax.broadcasted_iota(jnp.int32, (DEPTH, COLS), 0)
+    second = jnp.zeros((DEPTH, COLS), F32)
     for k in range(9):
         row = other_ref[k]
-        inside = level >= 0
-        if k % 3 == 2:
-            row = pltpu.roll(row, 1, 0)
-            inside = level > 0
-        elif k % 3 == 0:
-            row = pltpu.roll(row, DEPTH - 1, 0)
-            inside = level < DEPTH - 1
-        row = row * fluid
-        index = lead_index + k
-        at = pl.ds(index * PLANES + last, DEPTH, stride=ROWS)
-        free = inside & (which != 26.0 - lead - float(k))
-        new_ref[at, :] = jnp.where(free, row, new_ref[at, :])
-        at = pl.ds((26 - index) * PLANES + last, DEPTH, stride=ROWS)
-        hit = near & (which == lead + float(k))
-        new_ref[at, :] = new_ref[at, :] + jnp.where(hit, (1.0 - weight) * row, 0.0)
+        at = pl.ds((lead_index + k) * PLANES + last, DEPTH, stride=ROWS)
+        if k % 3 == 1:
+            new_ref[at, :] = row
+        else:
+            row = pltpu.roll(row, 1 if k % 3 == 2 else DEPTH - 1, 0)
+            inside = level > 0 if k % 3 == 2 else level < DEPTH - 1
+            new_ref[at, :] = jnp.where(inside, row, new_ref[at, :])
+        second = jnp.where(near & (which == lead + float(k)), row, second)
+    at = pl.ds(last, DEPTH, stride=ROWS)
+    bounce_ref[at, :] = bounce_ref[at, :] + (1.0 - weight) * second
+
+    def body(z, carry):
+        here_rows = pl.ds(pl.multiple_of(z * ROWS, ROWS), ROWS)
+        _, _, target = split_code(dense_ref[pl.ds(pl.multiple_of(PLANES + z * ROWS, ROWS), ROWS), :])
+        bounce = bounce_ref[here_rows, :]
+        fluid = (1 - mask_ref[here_rows, :]).astype(F32)
+        for d in range(27):
+            value = new_ref[plane_rows(d, z), :]
+            if d != 13:
+                value = jnp.where(target == float(26 - d), bounce, value)
+            new_ref[plane_rows(d, z), :] = value * fluid
+        return carry
+
+    lax.fori_loop(0, DEPTH, body, 0, unroll=UNROLL_F)
     copy = pltpu.make_async_copy(new_ref, out_ref, sem)
     copy.start()
     copy.wait()
@@ -548,13 +554,14 @@
     )(*tables)
     *tables, late_push, late_pan = tables
     dense = tables[0]
-    moved, force = pl.pallas_call(
+    moved, bounce, force = pl.pallas_call(
         stream_kernel,
         out_shape=(
             VMEM((27 * PLANES, COLS), F32),
+            VMEM((PLANES, COLS), F32),
             VMEM((24, PAN_DEV), F32),
         ),
-        in_specs=[WHOLE] * 10,
+        in_specs=[WHOLE] * 9,
         scratch_shapes=[
             VMEM((2, DEPTH, COLS), F32),
             VMEM((2, 9, DEPTH, COLS), F32),
@@ -562,7 +569,7 @@
         ],
         compiler_params=params(24),
         name="stream",
-    )(collided, y_pair, y_other, x_pair, *tables, solid_mask)
+    )(collided, y_pair, y_other, x_pair, *tables)
     own, to_pair, to_other = pl.pallas_call(
         late_kernel,
         out_shape=(small, small, small),
@@ -572,19 +579,20 @@
     )(x_other, dense, force, late_push, late_pan)
     from_other = lax.ppermute(to_other, "gx", other_swap(nx))
     from_pair = lax.ppermute(to_pair, "gx", pair_swap(nx))
-    populations_next, _ = pl.pallas_call(
+    populations_next, _, _ = pl.pallas_call(
         finish_kernel,
         out_shape=(
             jax.ShapeDtypeStruct((27 * PLANES, COLS), F32),
             VMEM((27 * PLANES, COLS), F32),
+            VMEM((PLANES, COLS), F32),
         ),
-        in_specs=[WHOLE] * 4,
-        out_specs=(SOMEWHERE, WHOLE),
-        input_output_aliases={0: 1},
+        in_specs=[WHOLE] * 5,
+        out_specs=(SOMEWHERE, WHOLE, WHOLE),
+        input_output_aliases={0: 1, 1: 2},
         scratch_shapes=[pltpu.SemaphoreType.DMA],
         compiler_params=params(16),
         name="finish",
-    )(moved, x_other, dense, solid_mask.reshape(PLANES, COLS))
+    )(moved, bounce, x_other, dense, solid_mask.reshape(PLANES, COLS))
     return populations_next.reshape(populations.shape), (own + from_pair + from_other)[:3]
 
 

time: 37.3 us -> 37.4 us (level)
  waiting for transfers between devices: 2.45 us -> 1.89 us
    ppermute x1, waiting for transfers between devices: 1.78 us -> 1.21 us  [per_device(): from_other = lax.ppermute(to_other, 'gx', other_swap(nx))]
  transfers between devices with their start and end apart: 6 -> 6, of which waited for: 2 -> 2; matrix products, arithmetic and copies ran while one was open for 0% -> 0% of each run, Pallas kernels for 21% -> 22%
where the time goes in v4:
time: 37.4 us; the launch traced here: 36.9 us
  starting transfers between devices  22.7 us (61%)
  Pallas kernels  11 us (29%)
  waiting for transfers between devices  1.89 us (5%)
  between operations  0.77 us (2%)
  local copies, waits for them, and re-layouts  0.61 us (2%)
    ppermute x1, starting transfers between devices, per_device(): x_other = lax.ppermute(x_other, 'gx', other_swap(nx))  9.89 us
    ppermute x1, starting transfers between devices, per_device(): from_other = lax.ppermute(to_other, 'gx', other_swap(nx))  8.62 us
    ppermute x1, starting transfers between devices, per_device(): y_other = lax.ppermute(y_other, 'gy', other_swap(ny))  2.99 us
    pallas_call x1, Pallas kernels, per_device(): pl.pallas_call(stream_kernel, out_shape=(VMEM((27 * PLANES, COLS), F32),...  2.39 us
    pallas_call x1, Pallas kernels, per_device(): pl.pallas_call(rim_kernel, out_shape=(VMEM(populations.shape, F32), colum...  2.38 us
    pallas_call x1, Pallas kernels, per_device(): pl.pallas_call(table_kernel, out_shape=(VMEM((3 * PLANES, COLS), F32), VM...  2.17 us
    pallas_call x1, Pallas kernels, per_device(): pl.pallas_call(finish_kernel, out_shape=(jax.ShapeDtypeStruct((27 * PLANE...  1.97 us
    pallas_call x1, Pallas kernels, per_device(): pl.pallas_call(collide_kernel, out_shape=VMEM((27 * PLANES, COLS), F32),...  1.45 us
  transfers between devices with their start and end apart: 6, of which 2 were waited for; matrix products, arithmetic and copies ran while one was open for 0% of the time, Pallas kernels for 22%

profile of v4, /device:TPU:0, one launch (start us, length us, event | category | flops | bytes accessed | tf_op | source)
XLA Modules:
  0.0 36.9 jit_solution(14303099088511620458)
XLA Ops:
  0.6 2.4 %rims.1 = (f32[27,24,8,128]{3,2,1,0:T(8,128)S(1)}, f32[48,128]{1,0:T(8,128)S(1)}, f32[48,128]{1,0:T(8,128)S(1)}) custom-call(f32[27,24,8,128]{3,2,1,0:T(8,128)} %pop_ref.1), custom_call_target="tpu_custom_call" | custom-call | tf_op jit(solution)/shard_map/rims/pallas_call | solution.py:506
  3.0 0.1 collective-permute-start
  3.1 3.0 %collective-permute-start.1 = (f32[48,128]{1,0:T(8,128)S(1)}, f32[48,128]{1,0:T(8,128)S(1)}, u32[]{:S(2)}, u32[]{:S(2)}) collective-permute-start(f32[48,128]{1,0:T(8,128)S(1)} %get-tuple-element.23), channel_id=1, source_target_pairs={{0,7},{1,2},{2,1},{3,4},{4,3},{5,6},{6,5},{7,0},{8,15},{9,10},{10,... | collective-permute-start | bytes 73736 | tf_op jit(solution)/shard_map/ppermute | solution.py:518
  6.1 1.4 %collide.1.col_ref = f32[5184,128]{1,0:T(8,128)S(1)} custom-call(f32[27,24,8,128]{3,2,1,0:T(8,128)S(1)} %get-tuple-element.21.buf_ref), custom_call_target="tpu_custom_call" | custom-call | flops 1000000000 | bytes 5000000 | tf_op jit(solution)/shard_map/collide/pallas_call | solution.py:520
  7.6 0.0 copy-start.1
  7.6 0.0 copy-start.2
  7.6 0.0 copy-start.3
  7.6 0.0 copy-start.4
  7.6 0.0 collective-permute-done.near_ref
  7.6 0.7 %collective-permute-done.1.far_ref = f32[48,128]{1,0:T(8,128)S(1)} collective-permute-done((f32[48,128]{1,0:T(8,128)S(1)}, f32[48,128]{1,0:T(8,128)S(1)}, u32[]{:S(2)}, u32[]{:S(2)}) %collective-permute-start.1) | collective-permute-done | bytes 24608 | tf_op jit(solution)/shard_map/ppermute | solution.py:518
  8.3 0.2 edges.1
  8.5 1.0 %collective-permute-start.2 = (f32[9,24,128]{2,1,0:T(8,128)S(1)}, f32[9,24,128]{2,1,0:T(8,128)S(1)}, u32[]{:S(2)}, u32[]{:S(2)}) collective-permute-start(f32[9,24,128]{2,1,0:T(8,128)S(1)} %get-tuple-element.24), channel_id=1, source_target_pairs={{0,8},{8,0},{16,24},{24,16},{32,40},{40,32},{48,56},{56,48},{64,72... | collective-permute-start | bytes 331784 | tf_op jit(solution)/shard_map/ppermute | solution.py:536
  9.5 9.9 %collective-permute-start.3 = (f32[9,24,128]{2,1,0:T(8,128)S(1)}, f32[9,24,128]{2,1,0:T(8,128)S(1)}, u32[]{:S(2)}, u32[]{:S(2)}) collective-permute-start(f32[9,24,128]{2,1,0:T(8,128)S(1)} %get-tuple-element.32), channel_id=1, source_target_pairs={{0,248},{8,16},{16,8},{24,32},{32,24},{40,48},{48,40},{56,64},{64,... | collective-permute-start | bytes 331784 | tf_op jit(solution)/shard_map/ppermute | solution.py:535
  19.4 0.0 copy-done.1
  19.4 0.0 copy-done.2
  19.4 0.0 copy-done.3
  19.4 0.0 copy-done.4
  19.4 2.2 %tables.1 = (f32[576,128]{1,0:T(8,128)S(1)}, bf16[192,4096]{1,0:T(8,128)(2,1)S(1)}, bf16[128,4096]{1,0:T(8,128)(2,1)S(1)}, bf16[128,4096]{1,0:T(8,128)(2,1)S(1)}...) custom-call(s32[32,128]{1,0:T(8,128)S(1)} %bitcast.7, s32[32,128]{1,0:T(8,128)S(1)} %bitcast.8, ...), custom_call_target="tpu_custom_call" | custom-call | flops 6000000000 | bytes 70000 | tf_op jit(solution)/shard_map/tables/pallas_call | solution.py:538
  21.6 0.0 collective-permute-done.2.pair_ref
  21.6 0.0 copy-start
  21.6 2.4 %stream.1 = (f32[5184,128]{1,0:T(8,128)S(1)}, f32[192,128]{1,0:T(8,128)S(1)}, f32[24,128]{1,0:T(8,128)S(1)}) custom-call(f32[5184,128]{1,0:T(8,128)S(1)} %collide.1.col_ref, f32[48,128]{1,0:T(8,128)S(1)} %collective-permute-done.near_ref, f32[48,128]{1,0:T(8,128)S(1)} %collective-permute-done.1.far_ref, f32[9,24,128]{2,1,0:T(8,128)S(1)} %collective-permute-done.2.pair_ref, ...), custom_call_target="tpu_custom_call" | custom-call | tf_op jit(solution)/shard_map/stream/pallas_call | solution.py:557
  24.0 0.0 collective-permute-done.3.other_ref
  24.0 0.4 %late.1 = (f32[8,128]{1,0:T(8,128)S(1)}, f32[8,128]{1,0:T(8,128)S(1)}, f32[8,128]{1,0:T(8,128)S(1)}) custom-call(f32[9,24,128]{2,1,0:T(8,128)S(1)} %collective-permute-done.3.other_ref, f32[576,128]{1,0:T(8,128)S(1)} %get-tuple-element.25.dense_ref, f32[24,128]{1,0:T(8,128)S(1)} %get-tuple-element.34.force_ref, ...), custom_call_target="tpu_custom_call" | custom-call | tf_op jit(solution)/shard_map/late/pallas_call | solution.py:573
  24.4 0.1 collective-permute-start.4
  24.5 8.6 %collective-permute-start.5 = (f32[8,128]{1,0:T(8,128)S(1)}, f32[8,128]{1,0:T(8,128)S(1)}, u32[]{:S(2)}, u32[]{:S(2)}) collective-permute-start(f32[8,128]{1,0:T(8,128)S(1)} %get-tuple-element.39), channel_id=1, source_target_pairs={{0,248},{8,16},{16,8},{24,32},{32,24},{40,48},{48,40},{56,64},{64,... | collective-permute-start | bytes 12296 | tf_op jit(solution)/shard_map/ppermute | solution.py:580
  33.1 0.0 copy-done
  33.2 2.0 %finish.1 = (f32[5184,128]{1,0:T(8,128)}, f32[5184,128]{1,0:T(8,128)S(1)}, f32[192,128]{1,0:T(8,128)S(1)}) custom-call(f32[5184,128]{1,0:T(8,128)S(1)} %get-tuple-element.30.new_in_ref, f32[192,128]{1,0:T(8,128)S(1)} %get-tuple-element.31.bounce_in_ref, ...), custom_call_target="tpu_custom_call", output_to_operand_aliasing={{1}: (0, {}), {2}: (1, {})} | custom-call | tf_op jit(solution)/shard_map/finish/pallas_call | solution.py:582
  35.1 0.0 collective-permute-done.4
  35.1 1.2 %collective-permute-done.5 = f32[8,128]{1,0:T(8,128)S(1)} collective-permute-done((f32[8,128]{1,0:T(8,128)S(1)}, f32[8,128]{1,0:T(8,128)S(1)}, u32[]{:S(2)}, u32[]{:S(2)}) %collective-permute-start.5) | collective-permute-done | bytes 4128 | tf_op jit(solution)/shard_map/ppermute | solution.py:580
  36.4 0.6 %slice.3 = f32[3,128]{1,0:T(4,128)} slice(f32[8,128]{1,0:T(8,128)S(1)} %add_add_fusion), slice={[0:3], [0:128]} | slice | bytes 3072 | tf_op jit(solution)/shard_map/slice | solution.py:596
  (1 shorter events, 0.0 us)
Async XLA Ops:
  3.0 4.6 %collective-permute-start = (f32[48,128]{1,0:T(8,128)S(1)}, f32[48,128]{1,0:T(8,128)S(1)}, u32[]{:S(2)}, u32[]{:S(2)}) collective-permute-start(f32[48,128]{1,0:T(8,128)S(1)} %get-tuple-element.22), channel_id=1, source_target_pairs={{0,1},{1,0},{2,3},{3,2},{4,5},{5,4},{6,7},{7,6},{8,9},{9,8},{10,11... | collective-permute-start | bytes 73736 | tf_op jit(solution)/shard_map/ppermute | solution.py:519
  3.1 5.2 %collective-permute-start.1 = (f32[48,128]{1,0:T(8,128)S(1)}, f32[48,128]{1,0:T(8,128)S(1)}, u32[]{:S(2)}, u32[]{:S(2)}) collective-permute-start(f32[48,128]{1,0:T(8,128)S(1)} %get-tuple-element.23), channel_id=1, source_target_pairs={{0,7},{1,2},{2,1},{3,4},{4,3},{5,6},{6,5},{7,0},{8,15},{9,10},{10,... | collective-permute-start | bytes 73736 | tf_op jit(solution)/shard_map/ppermute | solution.py:518
  7.6 11.9 %copy-start.1 = (s32[4096]{0:T(1024)S(1)}, s32[4096]{0:T(1024)}, u32[]{:S(2)}) copy-start(s32[4096]{0:T(1024)} %param.9) | copy-start | bytes 49156
  7.6 11.8 %copy-start.2 = (s32[4096]{0:T(1024)S(1)}, s32[4096]{0:T(1024)}, u32[]{:S(2)}) copy-start(s32[4096]{0:T(1024)} %param.10) | copy-start | bytes 49156
  7.6 11.8 %copy-start.3 = (f32[4096]{0:T(1024)S(1)}, f32[4096]{0:T(1024)}, u32[]{:S(2)}) copy-start(f32[4096]{0:T(1024)} %param.11) | copy-start | bytes 49156
  7.6 11.8 %copy-start.4 = (s32[4096]{0:T(1024)S(1)}, s32[4096]{0:T(1024)}, u32[]{:S(2)}) copy-start(s32[4096]{0:T(1024)} %param.12) | copy-start | bytes 49156
  8.5 13.1 %collective-permute-start.2 = (f32[9,24,128]{2,1,0:T(8,128)S(1)}, f32[9,24,128]{2,1,0:T(8,128)S(1)}, u32[]{:S(2)}, u32[]{:S(2)}) collective-permute-start(f32[9,24,128]{2,1,0:T(8,128)S(1)} %get-tuple-element.24), channel_id=1, source_target_pairs={{0,8},{8,0},{16,24},{24,16},{32,40},{40,32},{48,56},{56,48},{64,72... | collective-permute-start | bytes 331784 | tf_op jit(solution)/shard_map/ppermute | solution.py:536
  9.5 14.5 %collective-permute-start.3 = (f32[9,24,128]{2,1,0:T(8,128)S(1)}, f32[9,24,128]{2,1,0:T(8,128)S(1)}, u32[]{:S(2)}, u32[]{:S(2)}) collective-permute-start(f32[9,24,128]{2,1,0:T(8,128)S(1)} %get-tuple-element.32), channel_id=1, source_target_pairs={{0,248},{8,16},{16,8},{24,32},{32,24},{40,48},{48,40},{56,64},{64,... | collective-permute-start | bytes 331784 | tf_op jit(solution)/shard_map/ppermute | solution.py:535
  21.6 11.5 %copy-start = (s32[24,8,128]{2,1,0:T(8,128)S(1)}, s32[24,8,128]{2,1,0:T(8,128)}, u32[]{:S(2)}) copy-start(s32[24,8,128]{2,1,0:T(8,128)} %param.8) | copy-start | bytes 294916
  24.4 10.7 %collective-permute-start.4 = (f32[8,128]{1,0:T(8,128)S(1)}, f32[8,128]{1,0:T(8,128)S(1)}, u32[]{:S(2)}, u32[]{:S(2)}) collective-permute-start(f32[8,128]{1,0:T(8,128)S(1)} %get-tuple-element.38), channel_id=1, source_target_pairs={{0,8},{8,0},{16,24},{24,16},{32,40},{40,32},{48,56},{56,48},{64,72... | collective-permute-start | bytes 12296 | tf_op jit(solution)/shard_map/ppermute | solution.py:581
  24.5 11.8 %collective-permute-start.5 = (f32[8,128]{1,0:T(8,128)S(1)}, f32[8,128]{1,0:T(8,128)S(1)}, u32[]{:S(2)}, u32[]{:S(2)}) collective-permute-start(f32[8,128]{1,0:T(8,128)S(1)} %get-tuple-element.39), channel_id=1, source_target_pairs={{0,248},{8,16},{16,8},{24,32},{32,24},{40,48},{48,40},{56,64},{64,... | collective-permute-start | bytes 12296 | tf_op jit(solution)/shard_map/ppermute | solution.py:580

commit v5 on v4

--- a/solution.py
+++ b/solution.py
@@ -18,7 +18,8 @@
 UNROLL_T = 8
 UNROLL_S = 11
 UNROLL_G = 1
-UNROLL_F = 8
+UNROLL_F = 6
+OUT_COPIES = 4
 TABLE_WIDTH = 512
 GATHER_WIDTH = 4096
 F32 = jnp.float32
@@ -484,10 +485,19 @@
             new_ref[plane_rows(d, z), :] = value * fluid
         return carry
 
-    lax.fori_loop(0, DEPTH, body, 0, unroll=UNROLL_F)
-    copy = pltpu.make_async_copy(new_ref, out_ref, sem)
-    copy.start()
-    copy.wait()
+    copies = []
+    for i in range(OUT_COPIES):
+        depth = DEPTH // OUT_COPIES
+        lax.fori_loop(i * depth, (i + 1) * depth, body, 0, unroll=UNROLL_F)
+        at = pl.ds(i * depth * ROWS, depth * ROWS)
+        copies.append(
+            pltpu.make_async_copy(
+                new_ref.reshape(27, PLANES, COLS).at[:, at], out_ref.at[:, at], sem.at[i]
+            )
+        )
+        copies[i].start()
+    for copy in copies:
+        copy.wait()
 
 
 def pair_swap(count):
@@ -582,14 +592,14 @@
     populations_next, _, _ = pl.pallas_call(
         finish_kernel,
         out_shape=(
-            jax.ShapeDtypeStruct((27 * PLANES, COLS), F32),
+            jax.ShapeDtypeStruct((27, PLANES, COLS), F32),
             VMEM((27 * PLANES, COLS), F32),
             VMEM((PLANES, COLS), F32),
         ),
         in_specs=[WHOLE] * 5,
         out_specs=(SOMEWHERE, WHOLE, WHOLE),
         input_output_aliases={0: 1, 1: 2},
-        scratch_shapes=[pltpu.SemaphoreType.DMA],
+        scratch_shapes=[pltpu.SemaphoreType.DMA((OUT_COPIES,))],
         compiler_params=params(16),
         name="finish",
     )(moved, bounce, x_other, dense, solid_mask.reshape(PLANES, COLS))

time: 37.4 us -> 37.2 us (level)
  transfers between devices with their start and end apart: 6 -> 6, of which waited for: 2 -> 2; matrix products, arithmetic and copies ran while one was open for 0% -> 0% of each run, Pallas kernels for 22% -> 21%
where the time goes in v5:
time: 37.2 us; the launch traced here: 36.9 us
  starting transfers between devices  22.7 us (61%)
  Pallas kernels  10.7 us (29%)
  waiting for transfers between devices  2.17 us (6%)
  between operations  0.77 us (2%)
  local copies, waits for them, and re-layouts  0.61 us (2%)
    ppermute x1, starting transfers between devices, per_device(): x_other = lax.ppermute(x_other, 'gx', other_swap(nx))  9.89 us
    ppermute x1, starting transfers between devices, per_device(): from_other = lax.ppermute(to_other, 'gx', other_swap(nx))  8.62 us
    ppermute x1, starting transfers between devices, per_device(): y_other = lax.ppermute(y_other, 'gy', other_swap(ny))  2.99 us
    pallas_call x1, Pallas kernels, per_device(): pl.pallas_call(stream_kernel, out_shape=(VMEM((27 * PLANES, COLS), F32),...  2.39 us
    pallas_call x1, Pallas kernels, per_device(): pl.pallas_call(rim_kernel, out_shape=(VMEM(populations.shape, F32), colum...  2.38 us
    pallas_call x1, Pallas kernels, per_device(): pl.pallas_call(table_kernel, out_shape=(VMEM((3 * PLANES, COLS), F32), VM...  2.17 us
    pallas_call x1, Pallas kernels, per_device(): pl.pallas_call(finish_kernel, out_shape=(jax.ShapeDtypeStruct((27, PLANES...  1.68 us
    ppermute x1, waiting for transfers between devices, per_device(): from_other = lax.ppermute(to_other, 'gx', other_swap(nx))  1.5 us
  transfers between devices with their start and end apart: 6, of which 2 were waited for; matrix products, arithmetic and copies ran while one was open for 0% of the time, Pallas kernels for 21%

profile of v5, /device:TPU:0, one launch (start us, length us, event | category | flops | bytes accessed | tf_op | source)
XLA Modules:
  0.0 36.9 jit_solution(10944814229104031117)
XLA Ops:
  0.6 2.4 %rims.1 = (f32[27,24,8,128]{3,2,1,0:T(8,128)S(1)}, f32[48,128]{1,0:T(8,128)S(1)}, f32[48,128]{1,0:T(8,128)S(1)}) custom-call(f32[27,24,8,128]{3,2,1,0:T(8,128)} %pop_ref.1), custom_call_target="tpu_custom_call" | custom-call | tf_op jit(solution)/shard_map/rims/pallas_call | solution.py:516
  3.0 0.1 collective-permute-start
  3.1 3.0 %collective-permute-start.1 = (f32[48,128]{1,0:T(8,128)S(1)}, f32[48,128]{1,0:T(8,128)S(1)}, u32[]{:S(2)}, u32[]{:S(2)}) collective-permute-start(f32[48,128]{1,0:T(8,128)S(1)} %get-tuple-element.23), channel_id=1, source_target_pairs={{0,7},{1,2},{2,1},{3,4},{4,3},{5,6},{6,5},{7,0},{8,15},{9,10},{10,... | collective-permute-start | bytes 73736 | tf_op jit(solution)/shard_map/ppermute | solution.py:528
  6.1 1.4 %collide.1.col_ref = f32[5184,128]{1,0:T(8,128)S(1)} custom-call(f32[27,24,8,128]{3,2,1,0:T(8,128)S(1)} %get-tuple-element.21.buf_ref), custom_call_target="tpu_custom_call" | custom-call | flops 1000000000 | bytes 5000000 | tf_op jit(solution)/shard_map/collide/pallas_call | solution.py:530
  7.6 0.0 copy-start.1
  7.6 0.0 copy-start.2
  7.6 0.0 copy-start.3
  7.6 0.0 copy-start.4
  7.6 0.0 collective-permute-done.near_ref
  7.6 0.7 %collective-permute-done.1.far_ref = f32[48,128]{1,0:T(8,128)S(1)} collective-permute-done((f32[48,128]{1,0:T(8,128)S(1)}, f32[48,128]{1,0:T(8,128)S(1)}, u32[]{:S(2)}, u32[]{:S(2)}) %collective-permute-start.1) | collective-permute-done | bytes 24608 | tf_op jit(solution)/shard_map/ppermute | solution.py:528
  8.3 0.2 edges.1
  8.5 1.0 %collective-permute-start.2 = (f32[9,24,128]{2,1,0:T(8,128)S(1)}, f32[9,24,128]{2,1,0:T(8,128)S(1)}, u32[]{:S(2)}, u32[]{:S(2)}) collective-permute-start(f32[9,24,128]{2,1,0:T(8,128)S(1)} %get-tuple-element.24), channel_id=1, source_target_pairs={{0,8},{8,0},{16,24},{24,16},{32,40},{40,32},{48,56},{56,48},{64,72... | collective-permute-start | bytes 331784 | tf_op jit(solution)/shard_map/ppermute | solution.py:546
  9.5 9.9 %collective-permute-start.3 = (f32[9,24,128]{2,1,0:T(8,128)S(1)}, f32[9,24,128]{2,1,0:T(8,128)S(1)}, u32[]{:S(2)}, u32[]{:S(2)}) collective-permute-start(f32[9,24,128]{2,1,0:T(8,128)S(1)} %get-tuple-element.32), channel_id=1, source_target_pairs={{0,248},{8,16},{16,8},{24,32},{32,24},{40,48},{48,40},{56,64},{64,... | collective-permute-start | bytes 331784 | tf_op jit(solution)/shard_map/ppermute | solution.py:545
  19.4 0.0 copy-done.1
  19.4 0.0 copy-done.2
  19.4 0.0 copy-done.3
  19.4 0.0 copy-done.4
  19.4 2.2 %tables.1 = (f32[576,128]{1,0:T(8,128)S(1)}, bf16[192,4096]{1,0:T(8,128)(2,1)S(1)}, bf16[128,4096]{1,0:T(8,128)(2,1)S(1)}, bf16[128,4096]{1,0:T(8,128)(2,1)S(1)}...) custom-call(s32[32,128]{1,0:T(8,128)S(1)} %bitcast.7, s32[32,128]{1,0:T(8,128)S(1)} %bitcast.8, ...), custom_call_target="tpu_custom_call" | custom-call | flops 6000000000 | bytes 70000 | tf_op jit(solution)/shard_map/tables/pallas_call | solution.py:548
  21.6 0.0 collective-permute-done.2.pair_ref
  21.6 0.0 copy-start
  21.6 2.4 %stream.1 = (f32[5184,128]{1,0:T(8,128)S(1)}, f32[192,128]{1,0:T(8,128)S(1)}, f32[24,128]{1,0:T(8,128)S(1)}) custom-call(f32[5184,128]{1,0:T(8,128)S(1)} %collide.1.col_ref, f32[48,128]{1,0:T(8,128)S(1)} %collective-permute-done.near_ref, f32[48,128]{1,0:T(8,128)S(1)} %collective-permute-done.1.far_ref, f32[9,24,128]{2,1,0:T(8,128)S(1)} %collective-permute-done.2.pair_ref, ...), custom_call_target="tpu_custom_call" | custom-call | tf_op jit(solution)/shard_map/stream/pallas_call | solution.py:567
  24.0 0.0 collective-permute-done.3.other_ref
  24.0 0.4 %late.1 = (f32[8,128]{1,0:T(8,128)S(1)}, f32[8,128]{1,0:T(8,128)S(1)}, f32[8,128]{1,0:T(8,128)S(1)}) custom-call(f32[9,24,128]{2,1,0:T(8,128)S(1)} %collective-permute-done.3.other_ref, f32[576,128]{1,0:T(8,128)S(1)} %get-tuple-element.25.dense_ref, f32[24,128]{1,0:T(8,128)S(1)} %get-tuple-element.34.force_ref, ...), custom_call_target="tpu_custom_call" | custom-call | tf_op jit(solution)/shard_map/late/pallas_call | solution.py:583
  24.4 0.1 collective-permute-start.4
  24.5 8.6 %collective-permute-start.5 = (f32[8,128]{1,0:T(8,128)S(1)}, f32[8,128]{1,0:T(8,128)S(1)}, u32[]{:S(2)}, u32[]{:S(2)}) collective-permute-start(f32[8,128]{1,0:T(8,128)S(1)} %get-tuple-element.39), channel_id=1, source_target_pairs={{0,248},{8,16},{16,8},{24,32},{32,24},{40,48},{48,40},{56,64},{64,... | collective-permute-start | bytes 12296 | tf_op jit(solution)/shard_map/ppermute | solution.py:590
  33.1 0.0 copy-done
  33.2 1.7 %finish.1 = (f32[27,192,128]{2,1,0:T(8,128)}, f32[5184,128]{1,0:T(8,128)S(1)}, f32[192,128]{1,0:T(8,128)S(1)}) custom-call(f32[5184,128]{1,0:T(8,128)S(1)} %get-tuple-element.30.new_in_ref, f32[192,128]{1,0:T(8,128)S(1)} %get-tuple-element.31.bounce_in_ref, ...), custom_call_target="tpu_custom_call", output_to_operand_aliasing={{1}: (0, {}), {2}: (1, {})} | custom-call | tf_op jit(solution)/shard_map/finish/pallas_call | solution.py:592
  34.8 0.0 collective-permute-done.4
  34.9 1.5 %collective-permute-done.5 = f32[8,128]{1,0:T(8,128)S(1)} collective-permute-done((f32[8,128]{1,0:T(8,128)S(1)}, f32[8,128]{1,0:T(8,128)S(1)}, u32[]{:S(2)}, u32[]{:S(2)}) %collective-permute-start.5) | collective-permute-done | bytes 4128 | tf_op jit(solution)/shard_map/ppermute | solution.py:590
  36.4 0.6 %slice.3 = f32[3,128]{1,0:T(4,128)} slice(f32[8,128]{1,0:T(8,128)S(1)} %add_add_fusion), slice={[0:3], [0:128]} | slice | bytes 3072 | tf_op jit(solution)/shard_map/slice | solution.py:606
  (1 shorter events, 0.0 us)
Async XLA Ops:
  3.0 4.6 %collective-permute-start = (f32[48,128]{1,0:T(8,128)S(1)}, f32[48,128]{1,0:T(8,128)S(1)}, u32[]{:S(2)}, u32[]{:S(2)}) collective-permute-start(f32[48,128]{1,0:T(8,128)S(1)} %get-tuple-element.22), channel_id=1, source_target_pairs={{0,1},{1,0},{2,3},{3,2},{4,5},{5,4},{6,7},{7,6},{8,9},{9,8},{10,11... | collective-permute-start | bytes 73736 | tf_op jit(solution)/shard_map/ppermute | solution.py:529
  3.1 5.2 %collective-permute-start.1 = (f32[48,128]{1,0:T(8,128)S(1)}, f32[48,128]{1,0:T(8,128)S(1)}, u32[]{:S(2)}, u32[]{:S(2)}) collective-permute-start(f32[48,128]{1,0:T(8,128)S(1)} %get-tuple-element.23), channel_id=1, source_target_pairs={{0,7},{1,2},{2,1},{3,4},{4,3},{5,6},{6,5},{7,0},{8,15},{9,10},{10,... | collective-permute-start | bytes 73736 | tf_op jit(solution)/shard_map/ppermute | solution.py:528
  7.6 11.9 %copy-start.1 = (s32[4096]{0:T(1024)S(1)}, s32[4096]{0:T(1024)}, u32[]{:S(2)}) copy-start(s32[4096]{0:T(1024)} %param.9) | copy-start | bytes 49156
  7.6 11.8 %copy-start.2 = (s32[4096]{0:T(1024)S(1)}, s32[4096]{0:T(1024)}, u32[]{:S(2)}) copy-start(s32[4096]{0:T(1024)} %param.10) | copy-start | bytes 49156
  7.6 11.8 %copy-start.3 = (f32[4096]{0:T(1024)S(1)}, f32[4096]{0:T(1024)}, u32[]{:S(2)}) copy-start(f32[4096]{0:T(1024)} %param.11) | copy-start | bytes 49156
  7.6 11.8 %copy-start.4 = (s32[4096]{0:T(1024)S(1)}, s32[4096]{0:T(1024)}, u32[]{:S(2)}) copy-start(s32[4096]{0:T(1024)} %param.12) | copy-start | bytes 49156
  8.5 13.1 %collective-permute-start.2 = (f32[9,24,128]{2,1,0:T(8,128)S(1)}, f32[9,24,128]{2,1,0:T(8,128)S(1)}, u32[]{:S(2)}, u32[]{:S(2)}) collective-permute-start(f32[9,24,128]{2,1,0:T(8,128)S(1)} %get-tuple-element.24), channel_id=1, source_target_pairs={{0,8},{8,0},{16,24},{24,16},{32,40},{40,32},{48,56},{56,48},{64,72... | collective-permute-start | bytes 331784 | tf_op jit(solution)/shard_map/ppermute | solution.py:546
  9.5 14.5 %collective-permute-start.3 = (f32[9,24,128]{2,1,0:T(8,128)S(1)}, f32[9,24,128]{2,1,0:T(8,128)S(1)}, u32[]{:S(2)}, u32[]{:S(2)}) collective-permute-start(f32[9,24,128]{2,1,0:T(8,128)S(1)} %get-tuple-element.32), channel_id=1, source_target_pairs={{0,248},{8,16},{16,8},{24,32},{32,24},{40,48},{48,40},{56,64},{64,... | collective-permute-start | bytes 331784 | tf_op jit(solution)/shard_map/ppermute | solution.py:545
  21.6 11.5 %copy-start = (s32[24,8,128]{2,1,0:T(8,128)S(1)}, s32[24,8,128]{2,1,0:T(8,128)}, u32[]{:S(2)}) copy-start(s32[24,8,128]{2,1,0:T(8,128)} %param.8) | copy-start | bytes 294916
  24.4 10.4 %collective-permute-start.4 = (f32[8,128]{1,0:T(8,128)S(1)}, f32[8,128]{1,0:T(8,128)S(1)}, u32[]{:S(2)}, u32[]{:S(2)}) collective-permute-start(f32[8,128]{1,0:T(8,128)S(1)} %get-tuple-element.38), channel_id=1, source_target_pairs={{0,8},{8,0},{16,24},{24,16},{32,40},{40,32},{48,56},{56,48},{64,72... | collective-permute-start | bytes 12296 | tf_op jit(solution)/shard_map/ppermute | solution.py:591
  24.5 11.8 %collective-permute-start.5 = (f32[8,128]{1,0:T(8,128)S(1)}, f32[8,128]{1,0:T(8,128)S(1)}, u32[]{:S(2)}, u32[]{:S(2)}) collective-permute-start(f32[8,128]{1,0:T(8,128)S(1)} %get-tuple-element.39), channel_id=1, source_target_pairs={{0,248},{8,16},{16,8},{24,32},{32,24},{40,48},{48,40},{56,64},{64,... | collective-permute-start | bytes 12296 | tf_op jit(solution)/shard_map/ppermute | solution.py:590

commit v6 on v5

--- a/solution.py
+++ b/solution.py
@@ -242,7 +242,7 @@
 def table_kernel(
     cell_ref, dir_ref, q_ref, panel_ref,
     dense_ref, row_ref, lane_ref, pan_ref, push_ref, late_push_ref, late_pan_ref,
-    gathered,
+    gathered, fields,
 ):
     gx = lax.axis_index("gx")
     count = lax.axis_size("gx")
@@ -252,11 +252,37 @@
     lane_iota = lax.broadcasted_iota(jnp.int32, (COLS, width), 0).astype(F32).astype(BF16)
     one, zero = jnp.ones((), BF16), jnp.zeros((), BF16)
     push_iota = lax.broadcasted_iota(jnp.int32, (24, width), 0)
+    part, owner = push_iota % 8, (push_iota // 8).astype(F32)
     gathered[...] = jnp.zeros_like(gathered)
 
-    def load(ref, i):
-        n = width // COLS
-        return jnp.concatenate([ref[pl.ds(n * i + j, 1), :] for j in range(n)], axis=1)
+    cell, direction, q, panel = cell_ref[...], dir_ref[...], q_ref[...], panel_ref[...]
+    active = panel >= 0
+    near = q < 0.5
+    twice = 2.0 * q
+    weight = jnp.where(near, twice, 1.0 / twice)
+    weight_hi = weight.astype(BF16).astype(F32)
+    offset = panel // per_row - gx + 1
+    offset = jnp.where(offset < 0, offset + count, offset)
+    offset = jnp.where(offset >= count, offset - count, offset)
+    ninth, third = (direction * 57) >> 9, (direction * 43) >> 7
+    numbers = (
+        jnp.where(active, cell >> 7, -1),
+        cell & 127,
+        weight_hi,
+        weight - weight_hi,
+        direction + 1 + jnp.where(near, 27, 0) + 54 * offset,
+        panel & 127,
+        jnp.where(active, offset, -1),
+        ninth - 1,
+        third - 3 * ninth - 1,
+        direction - 3 * third - 1,
+    )
+    for n, value in enumerate(numbers):
+        fields[n] = value.astype(F32)
+
+    def load(n, i):
+        share = width // COLS
+        return jnp.concatenate([fields[n, pl.ds(share * i + j, 1), :] for j in range(share)], axis=1)
 
     def spread(value, count):
         tile = jnp.broadcast_to(value.astype(F32), (16, width)).astype(BF16)
@@ -264,43 +290,21 @@
 
     def body(i, carry):
         at = pl.ds(pl.multiple_of(i * width, width), width)
-        cell, direction = load(cell_ref, i), load(dir_ref, i)
-        q, panel = load(q_ref, i), load(panel_ref, i)
-        active = panel >= 0
-        near = q < 0.5
-        twice = 2.0 * q
-        weight = jnp.where(near, twice, 1.0 / twice)
-        weight_hi = weight.astype(BF16).astype(F32)
-        weight_lo = weight - weight_hi
-        offset = panel // per_row - gx + 1
-        offset = jnp.where(offset < 0, offset + count, offset)
-        offset = jnp.where(offset >= count, offset - count, offset)
-        code = (direction + 1 + jnp.where(near, 27, 0) + 54 * offset).astype(F32)
-        spot = panel % PAN_DEV
-        row = jnp.where(active, cell // COLS, -1)
-        rows = jnp.where(row_iota == spread(row, PLANES), one, zero)
+        rows = jnp.where(row_iota == spread(load(0, i), PLANES), one, zero)
         row_ref[:, at] = rows
-        here = lane_iota == spread(cell % COLS, COLS)
+        here = lane_iota == spread(load(1, i), COLS)
         lane_ref[:, at] = jnp.where(here, one, zero)
-        values = jnp.concatenate(
-            [
-                jnp.where(here, spread(v, COLS), zero)
-                for v in (weight_hi, weight_lo, code, spot)
-            ],
-            axis=0,
+        spot = spread(load(5, i), COLS)
+        values = [spread(load(n, i), COLS) for n in (2, 3, 4)] + [spot]
+        gathered[...] += lax.dot_general(
+            rows,
+            jnp.concatenate([jnp.where(here, v, zero) for v in values], axis=0),
+            (((1,), (1,)), ((), ())),
+            preferred_element_type=F32,
         )
-        gathered[...] += lax.dot_general(
-            rows, values, (((1,), (1,)), ((), ())), preferred_element_type=F32
-        )
-        pan_ref[:, at] = jnp.where(lane_iota == spread(spot, PAN_DEV), one, zero)
-        part = push_iota % 8
-        step = jnp.where(
-            part == 0,
-            direction // 9 - 1,
-            jnp.where(part == 1, direction // 3 % 3 - 1, direction % 3 - 1),
-        )
-        chosen = active & (push_iota // 8 == offset) & (part < 3)
-        push_ref[:, at] = jnp.where(chosen, step, 0).astype(F32)
+        pan_ref[:, at] = jnp.where(lane_iota == spot, one, zero)
+        step = jnp.where(part == 0, load(7, i), jnp.where(part == 1, load(8, i), load(9, i)))
+        push_ref[:, at] = jnp.where((owner == load(6, i)) & (part < 3), step, 0.0)
         return carry
 
     lax.fori_loop(0, LINKS // width, body, 0, unroll=UNROLL_T)
@@ -557,7 +561,10 @@
             VMEM((PAN_DEV, DEPTH * COLS), BF16),
         ),
         in_specs=[WHOLE] * 4,
-        scratch_shapes=[VMEM((PLANES, 4 * COLS), F32)],
+        scratch_shapes=[
+            VMEM((PLANES, 4 * COLS), F32),
+            VMEM((10, LINKS // COLS, COLS), F32),
+        ],
         compiler_params=params(16),
         cost_estimate=pl.CostEstimate(flops=6 * 10**9, bytes_accessed=70000, transcendentals=0),
         name="tables",

time: 37.2 us -> 37.2 us (level); the launches traced: 36.9 us -> 36.5 us
  starting transfers between devices: 22.7 us -> 23.1 us
  waiting for transfers between devices: 2.17 us -> 1.77 us
  Pallas kernels: 10.7 us -> 10.3 us
    pallas_call x1, Pallas kernels: 2.17 us -> 1.77 us  [per_device(): pl.pallas_call(table_kernel, out_shape=(VMEM((3 * PLANES, COLS), F32), VM...]
    ppermute x1, starting transfers between devices: 8.62 us -> 9.02 us  [per_device(): from_other = lax.ppermute(to_other, 'gx', other_swap(nx))]
    ppermute x1, waiting for transfers between devices: 1.5 us -> 1.1 us  [per_device(): from_other = lax.ppermute(to_other, 'gx', other_swap(nx))]
  transfers between devices with their start and end apart: 6 -> 6, of which waited for: 2 -> 2; matrix products, arithmetic and copies ran while one was open for 0% -> 0% of each run, Pallas kernels for 21% -> 20%
where the time goes in v6:
time: 37.2 us; the launch traced here: 36.5 us
  starting transfers between devices  23.1 us (62%)
  Pallas kernels  10.3 us (28%)
  waiting for transfers between devices  1.77 us (5%)
  between operations  0.77 us (2%)
  local copies, waits for them, and re-layouts  0.61 us (2%)
    ppermute x1, starting transfers between devices, per_device(): x_other = lax.ppermute(x_other, 'gx', other_swap(nx))  9.89 us
    ppermute x1, starting transfers between devices, per_device(): from_other = lax.ppermute(to_other, 'gx', other_swap(nx))  9.02 us
    ppermute x1, starting transfers between devices, per_device(): y_other = lax.ppermute(y_other, 'gy', other_swap(ny))  2.99 us
    pallas_call x1, Pallas kernels, per_device(): pl.pallas_call(stream_kernel, out_shape=(VMEM((27 * PLANES, COLS), F32),...  2.39 us
    pallas_call x1, Pallas kernels, per_device(): pl.pallas_call(rim_kernel, out_shape=(VMEM(populations.shape, F32), colum...  2.38 us
    pallas_call x1, Pallas kernels, per_device(): pl.pallas_call(table_kernel, out_shape=(VMEM((3 * PLANES, COLS), F32), VM...  1.77 us
    pallas_call x1, Pallas kernels, per_device(): pl.pallas_call(finish_kernel, out_shape=(jax.ShapeDtypeStruct((27, PLANES...  1.68 us
    pallas_call x1, Pallas kernels, per_device(): pl.pallas_call(collide_kernel, out_shape=VMEM((27 * PLANES, COLS), F32),...  1.45 us
  transfers between devices with their start and end apart: 6, of which 2 were waited for; matrix products, arithmetic and copies ran while one was open for 0% of the time, Pallas kernels for 20%

profile of v6, /device:TPU:0, one launch (start us, length us, event | category | flops | bytes accessed | tf_op | source)
XLA Modules:
  0.0 36.5 jit_solution(18231985770871250063)
XLA Ops:
  0.6 2.4 %rims.1 = (f32[27,24,8,128]{3,2,1,0:T(8,128)S(1)}, f32[48,128]{1,0:T(8,128)S(1)}, f32[48,128]{1,0:T(8,128)S(1)}) custom-call(f32[27,24,8,128]{3,2,1,0:T(8,128)} %pop_ref.1), custom_call_target="tpu_custom_call" | custom-call | tf_op jit(solution)/shard_map/rims/pallas_call | solution.py:520
  3.0 0.1 collective-permute-start
  3.1 3.0 %collective-permute-start.1 = (f32[48,128]{1,0:T(8,128)S(1)}, f32[48,128]{1,0:T(8,128)S(1)}, u32[]{:S(2)}, u32[]{:S(2)}) collective-permute-start(f32[48,128]{1,0:T(8,128)S(1)} %get-tuple-element.23), channel_id=1, source_target_pairs={{0,7},{1,2},{2,1},{3,4},{4,3},{5,6},{6,5},{7,0},{8,15},{9,10},{10,... | collective-permute-start | bytes 73736 | tf_op jit(solution)/shard_map/ppermute | solution.py:532
  6.1 1.4 %collide.1.col_ref = f32[5184,128]{1,0:T(8,128)S(1)} custom-call(f32[27,24,8,128]{3,2,1,0:T(8,128)S(1)} %get-tuple-element.21.buf_ref), custom_call_target="tpu_custom_call" | custom-call | flops 1000000000 | bytes 5000000 | tf_op jit(solution)/shard_map/collide/pallas_call | solution.py:534
  7.6 0.0 copy-start.1
  7.6 0.0 copy-start.2
  7.6 0.0 copy-start.3
  7.6 0.0 copy-start.4
  7.6 0.0 collective-permute-done.near_ref
  7.6 0.7 %collective-permute-done.1.far_ref = f32[48,128]{1,0:T(8,128)S(1)} collective-permute-done((f32[48,128]{1,0:T(8,128)S(1)}, f32[48,128]{1,0:T(8,128)S(1)}, u32[]{:S(2)}, u32[]{:S(2)}) %collective-permute-start.1) | collective-permute-done | bytes 24608 | tf_op jit(solution)/shard_map/ppermute | solution.py:532
  8.3 0.2 edges.1
  8.5 1.0 %collective-permute-start.2 = (f32[9,24,128]{2,1,0:T(8,128)S(1)}, f32[9,24,128]{2,1,0:T(8,128)S(1)}, u32[]{:S(2)}, u32[]{:S(2)}) collective-permute-start(f32[9,24,128]{2,1,0:T(8,128)S(1)} %get-tuple-element.24), channel_id=1, source_target_pairs={{0,8},{8,0},{16,24},{24,16},{32,40},{40,32},{48,56},{56,48},{64,72... | collective-permute-start | bytes 331784 | tf_op jit(solution)/shard_map/ppermute | solution.py:550
  9.5 9.9 %collective-permute-start.3 = (f32[9,24,128]{2,1,0:T(8,128)S(1)}, f32[9,24,128]{2,1,0:T(8,128)S(1)}, u32[]{:S(2)}, u32[]{:S(2)}) collective-permute-start(f32[9,24,128]{2,1,0:T(8,128)S(1)} %get-tuple-element.32), channel_id=1, source_target_pairs={{0,248},{8,16},{16,8},{24,32},{32,24},{40,48},{48,40},{56,64},{64,... | collective-permute-start | bytes 331784 | tf_op jit(solution)/shard_map/ppermute | solution.py:549
  19.4 0.0 copy-done.1
  19.4 0.0 copy-done.2
  19.4 0.0 copy-done.3
  19.4 0.0 copy-done.4
  19.4 1.8 %tables.1 = (f32[576,128]{1,0:T(8,128)S(1)}, bf16[192,4096]{1,0:T(8,128)(2,1)S(1)}, bf16[128,4096]{1,0:T(8,128)(2,1)S(1)}, bf16[128,4096]{1,0:T(8,128)(2,1)S(1)}...) custom-call(s32[32,128]{1,0:T(8,128)S(1)} %bitcast.7, s32[32,128]{1,0:T(8,128)S(1)} %bitcast.8, ...), custom_call_target="tpu_custom_call" | custom-call | flops 6000000000 | bytes 70000 | tf_op jit(solution)/shard_map/tables/pallas_call | solution.py:552
  21.2 0.0 collective-permute-done.2.pair_ref
  21.2 0.0 copy-start
  21.2 2.4 %stream.1 = (f32[5184,128]{1,0:T(8,128)S(1)}, f32[192,128]{1,0:T(8,128)S(1)}, f32[24,128]{1,0:T(8,128)S(1)}) custom-call(f32[5184,128]{1,0:T(8,128)S(1)} %collide.1.col_ref, f32[48,128]{1,0:T(8,128)S(1)} %collective-permute-done.near_ref, f32[48,128]{1,0:T(8,128)S(1)} %collective-permute-done.1.far_ref, f32[9,24,128]{2,1,0:T(8,128)S(1)} %collective-permute-done.2.pair_ref, ...), custom_call_target="tpu_custom_call" | custom-call | tf_op jit(solution)/shard_map/stream/pallas_call | solution.py:574
  23.6 0.0 collective-permute-done.3.other_ref
  23.6 0.4 %late.1 = (f32[8,128]{1,0:T(8,128)S(1)}, f32[8,128]{1,0:T(8,128)S(1)}, f32[8,128]{1,0:T(8,128)S(1)}) custom-call(f32[9,24,128]{2,1,0:T(8,128)S(1)} %collective-permute-done.3.other_ref, f32[576,128]{1,0:T(8,128)S(1)} %get-tuple-element.25.dense_ref, f32[24,128]{1,0:T(8,128)S(1)} %get-tuple-element.34.force_ref, ...), custom_call_target="tpu_custom_call" | custom-call | tf_op jit(solution)/shard_map/late/pallas_call | solution.py:590
  24.0 0.1 collective-permute-start.4
  24.1 9.0 %collective-permute-start.5 = (f32[8,128]{1,0:T(8,128)S(1)}, f32[8,128]{1,0:T(8,128)S(1)}, u32[]{:S(2)}, u32[]{:S(2)}) collective-permute-start(f32[8,128]{1,0:T(8,128)S(1)} %get-tuple-element.39), channel_id=1, source_target_pairs={{0,248},{8,16},{16,8},{24,32},{32,24},{40,48},{48,40},{56,64},{64,... | collective-permute-start | bytes 12296 | tf_op jit(solution)/shard_map/ppermute | solution.py:597
  33.1 0.0 copy-done
  33.2 1.7 %finish.1 = (f32[27,192,128]{2,1,0:T(8,128)}, f32[5184,128]{1,0:T(8,128)S(1)}, f32[192,128]{1,0:T(8,128)S(1)}) custom-call(f32[5184,128]{1,0:T(8,128)S(1)} %get-tuple-element.30.new_in_ref, f32[192,128]{1,0:T(8,128)S(1)} %get-tuple-element.31.bounce_in_ref, ...), custom_call_target="tpu_custom_call", output_to_operand_aliasing={{1}: (0, {}), {2}: (1, {})} | custom-call | tf_op jit(solution)/shard_map/finish/pallas_call | solution.py:599
  34.8 0.0 collective-permute-done.4
  34.9 1.1 %collective-permute-done.5 = f32[8,128]{1,0:T(8,128)S(1)} collective-permute-done((f32[8,128]{1,0:T(8,128)S(1)}, f32[8,128]{1,0:T(8,128)S(1)}, u32[]{:S(2)}, u32[]{:S(2)}) %collective-permute-start.5) | collective-permute-done | bytes 4128 | tf_op jit(solution)/shard_map/ppermute | solution.py:597
  36.0 0.6 %slice.3 = f32[3,128]{1,0:T(4,128)} slice(f32[8,128]{1,0:T(8,128)S(1)} %add_add_fusion), slice={[0:3], [0:128]} | slice | bytes 3072 | tf_op jit(solution)/shard_map/slice | solution.py:613
  (1 shorter events, 0.0 us)
Async XLA Ops:
  3.0 4.6 %collective-permute-start = (f32[48,128]{1,0:T(8,128)S(1)}, f32[48,128]{1,0:T(8,128)S(1)}, u32[]{:S(2)}, u32[]{:S(2)}) collective-permute-start(f32[48,128]{1,0:T(8,128)S(1)} %get-tuple-element.22), channel_id=1, source_target_pairs={{0,1},{1,0},{2,3},{3,2},{4,5},{5,4},{6,7},{7,6},{8,9},{9,8},{10,11... | collective-permute-start | bytes 73736 | tf_op jit(solution)/shard_map/ppermute | solution.py:533
  3.1 5.2 %collective-permute-start.1 = (f32[48,128]{1,0:T(8,128)S(1)}, f32[48,128]{1,0:T(8,128)S(1)}, u32[]{:S(2)}, u32[]{:S(2)}) collective-permute-start(f32[48,128]{1,0:T(8,128)S(1)} %get-tuple-element.23), channel_id=1, source_target_pairs={{0,7},{1,2},{2,1},{3,4},{4,3},{5,6},{6,5},{7,0},{8,15},{9,10},{10,... | collective-permute-start | bytes 73736 | tf_op jit(solution)/shard_map/ppermute | solution.py:532
  7.6 11.9 %copy-start.1 = (s32[4096]{0:T(1024)S(1)}, s32[4096]{0:T(1024)}, u32[]{:S(2)}) copy-start(s32[4096]{0:T(1024)} %param.9) | copy-start | bytes 49156
  7.6 11.8 %copy-start.2 = (s32[4096]{0:T(1024)S(1)}, s32[4096]{0:T(1024)}, u32[]{:S(2)}) copy-start(s32[4096]{0:T(1024)} %param.10) | copy-start | bytes 49156
  7.6 11.8 %copy-start.3 = (f32[4096]{0:T(1024)S(1)}, f32[4096]{0:T(1024)}, u32[]{:S(2)}) copy-start(f32[4096]{0:T(1024)} %param.11) | copy-start | bytes 49156
  7.6 11.8 %copy-start.4 = (s32[4096]{0:T(1024)S(1)}, s32[4096]{0:T(1024)}, u32[]{:S(2)}) copy-start(s32[4096]{0:T(1024)} %param.12) | copy-start | bytes 49156
  8.5 12.7 %collective-permute-start.2 = (f32[9,24,128]{2,1,0:T(8,128)S(1)}, f32[9,24,128]{2,1,0:T(8,128)S(1)}, u32[]{:S(2)}, u32[]{:S(2)}) collective-permute-start(f32[9,24,128]{2,1,0:T(8,128)S(1)} %get-tuple-element.24), channel_id=1, source_target_pairs={{0,8},{8,0},{16,24},{24,16},{32,40},{40,32},{48,56},{56,48},{64,72... | collective-permute-start | bytes 331784 | tf_op jit(solution)/shard_map/ppermute | solution.py:550
  9.5 14.1 %collective-permute-start.3 = (f32[9,24,128]{2,1,0:T(8,128)S(1)}, f32[9,24,128]{2,1,0:T(8,128)S(1)}, u32[]{:S(2)}, u32[]{:S(2)}) collective-permute-start(f32[9,24,128]{2,1,0:T(8,128)S(1)} %get-tuple-element.32), channel_id=1, source_target_pairs={{0,248},{8,16},{16,8},{24,32},{32,24},{40,48},{48,40},{56,64},{64,... | collective-permute-start | bytes 331784 | tf_op jit(solution)/shard_map/ppermute | solution.py:549
  21.2 11.9 %copy-start = (s32[24,8,128]{2,1,0:T(8,128)S(1)}, s32[24,8,128]{2,1,0:T(8,128)}, u32[]{:S(2)}) copy-start(s32[24,8,128]{2,1,0:T(8,128)} %param.8) | copy-start | bytes 294916
  24.0 10.8 %collective-permute-start.4 = (f32[8,128]{1,0:T(8,128)S(1)}, f32[8,128]{1,0:T(8,128)S(1)}, u32[]{:S(2)}, u32[]{:S(2)}) collective-permute-start(f32[8,128]{1,0:T(8,128)S(1)} %get-tuple-element.38), channel_id=1, source_target_pairs={{0,8},{8,0},{16,24},{24,16},{32,40},{40,32},{48,56},{56,48},{64,72... | collective-permute-start | bytes 12296 | tf_op jit(solution)/shard_map/ppermute | solution.py:598
  24.1 11.8 %collective-permute-start.5 = (f32[8,128]{1,0:T(8,128)S(1)}, f32[8,128]{1,0:T(8,128)S(1)}, u32[]{:S(2)}, u32[]{:S(2)}) collective-permute-start(f32[8,128]{1,0:T(8,128)S(1)} %get-tuple-element.39), channel_id=1, source_target_pairs={{0,248},{8,16},{16,8},{24,32},{32,24},{40,48},{48,40},{56,64},{64,... | collective-permute-start | bytes 12296 | tf_op jit(solution)/shard_map/ppermute | solution.py:597
